TPU v7x, 32 devices: a whole 2x2x4 slice. The times are simulated.
32 devices in a mesh: lat: 8 (over y, x, core), lev: 4 (over z).
Axes of the slice: x: 2, y: 2, z: 4, core: 2. Of those that a mesh axis runs over, the one named last changes fastest.
Arguments:
- grid: bfloat16 [16, 1024, 2, 2, 8, 128], P(None, 'lat', None, None, None, 'lev'), may hold values from -6 to 6
- legendre: bfloat16 [16, 2, 1024, 512], P('lat'), may hold values from -0.1875 to 0.1875
- quad_weights: float32 [1024], P('lat'), may hold values from 0.25 to 4
- cycle_points: int32 [1024], P('lat'), may hold values from 20 to 4116, as said below
- wave_ids: int32 [16], replicated, may hold values from 0 to 1023, as said below
- mode_projection: bfloat16 [128, 128], replicated, may hold values from -0.5 to 0.5
- vertical_modes: bfloat16 [128, 128], replicated, may hold values from -0.5 to 0.5
- mode_rates: float32 [128], replicated, may hold values from 0.05 to 5
Outputs:
- grid_out: bfloat16 [16, 1024, 2, 2, 8, 128], P(None, 'lat', None, None, None, 'lev')
Inputs may be any that keep to these rules, and one draw needn't show every extreme that they name: `cycle_points`: nondecreasing from the first cycle pair to the last; the first cycle pair has the fewest points and the last the most. `wave_ids`: slots 2 i and 2 i + 1 carry wavenumbers m and 1023 - m; no wavenumber appears twice.
All inputs are finite; a program needn't handle non-finite values.
Results may differ from a plain program's by a relative error of at most 0.0073.
Values may be sent and summed in bfloat16 or wider, within the bound.
No kernel may reach another device: no remote copies, remote signals or barrier semaphores. Data moves between devices by JAX's collectives and lax.ppermute only.
A program may use at most 64 MiB of HBM per device.

v0:
```python
import jax
import jax.numpy as jnp
from jax import lax
from jax.sharding import PartitionSpec as P

coupling = 2.0


def order_table(wave_local, k_count):
    parity = jnp.arange(2, dtype=jnp.int32)
    k_index = jnp.arange(k_count, dtype=jnp.int32)
    return wave_local[:, None, None] + parity[None, :, None] + 2 * k_index[None, None, :]


def forward_transform(legendre, values_in):
    return jnp.einsum("spjk,sjpc->spkc", legendre, values_in, preferred_element_type=jnp.float32)


def inverse_transform(legendre, coeffs):
    return jnp.einsum("spjk,spkc->sjpc", legendre, coeffs, preferred_element_type=jnp.float32)


def vertical_solve(spectral, growth, mode_projection, vertical_modes, mode_rates):
    level_dim = spectral.ndim - 1
    projected = lax.dot_general(
        spectral,
        mode_projection,
        (((level_dim,), (1,)), ((), ())),
        preferred_element_type=jnp.float32,
    )
    damped = (projected / (1.0 + growth * mode_rates)).astype(jnp.bfloat16)
    solved = lax.dot_general(
        damped, vertical_modes, (((level_dim,), (1,)), ((), ())), preferred_element_type=jnp.float32
    )
    return solved.astype(jnp.bfloat16)


def local(
    grid,
    legendre,
    quad_weights,
    cycle_points,
    wave_ids,
    mode_projection,
    vertical_modes,
    mode_rates,
):
    slot_count, cycle_local = (grid.shape[0], grid.shape[1])
    fields_count, levels_local = (grid.shape[4], grid.shape[5])
    per_device, cycles_all, k_half = (legendre.shape[0], legendre.shape[2], legendre.shape[3])
    mode_total = 2 * k_half
    levels_all = mode_projection.shape[0]
    present = (2 * wave_ids[:, None] < cycle_points[None, :]).astype(jnp.float32)
    weighting = (present * quad_weights[None, :])[:, :, None, None, None]
    north_cycle = grid[:, :, 0].astype(jnp.float32)
    south_cycle = grid[:, :, 1].astype(jnp.float32)
    even_part = (weighting * (north_cycle + south_cycle)).astype(jnp.bfloat16)
    odd_part = (weighting * (north_cycle - south_cycle)).astype(jnp.bfloat16)
    folded = jnp.stack([even_part, odd_part], axis=2)
    wave_local = lax.dynamic_slice_in_dim(wave_ids, lax.axis_index("lat") * per_device, per_device)
    full_order = order_table(wave_local, k_half)
    inside = (full_order <= mode_total - 1)[:, :, :, None]
    stacked = folded.reshape(slot_count, cycle_local, 2, 2 * fields_count, levels_local)
    gathered = lax.all_to_all(
        lax.all_to_all(stacked, "lat", split_axis=0, concat_axis=1, tiled=True),
        "lev",
        split_axis=3,
        concat_axis=4,
        tiled=True,
    )
    mixed_local = gathered.shape[3]
    values_in = gathered.reshape(per_device, cycles_all, 2, -1)
    spectral = jnp.where(inside, forward_transform(legendre, values_in), 0.0).astype(jnp.bfloat16)
    spectral = spectral.reshape(per_device, 2, k_half, mixed_local, levels_all)
    order_float = full_order.astype(jnp.float32)
    growth = (coupling * order_float * (order_float + 1.0) / (mode_total * mode_total))[
        :, :, :, None, None
    ]
    solved = vertical_solve(spectral, growth, mode_projection, vertical_modes, mode_rates)
    returned = inverse_transform(legendre, solved.reshape(per_device, 2, k_half, -1)).astype(
        jnp.bfloat16
    )
    returned = returned.reshape(per_device, cycles_all, 2, mixed_local, levels_all)
    unfolded = lax.all_to_all(
        lax.all_to_all(returned, "lat", split_axis=1, concat_axis=0, tiled=True),
        "lev",
        split_axis=4,
        concat_axis=3,
        tiled=True,
    )
    unfolded = unfolded.reshape(slot_count, cycle_local, 2, 2, fields_count, levels_local)
    even_back = unfolded[:, :, 0].astype(jnp.float32)
    odd_back = unfolded[:, :, 1].astype(jnp.float32)
    mask_cycles = present[:, :, None, None, None]
    north_out = mask_cycles * (even_back + odd_back)
    south_out = mask_cycles * (even_back - odd_back)
    return jnp.stack([north_out, south_out], axis=2).astype(jnp.bfloat16)


def solution(mesh):
    placed = (
        P(None, "lat", None, None, None, "lev"),
        P("lat", None, None, None),
        P("lat"),
        P("lat"),
        P(),
        P(),
        P(),
        P(),
    )
    return jax.shard_map(
        local,
        mesh=mesh,
        in_specs=placed,
        out_specs=P(None, "lat", None, None, None, "lev"),
        check_vma=False,
    )
```

profile of v0, /device:TPU:0, one launch (start us, length us, event | category | flops | bytes accessed | tf_op | source)
XLA Modules:
  0.0 370.0 jit_solution(16791418457040069408)
XLA Ops:
  0.0 0.7 broadcast_multiply_fusion
  0.7 0.7 compare_select_fusion
  1.4 3.5 fusion.1
  4.9 0.4 pad_maximum_fusion
  5.3 54.0 %all_to_all.66 = bf16[16,128,2,16,32]{1,4,3,2,0:T(8,128)(2,1)S(1)} all-to-all(bf16[16,128,2,16,32]{1,4,3,2,0:T(8,128)(2,1)S(1)} %pad_maximum_fusion), channel_id=1, replica_groups=mesh['lat'=8,'lev'=4] {'lat'}, dimensions={0} | all-to-all | bytes 8388608 | tf_op jit(solution)/shard_map/all_to_all | solution.py:65
  59.3 6.9 %copy.32 = bf16[2,8,128,2,16,32]{2,1,5,3,0,4:T(8,128)(2,1)} copy(bf16[2,8,128,2,16,32]{2,5,4,3,0,1:T(8,128)(2,1)S(1)} %bitcast.45) | data formatting | bytes 8388608 | tf_op jit(solution)/shard_map/all_to_all | solution.py:65
  66.2 7.3 %reshape.137 = bf16[2,1024,2,16,32]{1,4,2,0,3:T(8,128)(2,1)} reshape(bf16[2,8,128,2,16,32]{2,1,5,3,0,4:T(8,128)(2,1)} %copy.32) | data formatting | bytes 8388608 | tf_op jit(solution)/shard_map/all_to_all | solution.py:65
  73.6 5.2 %all-to-all-start.1 = ((bf16[2,1024,2,16,32]{1,4,2,0,3:T(8,128)(2,1)}), bf16[2,1024,2,16,32]{1,4,2,0,3:T(8,128)(2,1)}, u32[]{:S(2)}, u32[]{:S(2)}) async-start(bf16[2,1024,2,16,32]{1,4,2,0,3:T(8,128)(2,1)} %reshape.137), calls=%async_computation.1 | async-start | bytes 8388608 | tf_op jit(solution)/shard_map/all_to_all | solution.py:64
  78.7 0.1 dynamic_slice.3
  78.8 0.1 iota_add_fusion
  78.9 0.1 add_compare_fusion
  79.0 0.1 fusion.16
  79.1 0.3 multiply_add_fusion
  79.4 92.1 %all-to-all-done.1 = bf16[2,1024,2,16,32]{1,4,2,0,3:T(8,128)(2,1)} async-done(((bf16[2,1024,2,16,32]{1,4,2,0,3:T(8,128)(2,1)}), bf16[2,1024,2,16,32]{1,4,2,0,3:T(8,128)(2,1)}, u32[]{:S(2)}, u32[]{:S(2)}) %all-to-all-start.1) | async-done | bytes 4194336 | tf_op jit(solution)/shard_map/all_to_all | solution.py:64
  171.5 2.8 copy.21
  174.3 0.6 copy-done.4
  175.0 2.3 select_convert_fusion
  177.3 2.8 fusion.9
  180.1 7.2 %convolution_convert_fusion = bf16[2,2,512,1024]{3,2,1,0:T(8,128)(2,1)} fusion(bf16[2,2,512,512]{2,3,1,0:T(8,128)(2,1)} %bitcast.54, bf16[2,2,1024,512]{3,2,1,0:T(8,128)(2,1)} %param.9), kind=kOutput, calls=%fused_computation.16 | convolution fusion | flops 2149580800 | bytes 10485760 | tf_op jit(solution)/shard_map/spjk,spkc->sjpc/dot_general | solution.py:20
  187.3 7.8 %copy.23 = bf16[2,1024,2,4,128]{4,3,2,0,1:T(4,128)(2,1)} copy(bf16[2,1024,2,4,128]{1,4,3,2,0:T(8,128)(2,1)} %bitcast.52) | data formatting | bytes 8388608 | tf_op jit(solution)/shard_map/reshape | solution.py:83
  195.1 52.7 %all_to_all.67 = bf16[2,1024,2,4,128]{4,3,2,0,1:T(4,128)(2,1)S(1)} all-to-all(bf16[2,1024,2,4,128]{4,3,2,0,1:T(4,128)(2,1)} %copy.23), channel_id=1, replica_groups=mesh['lat'=8,'lev'=4] {'lat'}, dimensions={1} | all-to-all | bytes 8388608 | tf_op jit(solution)/shard_map/all_to_all | solution.py:85
  247.8 1.1 copy.24
  248.9 2.3 copy.25
  251.2 7.9 %copy.26 = bf16[16,128,2,4,128]{1,3,2,0,4:T(4,128)(2,1)} copy(bf16[16,128,2,4,128]{4,1,3,2,0:T(8,128)(2,1)} %bitcast.47) | data formatting | bytes 8388608 | tf_op jit(solution)/shard_map/all_to_all | solution.py:85
  259.2 5.2 %all-to-all-start.3 = ((bf16[16,128,2,4,128]{1,3,2,0,4:T(4,128)(2,1)}), bf16[16,128,2,4,128]{1,3,2,0,4:T(4,128)(2,1)}, u32[]{:S(2)}, u32[]{:S(2)}) async-start(bf16[16,128,2,4,128]{1,3,2,0,4:T(4,128)(2,1)} %copy.26), calls=%async_computation.3 | async-start | bytes 8388608 | tf_op jit(solution)/shard_map/all_to_all | solution.py:84
  264.4 0.1 compare_convert_fusion
  264.5 92.5 %all-to-all-done.3 = bf16[16,128,2,4,128]{1,3,2,0,4:T(4,128)(2,1)} async-done(((bf16[16,128,2,4,128]{1,3,2,0,4:T(4,128)(2,1)}), bf16[16,128,2,4,128]{1,3,2,0,4:T(4,128)(2,1)}, u32[]{:S(2)}, u32[]{:S(2)}) %all-to-all-start.3) | async-done | bytes 4194336 | tf_op jit(solution)/shard_map/all_to_all | solution.py:84
  357.0 7.0 %copy.27 = bf16[16,128,2,4,128]{1,4,3,2,0:T(8,128)(2,1)S(1)} copy(bf16[16,128,2,4,128]{1,3,2,0,4:T(4,128)(2,1)} %all-to-all-done.3) | data formatting | bytes 8388608 | tf_op jit(solution)/shard_map/all_to_all | solution.py:84
  364.0 1.3 copy.28
  365.3 0.9 copy-done.5
  366.2 1.8 fusion.5
  368.0 2.0 copy-done.6
  (17 shorter events, 0.0 us)
Async XLA Ops:
  0.0 177.3 %copy-start = (bf16[128,128]{1,0:T(8,128)(2,1)S(1)}, bf16[128,128]{1,0:T(8,128)(2,1)}, u32[]{:S(2)}) copy-start(bf16[128,128]{1,0:T(8,128)(2,1)} %param.14) | copy-start | bytes 98308
  73.6 5.2 %copy-start.8 = (s32[16]{0:T(128)S(1)}, s32[16]{0:T(128)}, u32[]{:S(2)}) copy-start(s32[16]{0:T(128)} %param.12) | copy-start | bytes 196
  73.6 5.5 %copy-start.3 = (f32[128]{0:T(128)S(1)}, f32[128]{0:T(128)}, u32[]{:S(2)}) copy-start(f32[128]{0:T(128)} %param.15) | copy-start | bytes 1540
  73.6 97.9 %all-to-all-start.1 = ((bf16[2,1024,2,16,32]{1,4,2,0,3:T(8,128)(2,1)}), bf16[2,1024,2,16,32]{1,4,2,0,3:T(8,128)(2,1)}, u32[]{:S(2)}, u32[]{:S(2)}) async-start(bf16[2,1024,2,16,32]{1,4,2,0,3:T(8,128)(2,1)} %reshape.137), calls=%async_computation.1 | async-start | bytes 8388608 | tf_op jit(solution)/shard_map/all_to_all | solution.py:64
  171.5 3.4 copy-start.4
  175.0 2.4 copy-start.7
  259.2 5.2 %copy-start.2 = (s32[128]{0:T(128)S(1)}, s32[128]{0:T(128)}, u32[]{:S(2)}) copy-start(s32[128]{0:T(128)} %param.11) | copy-start | bytes 1540
  259.2 97.8 %all-to-all-start.3 = ((bf16[16,128,2,4,128]{1,3,2,0,4:T(4,128)(2,1)}), bf16[16,128,2,4,128]{1,3,2,0,4:T(4,128)(2,1)}, u32[]{:S(2)}, u32[]{:S(2)}) async-start(bf16[16,128,2,4,128]{1,3,2,0,4:T(4,128)(2,1)} %copy.26), calls=%async_computation.3 | async-start | bytes 8388608 | tf_op jit(solution)/shard_map/all_to_all | solution.py:84
  364.0 2.2 copy-start.5
  365.3 4.8 %copy-start.1 = (bf16[128,128]{1,0:T(8,128)(2,1)S(1)}, bf16[128,128]{1,0:T(8,128)(2,1)}, u32[]{:S(2)}) copy-start(bf16[128,128]{1,0:T(8,128)(2,1)} %param.14) | copy-start | bytes 98308
  368.0 2.0 copy-start.6
where the time goes:
time: 371 us; the launch traced here: 370 us
  waiting for transfers between devices  185 us (50%)
  blocking collectives  107 us (29%)
  local copies, waits for them, and re-layouts  48.1 us (13%)
  matrix products  12.3 us (3%)
  starting transfers between devices  10.4 us (3%)
  other arithmetic  7.74 us (2%)
    all_to_all x1, waiting for transfers between devices, local(): lax.all_to_all(lax.all_to_all(returned, 'lat', split_axis=1, concat_axis=...  92.5 us
    all_to_all x1, waiting for transfers between devices, local(): lax.all_to_all(lax.all_to_all(stacked, 'lat', split_axis=0, concat_axis=1...  92.1 us
    all_to_all x1, blocking collectives, local(): lax.all_to_all(stacked, 'lat', split_axis=0, concat_axis=1, tiled=True)  54 us
    all_to_all x1, blocking collectives, local(): lax.all_to_all(returned, 'lat', split_axis=1, concat_axis=0, tiled=True)  52.7 us
    all_to_all x2, local copies, waits for them, and re-layouts, local(): lax.all_to_all(stacked, 'lat', split_axis=0, concat_axis=1, tiled=True)  14.2 us
    all_to_all x3, local copies, waits for them, and re-layouts, local(): lax.all_to_all(returned, 'lat', split_axis=1, concat_axis=0, tiled=True)  11.3 us
    all_to_all x2, local copies, waits for them, and re-layouts, local(): lax.all_to_all(lax.all_to_all(returned, 'lat', split_axis=1, concat_axis=...  8.3 us
    reshape x1, local copies, waits for them, and re-layouts, local(): returned.reshape(per_device, cycles_all, 2, mixed_local, levels_all)  7.83 us
  transfers between devices with their start and end apart: 2, of which 2 were waited for; matrix products, arithmetic and copies ran while one was open for 0% of the time, Pallas kernels for 0%

commit v1 on v0

v1 whole, which is shorter than its diff:
```python
import functools

import jax
import jax.numpy as jnp
from jax import lax
from jax.experimental import pallas as pl
from jax.experimental.pallas import tpu as pltpu
from jax.sharding import PartitionSpec as P

coupling = 2.0
LANES = 128
VMEM_BYTES = 48 * 1024 * 1024


def packed_counts(wave_a, wave_b, parity, modes):
    count_a = lax.shift_right_arithmetic(modes + 1 - wave_a - parity, 1)
    count_b = lax.shift_right_arithmetic(modes + 1 - wave_b - parity, 1)
    return count_a, count_b


def table_kernel(cut, meta, wave, leg, table0, table1, back0, back1):
    lat_n, width, k_half = cut["lat"], cut["cycles"], leg.shape[3]
    me = meta[0]
    modes = 2 * k_half
    wave_a, wave_b = wave[2 * me], wave[2 * me + 1]
    for parity, (table, back) in enumerate(((table0, back0), (table1, back1))):
        kk = table.shape[1]
        count_a, count_b = packed_counts(wave_a, wave_b, parity, modes)
        for slot in range(2):
            shift = 0 if slot == 0 else count_a
            count = count_a if slot == 0 else count_b
            row = lax.broadcasted_iota(jnp.int32, (k_half, kk), 0)
            col = lax.broadcasted_iota(jnp.int32, (k_half, kk), 1)
            pick = jnp.where((col == row + shift) & (row < count), 1.0, 0.0).astype(jnp.bfloat16)
            row_t = lax.broadcasted_iota(jnp.int32, (kk, k_half), 1)
            col_t = lax.broadcasted_iota(jnp.int32, (kk, k_half), 0)
            pick_t = jnp.where((col_t == row_t + shift) & (row_t < count), 1.0, 0.0).astype(
                jnp.bfloat16
            )

            @pl.loop(0, lat_n)
            def _(step):
                owner = jnp.bitwise_xor(me, step)
                block = leg[slot, parity, pl.ds(pl.multiple_of(owner * width, width), width), :]
                start = pl.multiple_of(slot * lat_n * width + step * width, width)
                table[pl.ds(start, width), :] = jnp.dot(
                    block, pick, preferred_element_type=jnp.float32
                ).astype(jnp.bfloat16)
                back[:, pl.ds(start, width)] = lax.dot_general(
                    pick_t, block, (((1,), (1,)), ((), ())), preferred_element_type=jnp.float32
                ).astype(jnp.bfloat16)


def fold_kernel(cut, row0, meta, wave, quad, cycles, grid, *refs):
    lat_n = cut["lat"]
    outs, held, sems = refs[:lat_n], refs[lat_n], refs[lat_n + 1]
    rows = held.shape[3]
    me = meta[0]
    copies = []
    for step in range(lat_n):
        owner = jnp.bitwise_xor(me, step)
        copy = pltpu.make_async_copy(
            grid.at[pl.ds(2 * owner, 2), :, pl.ds(row0, rows), :], held.at[step], sems.at[step]
        )
        copy.start()
        copies.append(copy)
    for step in range(lat_n):
        owner = jnp.bitwise_xor(me, step)
        copies[step].wait()
        for slot in range(2):
            weight = jnp.where(2 * wave[2 * owner + slot] < cycles[...], quad[...], 0.0)
            north = held[step, slot, 0].astype(jnp.float32)
            south = held[step, slot, 1].astype(jnp.float32)
            outs[step][slot, 0] = (weight * (north + south)).astype(jnp.bfloat16)
            outs[step][slot, 1] = (weight * (north - south)).astype(jnp.bfloat16)


def forward_kernel(cut, meta, table0, table1, *refs):
    lat_n, lev_n = cut["lat"], cut["lev"]
    parts, outs, packed = refs[:lat_n], refs[lat_n : lat_n + lev_n], refs[lat_n + lev_n]
    share = outs[0].shape[0]
    at = 0
    for parity, table in enumerate((table0, table1)):
        kk = table.shape[1]
        values = jnp.concatenate(
            [parts[step][slot, parity] for slot in range(2) for step in range(lat_n)], axis=1
        )
        packed[:, at : at + kk] = jnp.dot(
            values, table[...], preferred_element_type=jnp.float32
        ).astype(jnp.bfloat16)
        at += kk
    for step in range(lev_n):
        owner = jnp.bitwise_xor(meta[1], step)
        outs[step][...] = packed[pl.ds(pl.multiple_of(owner * share, share), share), :]


def solve_kernel(cut, meta, wave, project, modes_back, rates, *refs):
    lev_n, levels, k_half, kk0 = cut["lev"], cut["levels"], cut["k_half"], cut["kk"][0]
    parts, outs = refs[:lev_n], refs[lev_n:]
    rows, kk_all = parts[0].shape
    me = meta[0]
    modes = 2 * k_half
    wave_a, wave_b = wave[2 * me], wave[2 * me + 1]
    column = lax.broadcasted_iota(jnp.int32, (8, kk_all), 1)
    odd = column >= kk0
    counts = [packed_counts(wave_a, wave_b, parity, modes) for parity in range(2)]
    count_a = jnp.where(odd, counts[1][0], counts[0][0])
    count_b = jnp.where(odd, counts[1][1], counts[0][1])
    parity = jnp.where(odd, 1, 0)
    place = jnp.where(odd, column - kk0, column)
    order = parity + jnp.where(
        place < count_a, wave_a + 2 * place, wave_b + 2 * (place - count_a)
    )
    order = jnp.where(place < count_a + count_b, order, 0).astype(jnp.float32)
    growth = (coupling * order * (order + 1.0) / (modes * modes))[:1]
    damping = 1.0 + growth * rates[...]
    for col in range(rows // levels):
        at = slice(col * levels, (col + 1) * levels)
        values = jnp.concatenate([parts[step][at, :] for step in range(lev_n)], axis=0)
        projected = jnp.dot(project[...], values, preferred_element_type=jnp.float32)
        damped = (projected / damping).astype(jnp.bfloat16)
        solved = jnp.dot(modes_back[...], damped, preferred_element_type=jnp.float32)
        solved = solved.astype(jnp.bfloat16)
        for step in range(lev_n):
            outs[step][at, :] = solved[step * levels : (step + 1) * levels]


def inverse_kernel(cut, meta, back0, back1, *refs):
    lat_n, lev_n, width = cut["lat"], cut["lev"], cut["cycles"]
    parts, outs, packed = refs[:lev_n], refs[lev_n : lev_n + lat_n], refs[lev_n + lat_n]
    share = parts[0].shape[0]
    for step in range(lev_n):
        owner = jnp.bitwise_xor(meta[1], step)
        packed[pl.ds(pl.multiple_of(owner * share, share), share), :] = parts[step][...]
    at = 0
    for parity, back in enumerate((back0, back1)):
        kk = back.shape[0]
        returned = jnp.dot(
            packed[:, at : at + kk], back[...], preferred_element_type=jnp.float32
        ).astype(jnp.bfloat16)
        for slot in range(2):
            for step in range(lat_n):
                start = (slot * lat_n + step) * width
                outs[step][slot, parity] = returned[:, start : start + width]
        at += kk


def unfold_kernel(cut, row0, chained, meta, wave, cycles, *refs):
    lat_n = cut["lat"]
    parts = refs[:lat_n]
    out, held, sems = refs[lat_n + (1 if chained else 0) :]
    rows = held.shape[3]
    me = meta[0]
    copies = []
    for step in range(lat_n):
        owner = jnp.bitwise_xor(me, step)
        for slot in range(2):
            seen = 2 * wave[2 * owner + slot] < cycles[...]
            even = parts[step][slot, 0].astype(jnp.float32)
            odd = parts[step][slot, 1].astype(jnp.float32)
            held[step, slot, 0] = jnp.where(seen, even + odd, 0.0).astype(jnp.bfloat16)
            held[step, slot, 1] = jnp.where(seen, even - odd, 0.0).astype(jnp.bfloat16)
        copy = pltpu.make_async_copy(
            held.at[step], out.at[pl.ds(2 * owner, 2), :, pl.ds(row0, rows), :], sems.at[step]
        )
        copy.start()
        copies.append(copy)
    for copy in copies:
        copy.wait()


vmem = pl.BlockSpec(memory_space=pltpu.VMEM)
smem = pl.BlockSpec(memory_space=pltpu.SMEM)
anywhere = pl.BlockSpec(memory_space=pl.ANY)


def call(body, name, ins, in_specs, outs, out_specs, scratch, flops=0, aliases=None):
    moved = sum(x.size * x.dtype.itemsize for x in list(ins) + list(outs))
    return pl.pallas_call(
        body,
        name=name,
        out_shape=list(outs),
        in_specs=list(in_specs),
        out_specs=list(out_specs),
        scratch_shapes=list(scratch),
        input_output_aliases=aliases or {},
        cost_estimate=pl.CostEstimate(flops=flops, bytes_accessed=moved, transcendentals=0),
        compiler_params=pltpu.CompilerParams(vmem_limit_bytes=VMEM_BYTES),
    )(*ins)


def struct(*shape):
    return jax.ShapeDtypeStruct(shape, jnp.bfloat16)


def exchange(parts, axis, count):
    return [parts[0]] + [
        lax.ppermute(parts[r], axis, [(i, i ^ r) for i in range(count)]) for r in range(1, count)
    ]


def reordered(array, owner, count, axis):
    size = array.shape[axis] // count
    return jnp.concatenate(
        [
            lax.dynamic_slice_in_dim(array, jnp.bitwise_xor(owner, r) * size, size, axis)
            for r in range(count)
        ],
        axis=axis,
    )


def blocks_of(cols, lev_n):
    pieces = 2
    while pieces > 1 and cols % (pieces * lev_n):
        pieces //= 2
    return [(p * cols // pieces, cols // pieces) for p in range(pieces)]


def local_packed(
    lat_n, lev_n, grid, legendre, quad, cycle_points, wave_ids, projection, vertical, rates
):
    slots, width, halves, parts_c, fields, levels = grid.shape
    k_half = legendre.shape[3]
    cols = parts_c * fields
    kk = (-(-(k_half + 1) // LANES) * LANES, k_half)
    kk_all = sum(kk)
    wide = 2 * lat_n * width
    cut = {
        "lat": lat_n,
        "lev": lev_n,
        "cycles": width,
        "levels": levels,
        "k_half": k_half,
        "kk": kk,
    }
    me_lat, me_lev = lax.axis_index("lat"), lax.axis_index("lev")
    meta = jnp.stack([me_lat, me_lev]).astype(jnp.int32)
    lines = jnp.transpose(grid, (0, 2, 3, 4, 5, 1)).reshape(slots, halves, cols * levels, width)
    quad_row, cycle_row = quad.reshape(1, width), cycle_points.reshape(1, width)
    rates_col = rates.reshape(-1, 1)
    project = reordered(projection, me_lev, lev_n, 1)
    modes_back = reordered(vertical, me_lev, lev_n, 0)

    blocks = blocks_of(cols, lev_n)
    arrived = []
    for first, count in blocks:
        rows = count * levels
        folded = call(
            functools.partial(fold_kernel, cut, first * levels),
            "fold",
            (meta, wave_ids, quad_row, cycle_row, lines),
            (smem, smem, vmem, vmem, anywhere),
            [struct(2, 2, rows, width)] * lat_n,
            [vmem] * lat_n,
            [
                pltpu.VMEM((lat_n, 2, 2, rows, width), jnp.bfloat16),
                pltpu.SemaphoreType.DMA((lat_n,)),
            ],
        )
        arrived.append(exchange(folded, "lat", lat_n))

    table0, table1, back0, back1 = call(
        functools.partial(table_kernel, cut),
        "tables",
        (meta, wave_ids, legendre),
        (smem, smem, vmem),
        [struct(wide, kk[0]), struct(wide, kk[1]), struct(kk[0], wide), struct(kk[1], wide)],
        [vmem] * 4,
        [],
        flops=4 * wide * k_half * kk_all,
    )

    out = None
    for (first, count), parts in zip(blocks, arrived):
        rows = count * levels
        share = rows // lev_n
        flops = 2 * rows * wide * kk_all
        packed = call(
            functools.partial(forward_kernel, cut),
            "forward",
            (meta, table0, table1, *parts),
            [smem] + [vmem] * (2 + lat_n),
            [struct(share, kk_all)] * lev_n,
            [vmem] * lev_n,
            [pltpu.VMEM((rows, kk_all), jnp.bfloat16)],
            flops=flops,
        )
        packed = exchange(packed, "lev", lev_n)
        solved = call(
            functools.partial(solve_kernel, cut),
            "solve",
            (meta, wave_ids, project, modes_back, rates_col, *packed),
            [smem] * 2 + [vmem] * (3 + lev_n),
            [struct(share, kk_all)] * lev_n,
            [vmem] * lev_n,
            [],
            flops=4 * share * lev_n * kk_all * lev_n * levels,
        )
        solved = exchange(solved, "lev", lev_n)
        returned = call(
            functools.partial(inverse_kernel, cut),
            "inverse",
            (meta, back0, back1, *solved),
            [smem] + [vmem] * (2 + lev_n),
            [struct(2, 2, rows, width)] * lat_n,
            [vmem] * lat_n,
            [pltpu.VMEM((rows, kk_all), jnp.bfloat16)],
            flops=flops,
        )
        returned = exchange(returned, "lat", lat_n)
        chained = out is not None
        (out,) = call(
            functools.partial(unfold_kernel, cut, first * levels, chained),
            "unfold",
            (meta, wave_ids, cycle_row, *returned) + ((out,) if chained else ()),
            [smem] * 2 + [vmem] * (1 + lat_n) + ([anywhere] if chained else []),
            [struct(slots, halves, cols * levels, width)],
            [anywhere],
            [
                pltpu.VMEM((lat_n, 2, 2, rows, width), jnp.bfloat16),
                pltpu.SemaphoreType.DMA((lat_n,)),
            ],
            aliases={3 + lat_n: 0} if chained else None,
        )
    out = out.reshape(slots, halves, parts_c, fields, levels, width)
    return jnp.transpose(out, (0, 5, 1, 2, 3, 4))


def local_plain(
    lat_n, lev_n, grid, legendre, quad, cycle_points, wave_ids, projection, vertical, rates
):
    slots, width = grid.shape[:2]
    fields, levels = grid.shape[4:]
    owned, cycles_all, k_half = legendre.shape[0], legendre.shape[2], legendre.shape[3]
    modes = 2 * k_half
    levels_all = projection.shape[0]
    present = (2 * wave_ids[:, None] < cycle_points[None, :]).astype(jnp.float32)
    weighting = (present * quad[None, :])[:, :, None, None, None]
    north, south = grid[:, :, 0].astype(jnp.float32), grid[:, :, 1].astype(jnp.float32)
    even = (weighting * (north + south)).astype(jnp.bfloat16)
    odd = (weighting * (north - south)).astype(jnp.bfloat16)
    folded = jnp.stack([even, odd], axis=2).reshape(slots, width, 2, 2 * fields, levels)
    wave_local = lax.dynamic_slice_in_dim(wave_ids, lax.axis_index("lat") * owned, owned)
    order = (
        wave_local[:, None, None]
        + jnp.arange(2, dtype=jnp.int32)[None, :, None]
        + 2 * jnp.arange(k_half, dtype=jnp.int32)[None, None, :]
    )
    values = lax.all_to_all(folded, "lat", split_axis=0, concat_axis=1, tiled=True)
    values = lax.all_to_all(values, "lev", split_axis=3, concat_axis=4, tiled=True)
    mixed = values.shape[3]
    values = values.reshape(owned, cycles_all, 2, -1)
    spectral = jnp.einsum("spjk,sjpc->spkc", legendre, values, preferred_element_type=jnp.float32)
    spectral = jnp.where((order <= modes - 1)[..., None], spectral, 0.0).astype(jnp.bfloat16)
    spectral = spectral.reshape(owned, 2, k_half, mixed, levels_all)
    order = order.astype(jnp.float32)
    growth = (coupling * order * (order + 1.0) / (modes * modes))[..., None, None]
    last = (((4,), (1,)), ((), ()))
    projected = lax.dot_general(spectral, projection, last, preferred_element_type=jnp.float32)
    damped = (projected / (1.0 + growth * rates)).astype(jnp.bfloat16)
    solved = lax.dot_general(damped, vertical, last, preferred_element_type=jnp.float32)
    solved = solved.astype(jnp.bfloat16).reshape(owned, 2, k_half, -1)
    returned = jnp.einsum("spjk,spkc->sjpc", legendre, solved, preferred_element_type=jnp.float32)
    returned = returned.astype(jnp.bfloat16).reshape(owned, cycles_all, 2, mixed, levels_all)
    back = lax.all_to_all(returned, "lat", split_axis=1, concat_axis=0, tiled=True)
    back = lax.all_to_all(back, "lev", split_axis=4, concat_axis=3, tiled=True)
    back = back.reshape(slots, width, 2, 2, fields, levels).astype(jnp.float32)
    seen = present[:, :, None, None, None]
    north, south = seen * (back[:, :, 0] + back[:, :, 1]), seen * (back[:, :, 0] - back[:, :, 1])
    return jnp.stack([north, south], axis=2).astype(jnp.bfloat16)


def local(lat_n, lev_n, grid, legendre, *rest):
    width, levels = grid.shape[1], grid.shape[5]
    fits = (
        legendre.shape[0] == 2
        and lat_n & (lat_n - 1) == 0
        and lev_n & (lev_n - 1) == 0
        and width % LANES == 0
        and legendre.shape[3] % LANES == 0
        and levels % 16 == 0
        and (grid.shape[3] * grid.shape[4]) % lev_n == 0
    )
    step = local_packed if fits else local_plain
    return step(lat_n, lev_n, grid, legendre, *rest)


def solution(mesh):
    placed = P(None, "lat", None, None, None, "lev")
    return jax.shard_map(
        functools.partial(local, mesh.shape["lat"], mesh.shape["lev"]),
        mesh=mesh,
        in_specs=(placed, P("lat", None, None, None), P("lat"), P("lat"), P(), P(), P(), P()),
        out_specs=placed,
        check_vma=False,
    )
```

time: 371 us -> 172 us (0.46)
  waiting for transfers between devices: 185 us -> 54.2 us
  blocking collectives: 107 us -> 0 us
  starting transfers between devices: 10.4 us -> 60.3 us
  Pallas kernels: 0 us -> 44.4 us
  local copies, waits for them, and re-layouts: 48.1 us -> 11.5 us
  matrix products: 12.3 us -> 0 us
  other arithmetic: 7.74 us -> 0.18 us
    all_to_all x2 -> x0, waiting for transfers between devices: 185 us -> none  [the longest x1 92.5 us: local(): lax.all_to_all(lax.all_to_all(returned, 'lat', split_axis=1, concat_axis=...]
    all_to_all x2 -> x0, blocking collectives: 107 us -> none  [the longest x1 54 us: local(): lax.all_to_all(stacked, 'lat', split_axis=0, concat_axis=1, tiled=True)]
    ppermute x0 -> x40, starting transfers between devices: none -> 60.3 us  [exchange(): lax.ppermute(parts[r], axis, [(i, i ^ r) for i in range(count)])]
    ppermute x0 -> x40, waiting for transfers between devices: none -> 54.2 us  [exchange(): lax.ppermute(parts[r], axis, [(i, i ^ r) for i in range(count)])]
    pallas_call x0 -> x11, Pallas kernels: none -> 44.4 us  [call(): pl.pallas_call(body, name=name, out_shape=list(outs), in_specs=list(in_sp...]
    all_to_all x8 -> x0, local copies, waits for them, and re-layouts: 36.7 us -> none  [the longest x2 14.2 us: local(): lax.all_to_all(stacked, 'lat', split_axis=0, concat_axis=1, tiled=True)]
    dot_general x3 -> x0, matrix products: 12.3 us -> none  [the longest x1 7.21 us: inverse_transform(): jnp.einsum('spjk,spkc->sjpc', legendre, coeffs, preferred_element_type=jn...]
    all_to_all x2 -> x0, starting transfers between devices: 10.4 us -> none  [the longest x1 5.2 us: local(): lax.all_to_all(lax.all_to_all(returned, 'lat', split_axis=1, concat_axis=...]
  transfers between devices with their start and end apart: 2 -> 40, of which waited for: 2 -> 11; matrix products, arithmetic and copies ran while one was open for 0% -> 0% of each run, Pallas kernels for 0% -> 23%
where the time goes in v1:
time: 172 us; the launch traced here: 171 us
  starting transfers between devices  60.3 us (35%)
  waiting for transfers between devices  54.2 us (32%)
  Pallas kernels  44.4 us (26%)
  local copies, waits for them, and re-layouts  11.5 us (7%)
    ppermute x40, starting transfers between devices, exchange(): lax.ppermute(parts[r], axis, [(i, i ^ r) for i in range(count)])  60.3 us
    ppermute x40, waiting for transfers between devices, exchange(): lax.ppermute(parts[r], axis, [(i, i ^ r) for i in range(count)])  54.2 us
    pallas_call x11, Pallas kernels, call(): pl.pallas_call(body, name=name, out_shape=list(outs), in_specs=list(in_sp...  44.4 us
    unnamed x42, local copies, waits for them, and re-layouts  11.3 us
  transfers between devices with their start and end apart: 40, of which 11 were waited for; matrix products, arithmetic and copies ran while one was open for 0% of the time, Pallas kernels for 23%

profile of v1, /device:TPU:0, one launch (start us, length us, event | category | flops | bytes accessed | tf_op | source)
XLA Modules:
  0.0 170.9 jit_solution(8133227299578018750)
XLA Ops:
  2.0 3.0 %fold.2 = (bf16[2,2,256,128]{3,2,1,0:T(8,128)(2,1)S(1)}, bf16[2,2,256,128]{3,2,1,0:T(8,128)(2,1)S(1)}, bf16[2,2,256,128]{3,2,1,0:T(8,128)(2,1)S(1)}, bf16[2,2,25...) custom-call(s32[2]{0:T(128)S(1)} %pad_add_fusion.meta, ...), custom_call_target="tpu_custom_call" | custom-call | bytes 6292552 | tf_op jit(solution)/shard_map/fold/pallas_call | solution.py:179
  5.6 2.6 %collective-permute-start.1 = (bf16[2,2,256,128]{3,2,1,0:T(8,128)(2,1)S(1)}, bf16[2,2,256,128]{3,2,1,0:T(8,128)(2,1)S(1)}, u32[]{:S(2)}, u32[]{:S(2)}) collective-permute-start(bf16[2,2,256,128]{3,2,1,0:T(8,128)(2,1)S(1)} %get-tuple-element.63), channel_id=1, source_target_pairs={{0,8},{4,12},{8,0},{12,4},{16,24},{20,28},{24,16},{28,20},{1,9},{5... | collective-permute-start | bytes 786440 | tf_op jit(solution)/shard_map/ppermute | solution.py:198
  10.0 3.4 %fold.3 = (bf16[2,2,256,128]{3,2,1,0:T(8,128)(2,1)S(1)}, bf16[2,2,256,128]{3,2,1,0:T(8,128)(2,1)}, bf16[2,2,256,128]{3,2,1,0:T(8,128)(2,1)}, bf16[2,2,256,128]{3...) custom-call(s32[2]{0:T(128)S(1)} %pad_add_fusion.meta, ...), custom_call_target="tpu_custom_call" | custom-call | bytes 6292552 | tf_op jit(solution)/shard_map/fold/pallas_call | solution.py:179
  13.5 2.7 %collective-permute-start.5 = (bf16[2,2,256,128]{3,2,1,0:T(8,128)(2,1)}, bf16[2,2,256,128]{3,2,1,0:T(8,128)(2,1)S(1)}, u32[]{:S(2)}, u32[]{:S(2)}) collective-permute-start(bf16[2,2,256,128]{3,2,1,0:T(8,128)(2,1)} %get-tuple-element.67), channel_id=1, source_target_pairs={{0,24},{4,28},{8,16},{12,20},{16,8},{20,12},{24,0},{28,4},{1,25},{... | collective-permute-start | bytes 786440 | tf_op jit(solution)/shard_map/ppermute | solution.py:198
  17.0 3.4 %collective-permute-done.2.refs_3_ = bf16[2,2,256,128]{3,2,1,0:T(8,128)(2,1)S(1)} collective-permute-done((bf16[2,2,256,128]{3,2,1,0:T(8,128)(2,1)S(1)}, bf16[2,2,256,128]{3,2,1,0:T(8,128)(2,1)S(1)}, u32[]{:S(2)}, u32[]{:S(2)}) %collective-permute-start.2) | collective-permute-done | bytes 262176 | tf_op jit(solution)/shard_map/ppermute | solution.py:198
  21.9 1.9 %collective-permute-start.21 = (bf16[2,2,256,128]{3,2,1,0:T(8,128)(2,1)}, bf16[2,2,256,128]{3,2,1,0:T(8,128)(2,1)S(1)}, u32[]{:S(2)}, u32[]{:S(2)}) collective-permute-start(bf16[2,2,256,128]{3,2,1,0:T(8,128)(2,1)} %get-tuple-element.87), channel_id=1, source_target_pairs={{0,8},{4,12},{8,0},{12,4},{16,24},{20,28},{24,16},{28,20},{1,9},{5... | collective-permute-start | bytes 786440 | tf_op jit(solution)/shard_map/ppermute | solution.py:198
  23.8 18.0 %tables.1 = (bf16[2048,640]{1,0:T(8,128)(2,1)}, bf16[2048,512]{1,0:T(8,128)(2,1)S(1)}, bf16[640,2048]{1,0:T(8,128)(2,1)}, bf16[512,2048]{1,0:T(8,128)(2,1)S(1)}) custom-call(s32[2]{0:T(128)S(1)} %pad_add_fusion.meta, s32[16]{0:T(128)S(1)} %copy-done.13, bf16[2,2,1024,512]{3,2,1,0:T(8,128)(2,1)} %leg.1), custom_call_target="tpu_custom_call" | custom-call | flops 4831838208 | bytes 13631560 | tf_op jit(solution)/shard_map/tables/pallas_call | solution.py:179
  47.1 2.7 %collective-permute-start.25 = (bf16[2,2,256,128]{3,2,1,0:T(8,128)(2,1)}, bf16[2,2,256,128]{3,2,1,0:T(8,128)(2,1)}, u32[]{:S(2)}, u32[]{:S(2)}) collective-permute-start(bf16[2,2,256,128]{3,2,1,0:T(8,128)(2,1)} %get-tuple-element.91), channel_id=1, source_target_pairs={{0,24},{4,28},{8,16},{12,20},{16,8},{20,12},{24,0},{28,4},{1,25},{... | collective-permute-start | bytes 786440 | tf_op jit(solution)/shard_map/ppermute | solution.py:198
  55.2 3.4 %forward.2 = (bf16[64,1152]{1,0:T(8,128)(2,1)S(1)}, bf16[64,1152]{1,0:T(8,128)(2,1)S(1)}, bf16[64,1152]{1,0:T(8,128)(2,1)S(1)}, bf16[64,1152]{1,0:T(8,128)(2,1)S(1)}) custom-call(s32[2]{0:T(128)S(1)} %pad_add_fusion.meta, bf16[2048,640]{1,0:T(8,128)(2,1)} %get-tuple-element.59.table0, bf16[2048,512]{1,0:T(8,128)(2,1)S(1)} %copy-done.1, ...), custom_call_target="tpu_custom_call" | custom-call | flops 1207959552 | bytes 7405576 | tf_op jit(solution)/shard_map/forward/pallas_call | solution.py:179
  60.2 4.3 %collective-permute-done.23.refs_4_ = bf16[2,2,256,128]{3,2,1,0:T(8,128)(2,1)} collective-permute-done((bf16[2,2,256,128]{3,2,1,0:T(8,128)(2,1)}, bf16[2,2,256,128]{3,2,1,0:T(8,128)(2,1)}, u32[]{:S(2)}, u32[]{:S(2)}) %collective-permute-start.23) | collective-permute-done | bytes 262176 | tf_op jit(solution)/shard_map/ppermute | solution.py:198
  64.5 2.7 %collective-permute-start.8 = (bf16[64,1152]{1,0:T(8,128)(2,1)S(1)}, bf16[64,1152]{1,0:T(8,128)(2,1)S(1)}, u32[]{:S(2)}, u32[]{:S(2)}) collective-permute-start(bf16[64,1152]{1,0:T(8,128)(2,1)S(1)} %get-tuple-element.71), channel_id=1, source_target_pairs={{0,2},{1,3},{2,0},{3,1},{4,6},{5,7},{6,4},{7,5},{8,10},{9,11},{10,... | collective-permute-start | bytes 442376 | tf_op jit(solution)/shard_map/ppermute | solution.py:198
  67.2 2.0 %collective-permute-done.24.refs_5_ = bf16[2,2,256,128]{3,2,1,0:T(8,128)(2,1)} collective-permute-done((bf16[2,2,256,128]{3,2,1,0:T(8,128)(2,1)}, bf16[2,2,256,128]{3,2,1,0:T(8,128)(2,1)}, u32[]{:S(2)}, u32[]{:S(2)}) %collective-permute-start.24) | collective-permute-done | bytes 262176 | tf_op jit(solution)/shard_map/ppermute | solution.py:198
  69.2 4.0 %collective-permute-start.9 = (bf16[64,1152]{1,0:T(8,128)(2,1)S(1)}, bf16[64,1152]{1,0:T(8,128)(2,1)S(1)}, u32[]{:S(2)}, u32[]{:S(2)}) collective-permute-start(bf16[64,1152]{1,0:T(8,128)(2,1)S(1)} %get-tuple-element.72), channel_id=1, source_target_pairs={{0,3},{1,2},{2,1},{3,0},{4,7},{5,6},{6,5},{7,4},{8,11},{9,10},{10,... | collective-permute-start | bytes 442376 | tf_op jit(solution)/shard_map/ppermute | solution.py:198
  73.2 3.7 %forward.3 = (bf16[64,1152]{1,0:T(8,128)(2,1)S(1)}, bf16[64,1152]{1,0:T(8,128)(2,1)S(1)}, bf16[64,1152]{1,0:T(8,128)(2,1)S(1)}, bf16[64,1152]{1,0:T(8,128)(2,1)S(1)}) custom-call(s32[2]{0:T(128)S(1)} %pad_add_fusion.meta, bf16[2048,640]{1,0:T(8,128)(2,1)} %get-tuple-element.59.table0, bf16[2048,512]{1,0:T(8,128)(2,1)S(1)} %copy-done.1, ...), custom_call_target="tpu_custom_call" | custom-call | flops 1207959552 | bytes 7405576 | tf_op jit(solution)/shard_map/forward/pallas_call | solution.py:179
  77.7 3.8 %collective-permute-start.29 = (bf16[64,1152]{1,0:T(8,128)(2,1)S(1)}, bf16[64,1152]{1,0:T(8,128)(2,1)S(1)}, u32[]{:S(2)}, u32[]{:S(2)}) collective-permute-start(bf16[64,1152]{1,0:T(8,128)(2,1)S(1)} %get-tuple-element.96), channel_id=1, source_target_pairs={{0,3},{1,2},{2,1},{3,0},{4,7},{5,6},{6,5},{7,4},{8,11},{9,10},{10,... | collective-permute-start | bytes 442376 | tf_op jit(solution)/shard_map/ppermute | solution.py:198
  84.0 3.1 %collective-permute-start.12 = (bf16[64,1152]{1,0:T(8,128)(2,1)S(1)}, bf16[64,1152]{1,0:T(8,128)(2,1)S(1)}, u32[]{:S(2)}, u32[]{:S(2)}) collective-permute-start(bf16[64,1152]{1,0:T(8,128)(2,1)S(1)} %get-tuple-element.76), channel_id=1, source_target_pairs={{0,3},{1,2},{2,1},{3,0},{4,7},{5,6},{6,5},{7,4},{8,11},{9,10},{10,... | collective-permute-start | bytes 442376 | tf_op jit(solution)/shard_map/ppermute | solution.py:198
  87.1 5.3 %collective-permute-done.28.refs_2_ = bf16[64,1152]{1,0:T(8,128)(2,1)S(1)} collective-permute-done((bf16[64,1152]{1,0:T(8,128)(2,1)S(1)}, bf16[64,1152]{1,0:T(8,128)(2,1)S(1)}, u32[]{:S(2)}, u32[]{:S(2)}) %collective-permute-start.28) | collective-permute-done | bytes 147488 | tf_op jit(solution)/shard_map/ppermute | solution.py:198
  93.6 8.8 %collective-permute-start.30 = (bf16[64,1152]{1,0:T(8,128)(2,1)S(1)}, bf16[64,1152]{1,0:T(8,128)(2,1)S(1)}, u32[]{:S(2)}, u32[]{:S(2)}) collective-permute-start(bf16[64,1152]{1,0:T(8,128)(2,1)S(1)} %get-tuple-element.98), channel_id=1, source_target_pairs={{0,1},{1,0},{2,3},{3,2},{4,5},{5,4},{6,7},{7,6},{8,9},{9,8},{10,11... | collective-permute-start | bytes 442376 | tf_op jit(solution)/shard_map/ppermute | solution.py:198
  102.5 2.3 %collective-permute-start.32 = (bf16[64,1152]{1,0:T(8,128)(2,1)S(1)}, bf16[64,1152]{1,0:T(8,128)(2,1)S(1)}, u32[]{:S(2)}, u32[]{:S(2)}) collective-permute-start(bf16[64,1152]{1,0:T(8,128)(2,1)S(1)} %get-tuple-element.100), channel_id=1, source_target_pairs={{0,3},{1,2},{2,1},{3,0},{4,7},{5,6},{6,5},{7,4},{8,11},{9,10},{10,... | collective-permute-start | bytes 442376 | tf_op jit(solution)/shard_map/ppermute | solution.py:198
  104.8 3.3 %inverse.2 = (bf16[2,2,256,128]{3,2,1,0:T(8,128)(2,1)S(1)}, bf16[2,2,256,128]{3,2,1,0:T(8,128)(2,1)S(1)}, bf16[2,2,256,128]{3,2,1,0:T(8,128)(2,1)S(1)}, bf16[2,2...) custom-call(s32[2]{0:T(128)S(1)} %pad_add_fusion.meta, ...), custom_call_target="tpu_custom_call" | custom-call | flops 1207959552 | bytes 7405576 | tf_op jit(solution)/shard_map/inverse/pallas_call | solution.py:179
  109.9 6.4 %collective-permute-done.31.refs_2_ = bf16[64,1152]{1,0:T(8,128)(2,1)S(1)} collective-permute-done((bf16[64,1152]{1,0:T(8,128)(2,1)S(1)}, bf16[64,1152]{1,0:T(8,128)(2,1)S(1)}, u32[]{:S(2)}, u32[]{:S(2)}) %collective-permute-start.31) | collective-permute-done | bytes 147488 | tf_op jit(solution)/shard_map/ppermute | solution.py:198
  116.4 3.3 %inverse.3 = (bf16[2,2,256,128]{3,2,1,0:T(8,128)(2,1)S(1)}, bf16[2,2,256,128]{3,2,1,0:T(8,128)(2,1)S(1)}, bf16[2,2,256,128]{3,2,1,0:T(8,128)(2,1)S(1)}, bf16[2,2...) custom-call(s32[2]{0:T(128)S(1)} %pad_add_fusion.meta, ...), custom_call_target="tpu_custom_call" | custom-call | flops 1207959552 | bytes 7405576 | tf_op jit(solution)/shard_map/inverse/pallas_call | solution.py:179
  123.3 2.6 %collective-permute-start.38 = (bf16[2,2,256,128]{3,2,1,0:T(8,128)(2,1)S(1)}, bf16[2,2,256,128]{3,2,1,0:T(8,128)(2,1)S(1)}, u32[]{:S(2)}, u32[]{:S(2)}) collective-permute-start(bf16[2,2,256,128]{3,2,1,0:T(8,128)(2,1)S(1)} %get-tuple-element.107), channel_id=1, source_target_pairs={{0,24},{4,28},{8,16},{12,20},{16,8},{20,12},{24,0},{28,4},{1,25},{... | collective-permute-start | bytes 786440 | tf_op jit(solution)/shard_map/ppermute | solution.py:198
  125.9 3.0 %collective-permute-done.34.refs_2_ = bf16[2,2,256,128]{3,2,1,0:T(8,128)(2,1)S(1)} collective-permute-done((bf16[2,2,256,128]{3,2,1,0:T(8,128)(2,1)S(1)}, bf16[2,2,256,128]{3,2,1,0:T(8,128)(2,1)S(1)}, u32[]{:S(2)}, u32[]{:S(2)}) %collective-permute-start.34) | collective-permute-done | bytes 262176 | tf_op jit(solution)/shard_map/ppermute | solution.py:198
  130.3 3.4 %collective-permute-done.35.refs_3_ = bf16[2,2,256,128]{3,2,1,0:T(8,128)(2,1)S(1)} collective-permute-done((bf16[2,2,256,128]{3,2,1,0:T(8,128)(2,1)S(1)}, bf16[2,2,256,128]{3,2,1,0:T(8,128)(2,1)S(1)}, u32[]{:S(2)}, u32[]{:S(2)}) %collective-permute-start.35) | collective-permute-done | bytes 262176 | tf_op jit(solution)/shard_map/ppermute | solution.py:198
  133.7 2.2 %collective-permute-start.15 = (bf16[2,2,256,128]{3,2,1,0:T(8,128)(2,1)S(1)}, bf16[2,2,256,128]{3,2,1,0:T(8,128)(2,1)S(1)}, u32[]{:S(2)}, u32[]{:S(2)}) collective-permute-start(bf16[2,2,256,128]{3,2,1,0:T(8,128)(2,1)S(1)} %get-tuple-element.80), channel_id=1, source_target_pairs={{0,12},{4,8},{8,4},{12,0},{16,28},{20,24},{24,20},{28,16},{1,13},{... | collective-permute-start | bytes 786440 | tf_op jit(solution)/shard_map/ppermute | solution.py:198
  137.4 9.3 %collective-permute-done.37.refs_5_ = bf16[2,2,256,128]{3,2,1,0:T(8,128)(2,1)S(1)} collective-permute-done((bf16[2,2,256,128]{3,2,1,0:T(8,128)(2,1)S(1)}, bf16[2,2,256,128]{3,2,1,0:T(8,128)(2,1)S(1)}, u32[]{:S(2)}, u32[]{:S(2)}) %collective-permute-start.37) | collective-permute-done | bytes 262176 | tf_op jit(solution)/shard_map/ppermute | solution.py:198
  146.7 2.2 %collective-permute-start.17 = (bf16[2,2,256,128]{3,2,1,0:T(8,128)(2,1)S(1)}, bf16[2,2,256,128]{3,2,1,0:T(8,128)(2,1)S(1)}, u32[]{:S(2)}, u32[]{:S(2)}) collective-permute-start(bf16[2,2,256,128]{3,2,1,0:T(8,128)(2,1)S(1)} %get-tuple-element.82), channel_id=1, source_target_pairs={{0,20},{4,16},{8,28},{12,24},{16,4},{20,0},{24,12},{28,8},{1,21},{... | collective-permute-start | bytes 786440 | tf_op jit(solution)/shard_map/ppermute | solution.py:198
  150.5 2.0 %unfold.2.refs_8_ = bf16[16,2,512,128]{3,2,1,0:T(8,128)(2,1)} custom-call(s32[2]{0:T(128)S(1)} %pad_add_fusion.meta, s32[16]{0:T(128)S(1)} %copy-done.13, s32[1,128]{1,0:T(1,128)S(1)} %bitcast.13, bf16[2,2,256,128]{3,2,1,0:T(8,128)(2,1)S(1)} %get-tuple-element.101.refs_0_, bf16[2,2,256,128]{3,2,1,0:T(8,128)(2,1)S(1)} %collective-permute-done.33.refs_1_, ...), custom_call_target="tpu_custom_call" | custom-call | bytes 6292040 | tf_op jit(solution)/shard_map/unfold/pallas_call | solution.py:179
  152.5 12.0 %collective-permute-done.16.refs_4_ = bf16[2,2,256,128]{3,2,1,0:T(8,128)(2,1)S(1)} collective-permute-done((bf16[2,2,256,128]{3,2,1,0:T(8,128)(2,1)S(1)}, bf16[2,2,256,128]{3,2,1,0:T(8,128)(2,1)S(1)}, u32[]{:S(2)}, u32[]{:S(2)}) %collective-permute-start.16) | collective-permute-done | bytes 262176 | tf_op jit(solution)/shard_map/ppermute | solution.py:198
  164.5 4.5 %collective-permute-done.17.refs_5_ = bf16[2,2,256,128]{3,2,1,0:T(8,128)(2,1)S(1)} collective-permute-done((bf16[2,2,256,128]{3,2,1,0:T(8,128)(2,1)S(1)}, bf16[2,2,256,128]{3,2,1,0:T(8,128)(2,1)S(1)}, u32[]{:S(2)}, u32[]{:S(2)}) %collective-permute-start.17) | collective-permute-done | bytes 262176 | tf_op jit(solution)/shard_map/ppermute | solution.py:198
  168.9 2.0 %unfold.3 = bf16[16,2,512,128]{3,2,1,0:T(8,128)(2,1)} custom-call(s32[2]{0:T(128)S(1)} %pad_add_fusion.meta, s32[16]{0:T(128)S(1)} %copy-done.13, s32[1,128]{1,0:T(1,128)S(1)} %bitcast.14, bf16[2,2,256,128]{3,2,1,0:T(8,128)(2,1)S(1)} %get-tuple-element.77.refs_0_, ...), custom_call_target="tpu_custom_call", output_to_operand_aliasing={{}: (11, {})} | custom-call | bytes 10486344 | tf_op jit(solution)/shard_map/unfold/pallas_call | solution.py:179
  (106 shorter events, 33.6 us)
Async XLA Ops:
  8.2 12.9 %collective-permute-start.3 = (bf16[2,2,256,128]{3,2,1,0:T(8,128)(2,1)S(1)}, bf16[2,2,256,128]{3,2,1,0:T(8,128)(2,1)S(1)}, u32[]{:S(2)}, u32[]{:S(2)}) collective-permute-start(bf16[2,2,256,128]{3,2,1,0:T(8,128)(2,1)S(1)} %get-tuple-element.65), channel_id=1, source_target_pairs={{0,16},{4,20},{8,24},{12,28},{16,0},{20,4},{24,8},{28,12},{1,17},{... | collective-permute-start | bytes 786440 | tf_op jit(solution)/shard_map/ppermute | solution.py:198
  10.0 33.1 %collective-permute-start.4 = (bf16[2,2,256,128]{3,2,1,0:T(8,128)(2,1)}, bf16[2,2,256,128]{3,2,1,0:T(8,128)(2,1)}, u32[]{:S(2)}, u32[]{:S(2)}) collective-permute-start(bf16[2,2,256,128]{3,2,1,0:T(8,128)(2,1)} %get-tuple-element.66), channel_id=1, source_target_pairs={{0,20},{4,16},{8,28},{12,24},{16,4},{20,0},{24,12},{28,8},{1,21},{... | collective-permute-start | bytes 786440 | tf_op jit(solution)/shard_map/ppermute | solution.py:198
  13.5 29.7 %collective-permute-start.5 = (bf16[2,2,256,128]{3,2,1,0:T(8,128)(2,1)}, bf16[2,2,256,128]{3,2,1,0:T(8,128)(2,1)S(1)}, u32[]{:S(2)}, u32[]{:S(2)}) collective-permute-start(bf16[2,2,256,128]{3,2,1,0:T(8,128)(2,1)} %get-tuple-element.67), channel_id=1, source_target_pairs={{0,24},{4,28},{8,16},{12,20},{16,8},{20,12},{24,0},{28,4},{1,25},{... | collective-permute-start | bytes 786440 | tf_op jit(solution)/shard_map/ppermute | solution.py:198
  16.1 29.2 %collective-permute-start.6 = (bf16[2,2,256,128]{3,2,1,0:T(8,128)(2,1)}, bf16[2,2,256,128]{3,2,1,0:T(8,128)(2,1)S(1)}, u32[]{:S(2)}, u32[]{:S(2)}) collective-permute-start(bf16[2,2,256,128]{3,2,1,0:T(8,128)(2,1)} %get-tuple-element.68), channel_id=1, source_target_pairs={{0,28},{4,24},{8,20},{12,16},{16,12},{20,8},{24,4},{28,0},{1,29},{... | collective-permute-start | bytes 786440 | tf_op jit(solution)/shard_map/ppermute | solution.py:198
  20.4 25.9 %collective-permute-start.20 = (bf16[2,2,256,128]{3,2,1,0:T(8,128)(2,1)}, bf16[2,2,256,128]{3,2,1,0:T(8,128)(2,1)S(1)}, u32[]{:S(2)}, u32[]{:S(2)}) collective-permute-start(bf16[2,2,256,128]{3,2,1,0:T(8,128)(2,1)} %get-tuple-element.86), channel_id=1, source_target_pairs={{0,4},{4,0},{8,12},{12,8},{16,20},{20,16},{24,28},{28,24},{1,5},{5... | collective-permute-start | bytes 786440 | tf_op jit(solution)/shard_map/ppermute | solution.py:198
  21.9 27.9 %collective-permute-start.21 = (bf16[2,2,256,128]{3,2,1,0:T(8,128)(2,1)}, bf16[2,2,256,128]{3,2,1,0:T(8,128)(2,1)S(1)}, u32[]{:S(2)}, u32[]{:S(2)}) collective-permute-start(bf16[2,2,256,128]{3,2,1,0:T(8,128)(2,1)} %get-tuple-element.87), channel_id=1, source_target_pairs={{0,8},{4,12},{8,0},{12,4},{16,24},{20,28},{24,16},{28,20},{1,9},{5... | collective-permute-start | bytes 786440 | tf_op jit(solution)/shard_map/ppermute | solution.py:198
  43.1 15.4 %collective-permute-start.22 = (bf16[2,2,256,128]{3,2,1,0:T(8,128)(2,1)}, bf16[2,2,256,128]{3,2,1,0:T(8,128)(2,1)}, u32[]{:S(2)}, u32[]{:S(2)}) collective-permute-start(bf16[2,2,256,128]{3,2,1,0:T(8,128)(2,1)} %get-tuple-element.88), channel_id=1, source_target_pairs={{0,12},{4,8},{8,4},{12,0},{16,28},{20,24},{24,20},{28,16},{1,13},{... | collective-permute-start | bytes 786440 | tf_op jit(solution)/shard_map/ppermute | solution.py:198
  43.8 20.7 %collective-permute-start.23 = (bf16[2,2,256,128]{3,2,1,0:T(8,128)(2,1)}, bf16[2,2,256,128]{3,2,1,0:T(8,128)(2,1)}, u32[]{:S(2)}, u32[]{:S(2)}) collective-permute-start(bf16[2,2,256,128]{3,2,1,0:T(8,128)(2,1)} %get-tuple-element.89), channel_id=1, source_target_pairs={{0,16},{4,20},{8,24},{12,28},{16,0},{20,4},{24,8},{28,12},{1,17},{... | collective-permute-start | bytes 786440 | tf_op jit(solution)/shard_map/ppermute | solution.py:198
  46.1 23.1 %collective-permute-start.24 = (bf16[2,2,256,128]{3,2,1,0:T(8,128)(2,1)}, bf16[2,2,256,128]{3,2,1,0:T(8,128)(2,1)}, u32[]{:S(2)}, u32[]{:S(2)}) collective-permute-start(bf16[2,2,256,128]{3,2,1,0:T(8,128)(2,1)} %get-tuple-element.90), channel_id=1, source_target_pairs={{0,20},{4,16},{8,28},{12,24},{16,4},{20,0},{24,12},{28,8},{1,21},{... | collective-permute-start | bytes 786440 | tf_op jit(solution)/shard_map/ppermute | solution.py:198
  47.1 26.1 %collective-permute-start.25 = (bf16[2,2,256,128]{3,2,1,0:T(8,128)(2,1)}, bf16[2,2,256,128]{3,2,1,0:T(8,128)(2,1)}, u32[]{:S(2)}, u32[]{:S(2)}) collective-permute-start(bf16[2,2,256,128]{3,2,1,0:T(8,128)(2,1)} %get-tuple-element.91), channel_id=1, source_target_pairs={{0,24},{4,28},{8,16},{12,20},{16,8},{20,12},{24,0},{28,4},{1,25},{... | collective-permute-start | bytes 786440 | tf_op jit(solution)/shard_map/ppermute | solution.py:198
  50.4 22.7 %collective-permute-start.26 = (bf16[2,2,256,128]{3,2,1,0:T(8,128)(2,1)}, bf16[2,2,256,128]{3,2,1,0:T(8,128)(2,1)}, u32[]{:S(2)}, u32[]{:S(2)}) collective-permute-start(bf16[2,2,256,128]{3,2,1,0:T(8,128)(2,1)} %get-tuple-element.92), channel_id=1, source_target_pairs={{0,28},{4,24},{8,20},{12,16},{16,12},{20,8},{24,4},{28,0},{1,29},{... | collective-permute-start | bytes 786440 | tf_op jit(solution)/shard_map/ppermute | solution.py:198
  58.6 19.1 %collective-permute-start.7 = (bf16[64,1152]{1,0:T(8,128)(2,1)S(1)}, bf16[64,1152]{1,0:T(8,128)(2,1)S(1)}, u32[]{:S(2)}, u32[]{:S(2)}) collective-permute-start(bf16[64,1152]{1,0:T(8,128)(2,1)S(1)} %get-tuple-element.70), channel_id=1, source_target_pairs={{0,1},{1,0},{2,3},{3,2},{4,5},{5,4},{6,7},{7,6},{8,9},{9,8},{10,11... | collective-permute-start | bytes 442376 | tf_op jit(solution)/shard_map/ppermute | solution.py:198
  64.5 17.0 %collective-permute-start.8 = (bf16[64,1152]{1,0:T(8,128)(2,1)S(1)}, bf16[64,1152]{1,0:T(8,128)(2,1)S(1)}, u32[]{:S(2)}, u32[]{:S(2)}) collective-permute-start(bf16[64,1152]{1,0:T(8,128)(2,1)S(1)} %get-tuple-element.71), channel_id=1, source_target_pairs={{0,2},{1,3},{2,0},{3,1},{4,6},{5,7},{6,4},{7,5},{8,10},{9,11},{10,... | collective-permute-start | bytes 442376 | tf_op jit(solution)/shard_map/ppermute | solution.py:198
  77.0 15.4 %collective-permute-start.28 = (bf16[64,1152]{1,0:T(8,128)(2,1)S(1)}, bf16[64,1152]{1,0:T(8,128)(2,1)S(1)}, u32[]{:S(2)}, u32[]{:S(2)}) collective-permute-start(bf16[64,1152]{1,0:T(8,128)(2,1)S(1)} %get-tuple-element.95), channel_id=1, source_target_pairs={{0,2},{1,3},{2,0},{3,1},{4,6},{5,7},{6,4},{7,5},{8,10},{9,11},{10,... | collective-permute-start | bytes 442376 | tf_op jit(solution)/shard_map/ppermute | solution.py:198
  77.7 14.7 %collective-permute-start.29 = (bf16[64,1152]{1,0:T(8,128)(2,1)S(1)}, bf16[64,1152]{1,0:T(8,128)(2,1)S(1)}, u32[]{:S(2)}, u32[]{:S(2)}) collective-permute-start(bf16[64,1152]{1,0:T(8,128)(2,1)S(1)} %get-tuple-element.96), channel_id=1, source_target_pairs={{0,3},{1,2},{2,1},{3,0},{4,7},{5,6},{6,5},{7,4},{8,11},{9,10},{10,... | collective-permute-start | bytes 442376 | tf_op jit(solution)/shard_map/ppermute | solution.py:198
  82.7 19.8 %collective-permute-start.10 = (bf16[64,1152]{1,0:T(8,128)(2,1)S(1)}, bf16[64,1152]{1,0:T(8,128)(2,1)S(1)}, u32[]{:S(2)}, u32[]{:S(2)}) collective-permute-start(bf16[64,1152]{1,0:T(8,128)(2,1)S(1)} %get-tuple-element.74), channel_id=1, source_target_pairs={{0,1},{1,0},{2,3},{3,2},{4,5},{5,4},{6,7},{7,6},{8,9},{9,8},{10,11... | collective-permute-start | bytes 442376 | tf_op jit(solution)/shard_map/ppermute | solution.py:198
  82.7 22.1 %collective-permute-start.11 = (bf16[64,1152]{1,0:T(8,128)(2,1)S(1)}, bf16[64,1152]{1,0:T(8,128)(2,1)S(1)}, u32[]{:S(2)}, u32[]{:S(2)}) collective-permute-start(bf16[64,1152]{1,0:T(8,128)(2,1)S(1)} %get-tuple-element.75), channel_id=1, source_target_pairs={{0,2},{1,3},{2,0},{3,1},{4,6},{5,7},{6,4},{7,5},{8,10},{9,11},{10,... | collective-permute-start | bytes 442376 | tf_op jit(solution)/shard_map/ppermute | solution.py:198
  84.0 20.8 %collective-permute-start.12 = (bf16[64,1152]{1,0:T(8,128)(2,1)S(1)}, bf16[64,1152]{1,0:T(8,128)(2,1)S(1)}, u32[]{:S(2)}, u32[]{:S(2)}) collective-permute-start(bf16[64,1152]{1,0:T(8,128)(2,1)S(1)} %get-tuple-element.76), channel_id=1, source_target_pairs={{0,3},{1,2},{2,1},{3,0},{4,7},{5,6},{6,5},{7,4},{8,11},{9,10},{10,... | collective-permute-start | bytes 442376 | tf_op jit(solution)/shard_map/ppermute | solution.py:198
  93.6 16.4 %collective-permute-start.30 = (bf16[64,1152]{1,0:T(8,128)(2,1)S(1)}, bf16[64,1152]{1,0:T(8,128)(2,1)S(1)}, u32[]{:S(2)}, u32[]{:S(2)}) collective-permute-start(bf16[64,1152]{1,0:T(8,128)(2,1)S(1)} %get-tuple-element.98), channel_id=1, source_target_pairs={{0,1},{1,0},{2,3},{3,2},{4,5},{5,4},{6,7},{7,6},{8,9},{9,8},{10,11... | collective-permute-start | bytes 442376 | tf_op jit(solution)/shard_map/ppermute | solution.py:198
  102.4 14.0 %collective-permute-start.31 = (bf16[64,1152]{1,0:T(8,128)(2,1)S(1)}, bf16[64,1152]{1,0:T(8,128)(2,1)S(1)}, u32[]{:S(2)}, u32[]{:S(2)}) collective-permute-start(bf16[64,1152]{1,0:T(8,128)(2,1)S(1)} %get-tuple-element.99), channel_id=1, source_target_pairs={{0,2},{1,3},{2,0},{3,1},{4,6},{5,7},{6,4},{7,5},{8,10},{9,11},{10,... | collective-permute-start | bytes 442376 | tf_op jit(solution)/shard_map/ppermute | solution.py:198
  102.5 13.9 %collective-permute-start.32 = (bf16[64,1152]{1,0:T(8,128)(2,1)S(1)}, bf16[64,1152]{1,0:T(8,128)(2,1)S(1)}, u32[]{:S(2)}, u32[]{:S(2)}) collective-permute-start(bf16[64,1152]{1,0:T(8,128)(2,1)S(1)} %get-tuple-element.100), channel_id=1, source_target_pairs={{0,3},{1,2},{2,1},{3,0},{4,7},{5,6},{6,5},{7,4},{8,11},{9,10},{10,... | collective-permute-start | bytes 442376 | tf_op jit(solution)/shard_map/ppermute | solution.py:198
  108.2 13.5 %collective-permute-start.13 = (bf16[2,2,256,128]{3,2,1,0:T(8,128)(2,1)S(1)}, bf16[2,2,256,128]{3,2,1,0:T(8,128)(2,1)S(1)}, u32[]{:S(2)}, u32[]{:S(2)}) collective-permute-start(bf16[2,2,256,128]{3,2,1,0:T(8,128)(2,1)S(1)} %get-tuple-element.78), channel_id=1, source_target_pairs={{0,4},{4,0},{8,12},{12,8},{16,20},{20,16},{24,28},{28,24},{1,5},{5... | collective-permute-start | bytes 786440 | tf_op jit(solution)/shard_map/ppermute | solution.py:198
  108.2 15.0 %collective-permute-start.14 = (bf16[2,2,256,128]{3,2,1,0:T(8,128)(2,1)S(1)}, bf16[2,2,256,128]{3,2,1,0:T(8,128)(2,1)S(1)}, u32[]{:S(2)}, u32[]{:S(2)}) collective-permute-start(bf16[2,2,256,128]{3,2,1,0:T(8,128)(2,1)S(1)} %get-tuple-element.79), channel_id=1, source_target_pairs={{0,8},{4,12},{8,0},{12,4},{16,24},{20,28},{24,16},{28,20},{1,9},{5... | collective-permute-start | bytes 786440 | tf_op jit(solution)/shard_map/ppermute | solution.py:198
  121.6 14.3 %collective-permute-start.36 = (bf16[2,2,256,128]{3,2,1,0:T(8,128)(2,1)S(1)}, bf16[2,2,256,128]{3,2,1,0:T(8,128)(2,1)S(1)}, u32[]{:S(2)}, u32[]{:S(2)}) collective-permute-start(bf16[2,2,256,128]{3,2,1,0:T(8,128)(2,1)S(1)} %get-tuple-element.105), channel_id=1, source_target_pairs={{0,16},{4,20},{8,24},{12,28},{16,0},{20,4},{24,8},{28,12},{1,17},{... | collective-permute-start | bytes 786440 | tf_op jit(solution)/shard_map/ppermute | solution.py:198
  123.2 23.5 %collective-permute-start.37 = (bf16[2,2,256,128]{3,2,1,0:T(8,128)(2,1)S(1)}, bf16[2,2,256,128]{3,2,1,0:T(8,128)(2,1)S(1)}, u32[]{:S(2)}, u32[]{:S(2)}) collective-permute-start(bf16[2,2,256,128]{3,2,1,0:T(8,128)(2,1)S(1)} %get-tuple-element.106), channel_id=1, source_target_pairs={{0,20},{4,16},{8,28},{12,24},{16,4},{20,0},{24,12},{28,8},{1,21},{... | collective-permute-start | bytes 786440 | tf_op jit(solution)/shard_map/ppermute | solution.py:198
  123.3 25.6 %collective-permute-start.38 = (bf16[2,2,256,128]{3,2,1,0:T(8,128)(2,1)S(1)}, bf16[2,2,256,128]{3,2,1,0:T(8,128)(2,1)S(1)}, u32[]{:S(2)}, u32[]{:S(2)}) collective-permute-start(bf16[2,2,256,128]{3,2,1,0:T(8,128)(2,1)S(1)} %get-tuple-element.107), channel_id=1, source_target_pairs={{0,24},{4,28},{8,16},{12,20},{16,8},{20,12},{24,0},{28,4},{1,25},{... | collective-permute-start | bytes 786440 | tf_op jit(solution)/shard_map/ppermute | solution.py:198
  128.9 21.5 %collective-permute-start.39 = (bf16[2,2,256,128]{3,2,1,0:T(8,128)(2,1)S(1)}, bf16[2,2,256,128]{3,2,1,0:T(8,128)(2,1)S(1)}, u32[]{:S(2)}, u32[]{:S(2)}) collective-permute-start(bf16[2,2,256,128]{3,2,1,0:T(8,128)(2,1)S(1)} %get-tuple-element.108), channel_id=1, source_target_pairs={{0,28},{4,24},{8,20},{12,16},{16,12},{20,8},{24,4},{28,0},{1,29},{... | collective-permute-start | bytes 786440 | tf_op jit(solution)/shard_map/ppermute | solution.py:198
  133.7 18.7 %collective-permute-start.15 = (bf16[2,2,256,128]{3,2,1,0:T(8,128)(2,1)S(1)}, bf16[2,2,256,128]{3,2,1,0:T(8,128)(2,1)S(1)}, u32[]{:S(2)}, u32[]{:S(2)}) collective-permute-start(bf16[2,2,256,128]{3,2,1,0:T(8,128)(2,1)S(1)} %get-tuple-element.80), channel_id=1, source_target_pairs={{0,12},{4,8},{8,4},{12,0},{16,28},{20,24},{24,20},{28,16},{1,13},{... | collective-permute-start | bytes 786440 | tf_op jit(solution)/shard_map/ppermute | solution.py:198
  135.9 28.5 %collective-permute-start.16 = (bf16[2,2,256,128]{3,2,1,0:T(8,128)(2,1)S(1)}, bf16[2,2,256,128]{3,2,1,0:T(8,128)(2,1)S(1)}, u32[]{:S(2)}, u32[]{:S(2)}) collective-permute-start(bf16[2,2,256,128]{3,2,1,0:T(8,128)(2,1)S(1)} %get-tuple-element.81), channel_id=1, source_target_pairs={{0,16},{4,20},{8,24},{12,28},{16,0},{20,4},{24,8},{28,12},{1,17},{... | collective-permute-start | bytes 786440 | tf_op jit(solution)/shard_map/ppermute | solution.py:198
  146.7 22.2 %collective-permute-start.17 = (bf16[2,2,256,128]{3,2,1,0:T(8,128)(2,1)S(1)}, bf16[2,2,256,128]{3,2,1,0:T(8,128)(2,1)S(1)}, u32[]{:S(2)}, u32[]{:S(2)}) collective-permute-start(bf16[2,2,256,128]{3,2,1,0:T(8,128)(2,1)S(1)} %get-tuple-element.82), channel_id=1, source_target_pairs={{0,20},{4,16},{8,28},{12,24},{16,4},{20,0},{24,12},{28,8},{1,21},{... | collective-permute-start | bytes 786440 | tf_op jit(solution)/shard_map/ppermute | solution.py:198
  148.9 20.0 %collective-permute-start.18 = (bf16[2,2,256,128]{3,2,1,0:T(8,128)(2,1)S(1)}, bf16[2,2,256,128]{3,2,1,0:T(8,128)(2,1)S(1)}, u32[]{:S(2)}, u32[]{:S(2)}) collective-permute-start(bf16[2,2,256,128]{3,2,1,0:T(8,128)(2,1)S(1)} %get-tuple-element.83), channel_id=1, source_target_pairs={{0,24},{4,28},{8,16},{12,20},{16,8},{20,12},{24,0},{28,4},{1,25},{... | collective-permute-start | bytes 786440 | tf_op jit(solution)/shard_map/ppermute | solution.py:198
  150.5 18.5 %collective-permute-start.19 = (bf16[2,2,256,128]{3,2,1,0:T(8,128)(2,1)S(1)}, bf16[2,2,256,128]{3,2,1,0:T(8,128)(2,1)S(1)}, u32[]{:S(2)}, u32[]{:S(2)}) collective-permute-start(bf16[2,2,256,128]{3,2,1,0:T(8,128)(2,1)S(1)} %get-tuple-element.84), channel_id=1, source_target_pairs={{0,28},{4,24},{8,20},{12,16},{16,12},{20,8},{24,4},{28,0},{1,29},{... | collective-permute-start | bytes 786440 | tf_op jit(solution)/shard_map/ppermute | solution.py:198
  (29 other events, 243.5 us)

commit v2 on v1

v2 whole, which is shorter than its diff:
```python
import functools

import jax
import jax.numpy as jnp
from jax import lax
from jax.experimental import pallas as pl
from jax.experimental.pallas import tpu as pltpu
from jax.sharding import PartitionSpec as P

coupling = 2.0
LANES = 128
VMEM_BYTES = 48 * 1024 * 1024


def packed_counts(wave_a, wave_b, parity, modes):
    count_a = lax.shift_right_arithmetic(modes + 1 - wave_a - parity, 1)
    count_b = lax.shift_right_arithmetic(modes + 1 - wave_b - parity, 1)
    return count_a, count_b


def table_kernel(cut, wave, leg, *refs):
    lat_n, width, k_half = cut["lat"], cut["cycles"], leg.shape[3]
    table0, table1 = refs[-2:]
    me = lax.axis_index("lat")
    modes = 2 * k_half
    wave_a, wave_b = wave[2 * me], wave[2 * me + 1]
    for parity, table in enumerate((table0, table1)):
        kk = table.shape[1]
        count_a, count_b = packed_counts(wave_a, wave_b, parity, modes)
        row = lax.broadcasted_iota(jnp.int32, (k_half, kk), 0)
        col = lax.broadcasted_iota(jnp.int32, (k_half, kk), 1)
        pick = jnp.where((col == row + count_a) & (row < count_b), 1.0, 0.0).astype(jnp.bfloat16)
        kept = lax.broadcasted_iota(jnp.int32, (width, k_half), 1) < count_a
        blocks = []
        for step in range(lat_n):
            owner = jnp.bitwise_xor(me, step)
            place = pl.ds(pl.multiple_of(owner * width, width), width)
            first = jnp.where(kept, leg[0, parity, place, :].astype(jnp.float32), 0.0)
            table[step * width : (step + 1) * width, :k_half] = first.astype(jnp.bfloat16)
            if kk > k_half:
                table[step * width : (step + 1) * width, k_half:] = jnp.zeros(
                    (width, kk - k_half), jnp.bfloat16
                )
            blocks.append(leg[1, parity, place, :])
        table[lat_n * width :, :] = jnp.dot(
            jnp.concatenate(blocks, axis=0), pick, preferred_element_type=jnp.float32
        ).astype(jnp.bfloat16)


def fold_kernel(cut, row0, wave_in, quad_in, cycles_in, grid, *refs):
    lat_n = cut["lat"]
    outs = refs[-6 - lat_n // 2 : -6]
    held, wave, quad, cycles, sems, small = refs[-6:]
    rows = held.shape[3]
    me = lax.axis_index("lat")
    copies = [
        pltpu.make_async_copy(wave_in, wave, small.at[0]),
        pltpu.make_async_copy(quad_in, quad, small.at[1]),
        pltpu.make_async_copy(cycles_in, cycles, small.at[2]),
    ]
    for step in range(lat_n):
        owner = jnp.bitwise_xor(me, step)
        copies.append(
            pltpu.make_async_copy(
                grid.at[pl.ds(2 * owner, 2), :, pl.ds(row0, rows), :],
                held.at[step],
                sems.at[step],
            )
        )
    for copy in copies:
        copy.start()
    for copy in copies[:3]:
        copy.wait()
    for step in range(lat_n):
        owner = jnp.bitwise_xor(me, step)
        copies[3 + step].wait()
        for slot in range(2):
            weight = jnp.where(2 * wave[2 * owner + slot] < cycles[...], quad[...], 0.0)[None]
            north = held[step, slot, 0].astype(jnp.float32)
            south = held[step, slot, 1].astype(jnp.float32)
            outs[step // 2][step % 2, slot, 0] = (weight * (north + south)).astype(jnp.bfloat16)
            outs[step // 2][step % 2, slot, 1] = (weight * (north - south)).astype(jnp.bfloat16)


def in_order(values):
    me, bit = lax.axis_index("lev"), 1
    while bit < len(values):
        turned = jnp.bitwise_and(me, bit) > 0
        values = [jnp.where(turned, values[r ^ bit], values[r]) for r in range(len(values))]
        bit *= 2
    return values


def gather_kernel(cut, *refs):
    parts, out = refs[: cut["lat"] // 2], refs[-1]
    for step, part in enumerate(parts):
        out[step] = part[1]


def forward_kernel(cut, table0, table1, *refs):
    lat_n, lev_n = cut["lat"], cut["lev"]
    near, swapped, outs = refs[: lat_n // 2], refs[lat_n // 2], refs[-lev_n:]
    share = outs[0].shape[0]
    at = 0
    for parity, table in enumerate((table0, table1)):
        kk = table.shape[1]
        values = jnp.concatenate(
            [
                swapped[step // 2, slot, parity] if step % 2 else near[step // 2][0, slot, parity]
                for slot in range(2)
                for step in range(lat_n)
            ],
            axis=1,
        )
        packed = jnp.dot(values, table[...], preferred_element_type=jnp.float32)
        packed = packed.astype(jnp.bfloat16)
        shares = in_order([packed[r * share : (r + 1) * share] for r in range(lev_n)])
        for out, values in zip(outs, shares):
            out[:, at : at + kk] = values
        at += kk


def solve_kernel(cut, wave, project, vertical, rates, *refs):
    lev_n, levels, k_half, kk0 = cut["lev"], cut["levels"], cut["k_half"], cut["kk"][0]
    parts, outs = refs[:lev_n], refs[-lev_n:]
    rows, kk_all = parts[0].shape
    me = lax.axis_index("lat")

    modes = 2 * k_half
    wave_a, wave_b = wave[2 * me], wave[2 * me + 1]
    column = lax.broadcasted_iota(jnp.int32, (8, kk_all), 1)
    odd = column >= kk0
    counts = [packed_counts(wave_a, wave_b, parity, modes) for parity in range(2)]
    count_a = jnp.where(odd, counts[1][0], counts[0][0])
    count_b = jnp.where(odd, counts[1][1], counts[0][1])
    parity = jnp.where(odd, 1, 0)
    place = jnp.where(odd, column - kk0, column)
    order = parity + jnp.where(
        place < count_a, wave_a + 2 * place, wave_b + 2 * (place - count_a)
    )
    order = jnp.where(place < count_a + count_b, order, 0).astype(jnp.float32)
    growth = (coupling * order * (order + 1.0) / (modes * modes))[:1]
    across = jnp.broadcast_to(rates[...].reshape(1, -1), (LANES, rates.shape[0]))
    damping = 1.0 + growth * across.T[:, :1]
    for col in range(rows // levels):
        at = slice(col * levels, (col + 1) * levels)
        values = in_order([parts[step][at, :] for step in range(lev_n)])
        projected = jnp.dot(
            project[...], jnp.concatenate(values, axis=0), preferred_element_type=jnp.float32
        )
        damped = (projected / damping).astype(jnp.bfloat16)
        solved = jnp.dot(
            vertical[...], damped, preferred_element_type=jnp.float32
        ).astype(jnp.bfloat16)
        values = in_order(
            [solved[step * levels : (step + 1) * levels] for step in range(lev_n)]
        )
        for step in range(lev_n):
            outs[step][at, :] = values[step]


def inverse_kernel(cut, table0, table1, *refs):
    lat_n, lev_n, width = cut["lat"], cut["lev"], cut["cycles"]
    parts, near, swapped = refs[:lev_n], refs[-1 - lat_n // 2 : -1], refs[-1]
    at = 0
    for parity, table in enumerate((table0, table1)):
        kk = table.shape[1]
        shares = in_order([part[:, at : at + kk] for part in parts])
        returned = lax.dot_general(
            jnp.concatenate(shares, axis=0),
            table[...],
            (((1,), (1,)), ((), ())),
            preferred_element_type=jnp.float32,
        ).astype(jnp.bfloat16)
        for slot in range(2):
            for step in range(lat_n):
                start = (slot * lat_n + step) * width
                part = returned[:, start : start + width]
                if step % 2:
                    swapped[step // 2, slot, parity] = part
                else:
                    near[step // 2][0, slot, parity] = part
        at += kk


def merge_kernel(cut, swapped, *refs):
    outs = refs[-(cut["lat"] // 2) :]
    for step, out in enumerate(outs):
        out[1] = swapped[step]


def unfold_kernel(cut, row0, wave, cycles, *refs):
    lat_n = cut["lat"]
    parts = refs[: lat_n // 2]
    out, held, sems = refs[-3:]
    rows = held.shape[3]
    me = lax.axis_index("lat")
    copies = []
    for step in range(lat_n):
        owner = jnp.bitwise_xor(me, step)
        for slot in range(2):
            seen = 2 * wave[2 * owner + slot] < cycles[...]
            even = parts[step // 2][step % 2, slot, 0].astype(jnp.float32)
            odd = parts[step // 2][step % 2, slot, 1].astype(jnp.float32)
            held[step, slot, 0] = jnp.where(seen, even + odd, 0.0).astype(jnp.bfloat16)
            held[step, slot, 1] = jnp.where(seen, even - odd, 0.0).astype(jnp.bfloat16)
        copy = pltpu.make_async_copy(
            held.at[step], out.at[pl.ds(2 * owner, 2), :, pl.ds(row0, rows), :], sems.at[step]
        )
        copy.start()
        copies.append(copy)
    for copy in copies:
        copy.wait()


vmem = pl.BlockSpec(memory_space=pltpu.VMEM)
smem = pl.BlockSpec(memory_space=pltpu.SMEM)
anywhere = pl.BlockSpec(memory_space=pl.ANY)
in_hbm = pl.BlockSpec(memory_space=pltpu.HBM)


def call(body, name, ins, in_specs, outs, out_specs, scratch, aliases=None, after=()):
    return pl.pallas_call(
        body,
        name=name,
        out_shape=list(outs),
        in_specs=list(in_specs) + [anywhere] * len(after),
        out_specs=list(out_specs),
        scratch_shapes=list(scratch),
        input_output_aliases=aliases or {},
        cost_estimate=pl.CostEstimate(flops=0, bytes_accessed=0, transcendentals=0),
        compiler_params=pltpu.CompilerParams(vmem_limit_bytes=VMEM_BYTES),
    )(*ins, *after)


def struct(*shape):
    return jax.ShapeDtypeStruct(shape, jnp.bfloat16)


def exchange(parts, axis, count, stride=1):
    return [parts[0]] + [
        lax.ppermute(part, axis, [(i, i ^ (r * stride)) for i in range(count)])
        for r, part in enumerate(parts)
        if r
    ]


def between_levels(parts, count):
    out = [parts[0]]
    for r in range(1, count):
        part = parts[r]
        if r > 2:
            part, out[r - 2] = lax.optimization_barrier((part, out[r - 2]))
        out.append(lax.ppermute(part, "lev", [(i, i ^ r) for i in range(count)]))
    return out


def swap_cores(array, count):
    return lax.ppermute(array, "lat", [(i, i ^ 1) for i in range(count)])


def blocks_of(cols, lev_n):
    pieces = 2
    while pieces > 1 and cols % (pieces * lev_n):
        pieces //= 2
    return [(p * cols // pieces, cols // pieces) for p in range(pieces)]


def local_packed(
    lat_n, lev_n, grid, legendre, quad, cycle_points, wave_ids, projection, vertical, rates
):
    slots, width, halves, parts_c, fields, levels = grid.shape
    k_half = legendre.shape[3]
    cols = parts_c * fields
    kk = (-(-(k_half + 1) // LANES) * LANES, k_half)
    kk_all = sum(kk)
    wide = 2 * lat_n * width
    cut = {
        "lat": lat_n,
        "lev": lev_n,
        "cycles": width,
        "levels": levels,
        "k_half": k_half,
        "kk": kk,
    }
    lines = jnp.transpose(grid, (0, 2, 3, 4, 5, 1)).reshape(slots, halves, cols * levels, width)
    cycle_row = cycle_points.reshape(1, width)

    blocks = blocks_of(cols, lev_n)
    near_n = lat_n // 2
    last = ()
    arrived = []
    for first, count in blocks:
        rows = count * levels
        folded = call(
            functools.partial(fold_kernel, cut, first * levels),
            "fold",
            (wave_ids, quad, cycle_points, lines),
            [in_hbm] * 4,
            [struct(2, 2, 2, rows, width)] * near_n,
            [vmem] * near_n,
            [
                pltpu.VMEM((lat_n, 2, 2, rows, width), jnp.bfloat16),
                pltpu.SMEM((slots,), jnp.int32),
                pltpu.VMEM((width,), jnp.float32),
                pltpu.VMEM((width,), jnp.int32),
                pltpu.SemaphoreType.DMA((lat_n,)),
                pltpu.SemaphoreType.DMA((3,)),
            ],
            after=last,
        )
        last = (folded[0],)
        arrived.append(exchange(folded, "lat", lat_n, 2))

    table0, table1 = call(
        functools.partial(table_kernel, cut),
        "tables",
        (wave_ids, legendre),
        (smem, vmem),
        [struct(wide, kk[0]), struct(wide, kk[1])],
        [vmem] * 2,
        [],
        after=last,
    )
    last = (table1,)

    def forward(block, last):
        rows = blocks[block][1] * levels
        share = rows // lev_n
        near = arrived[block]
        (swapped,) = call(
            functools.partial(gather_kernel, cut),
            "gather",
            near,
            [vmem] * near_n,
            [struct(near_n, 2, 2, rows, width)],
            [vmem],
            [],
            after=last,
        )
        swapped = swap_cores(swapped, lat_n)
        packed = call(
            functools.partial(forward_kernel, cut),
            "forward",
            (table0, table1, *near, swapped),
            [vmem] * (3 + near_n),
            [struct(share, kk_all)] * lev_n,
            [vmem] * lev_n,
            [],
        )
        return between_levels(packed, lev_n), (packed[0],)

    def solve(packed, last):
        share = packed[0].shape[0]
        solved = call(
            functools.partial(solve_kernel, cut),
            "solve",
            (wave_ids, projection, vertical, rates, *packed),
            [smem] + [vmem] * (3 + lev_n),
            [struct(share, kk_all)] * lev_n,
            [vmem] * lev_n,
            [],
            after=last,
        )
        return between_levels(solved, lev_n), (solved[0],)

    def inverse(solved, last):
        rows = solved[0].shape[0] * lev_n
        *near, swapped = call(
            functools.partial(inverse_kernel, cut),
            "inverse",
            (table0, table1, *solved),
            [vmem] * (2 + lev_n),
            [struct(2, 2, 2, rows, width)] * near_n + [struct(near_n, 2, 2, rows, width)],
            [vmem] * (near_n + 1),
            [],
            after=last,
        )
        swapped = swap_cores(swapped, lat_n)
        merged = call(
            functools.partial(merge_kernel, cut),
            "merge",
            (swapped, *near),
            [vmem] * (1 + near_n),
            [struct(2, 2, 2, rows, width)] * near_n,
            [vmem] * near_n,
            [],
            aliases={1 + r: r for r in range(near_n)},
        )
        return exchange(merged, "lat", lat_n, 2), (merged[0],)

    def unfold(block, returned, out):
        rows = blocks[block][1] * levels
        return call(
            functools.partial(unfold_kernel, cut, blocks[block][0] * levels),
            "unfold",
            (wave_ids, cycle_row, *returned) + out,
            [smem] + [vmem] * (1 + near_n) + [anywhere] * len(out),
            [struct(slots, halves, cols * levels, width)],
            [anywhere],
            [
                pltpu.VMEM((lat_n, 2, 2, rows, width), jnp.bfloat16),
                pltpu.SemaphoreType.DMA((lat_n,)),
            ],
            aliases={2 + near_n: 0} if out else None,
        )

    count = len(blocks)
    packed, solved, returned = [None] * count, [None] * count, [None] * count
    for turn in range(count + 2):
        if 0 <= turn - 2:
            before = returned[turn - 3][1:] if turn - 3 >= 0 else []
            returned[turn - 2], last = inverse(solved[turn - 2], (*last, *before))
        if 0 <= turn - 1 < count:
            solved[turn - 1], last = solve(packed[turn - 1], last)
        if turn < count:
            packed[turn], last = forward(turn, last)
    out = ()
    for block in range(count):
        out = tuple(unfold(block, returned[block], out))
    (out,) = out
    out = out.reshape(slots, halves, parts_c, fields, levels, width)
    return jnp.transpose(out, (0, 5, 1, 2, 3, 4))


def local_plain(
    lat_n, lev_n, grid, legendre, quad, cycle_points, wave_ids, projection, vertical, rates
):
    slots, width = grid.shape[:2]
    fields, levels = grid.shape[4:]
    owned, cycles_all, k_half = legendre.shape[0], legendre.shape[2], legendre.shape[3]
    modes = 2 * k_half
    levels_all = projection.shape[0]
    present = (2 * wave_ids[:, None] < cycle_points[None, :]).astype(jnp.float32)
    weighting = (present * quad[None, :])[:, :, None, None, None]
    north, south = grid[:, :, 0].astype(jnp.float32), grid[:, :, 1].astype(jnp.float32)
    even = (weighting * (north + south)).astype(jnp.bfloat16)
    odd = (weighting * (north - south)).astype(jnp.bfloat16)
    folded = jnp.stack([even, odd], axis=2).reshape(slots, width, 2, 2 * fields, levels)
    wave_local = lax.dynamic_slice_in_dim(wave_ids, lax.axis_index("lat") * owned, owned)
    order = (
        wave_local[:, None, None]
        + jnp.arange(2, dtype=jnp.int32)[None, :, None]
        + 2 * jnp.arange(k_half, dtype=jnp.int32)[None, None, :]
    )
    values = lax.all_to_all(folded, "lat", split_axis=0, concat_axis=1, tiled=True)
    values = lax.all_to_all(values, "lev", split_axis=3, concat_axis=4, tiled=True)
    mixed = values.shape[3]
    values = values.reshape(owned, cycles_all, 2, -1)
    spectral = jnp.einsum("spjk,sjpc->spkc", legendre, values, preferred_element_type=jnp.float32)
    spectral = jnp.where((order <= modes - 1)[..., None], spectral, 0.0).astype(jnp.bfloat16)
    spectral = spectral.reshape(owned, 2, k_half, mixed, levels_all)
    order = order.astype(jnp.float32)
    growth = (coupling * order * (order + 1.0) / (modes * modes))[..., None, None]
    last = (((4,), (1,)), ((), ()))
    projected = lax.dot_general(spectral, projection, last, preferred_element_type=jnp.float32)
    damped = (projected / (1.0 + growth * rates)).astype(jnp.bfloat16)
    solved = lax.dot_general(damped, vertical, last, preferred_element_type=jnp.float32)
    solved = solved.astype(jnp.bfloat16).reshape(owned, 2, k_half, -1)
    returned = jnp.einsum("spjk,spkc->sjpc", legendre, solved, preferred_element_type=jnp.float32)
    returned = returned.astype(jnp.bfloat16).reshape(owned, cycles_all, 2, mixed, levels_all)
    back = lax.all_to_all(returned, "lat", split_axis=1, concat_axis=0, tiled=True)
    back = lax.all_to_all(back, "lev", split_axis=4, concat_axis=3, tiled=True)
    back = back.reshape(slots, width, 2, 2, fields, levels).astype(jnp.float32)
    seen = present[:, :, None, None, None]
    north, south = seen * (back[:, :, 0] + back[:, :, 1]), seen * (back[:, :, 0] - back[:, :, 1])
    return jnp.stack([north, south], axis=2).astype(jnp.bfloat16)


def local(lat_n, lev_n, grid, legendre, *rest):
    width, levels = grid.shape[1], grid.shape[5]
    fits = (
        legendre.shape[0] == 2
        and lat_n & (lat_n - 1) == 0
        and lev_n & (lev_n - 1) == 0
        and width % LANES == 0
        and legendre.shape[3] % LANES == 0
        and levels % 16 == 0
        and lev_n * levels % LANES == 0
        and (grid.shape[3] * grid.shape[4]) % lev_n == 0
    )
    step = local_packed if fits else local_plain
    return step(lat_n, lev_n, grid, legendre, *rest)


def solution(mesh):
    placed = P(None, "lat", None, None, None, "lev")
    return jax.shard_map(
        functools.partial(local, mesh.shape["lat"], mesh.shape["lev"]),
        mesh=mesh,
        in_specs=(placed, P("lat", None, None, None), P("lat"), P("lat"), P(), P(), P(), P()),
        out_specs=placed,
        check_vma=False,
    )
```

time: 172 us -> 150 us (0.87)
  waiting for transfers between devices: 54.2 us -> 75.7 us
  starting transfers between devices: 60.3 us -> 42 us
  Pallas kernels: 44.4 us -> 27.9 us
  local copies, waits for them, and re-layouts: 11.5 us -> 3.49 us
    ppermute x40 -> x28, waiting for transfers between devices: 54.2 us -> 75.7 us  [the longest x12 39.6 us: exchange(): lax.ppermute(part, axis, [(i, i ^ r * stride) for i in range(count)])]
    ppermute x40 -> x28, starting transfers between devices: 60.3 us -> 42 us  [the longest x12 26.6 us: between_levels(): out.append(lax.ppermute(part, 'lev', [(i, i ^ r) for i in range(count)]))]
    pallas_call x11 -> x15, Pallas kernels: 44.4 us -> 27.9 us  [call(): pl.pallas_call(body, name=name, out_shape=list(outs), in_specs=list(in_sp...]
    unnamed x42 -> x20, local copies, waits for them, and re-layouts: 11.3 us -> 3.49 us
  transfers between devices with their start and end apart: 40 -> 28, of which waited for: 11 -> 16; matrix products, arithmetic and copies ran while one was open for 0% -> 0% of each run, Pallas kernels for 23% -> 11%
where the time goes in v2:
time: 150 us; the launch traced here: 149 us
  waiting for transfers between devices  75.7 us (50%)
  starting transfers between devices  42 us (28%)
  Pallas kernels  27.9 us (19%)
  local copies, waits for them, and re-layouts  3.49 us (2%)
    ppermute x12, waiting for transfers between devices, exchange(): lax.ppermute(part, axis, [(i, i ^ r * stride) for i in range(count)])  39.6 us
    ppermute x12, waiting for transfers between devices, between_levels(): out.append(lax.ppermute(part, 'lev', [(i, i ^ r) for i in range(count)]))  32.9 us
    pallas_call x15, Pallas kernels, call(): pl.pallas_call(body, name=name, out_shape=list(outs), in_specs=list(in_sp...  27.9 us
    ppermute x12, starting transfers between devices, between_levels(): out.append(lax.ppermute(part, 'lev', [(i, i ^ r) for i in range(count)]))  26.6 us
    ppermute x12, starting transfers between devices, exchange(): lax.ppermute(part, axis, [(i, i ^ r * stride) for i in range(count)])  15.2 us
    unnamed x20, local copies, waits for them, and re-layouts  3.49 us
    ppermute x4, waiting for transfers between devices, swap_cores(): return lax.ppermute(array, 'lat', [(i, i ^ 1) for i in range(count)])  3.21 us
  transfers between devices with their start and end apart: 28, of which 16 were waited for; matrix products, arithmetic and copies ran while one was open for 0% of the time, Pallas kernels for 11%

profile of v2, /device:TPU:0, one launch (start us, length us, event | category | flops | bytes accessed | tf_op | source)
XLA Modules:
  0.0 149.4 jit_solution(18131437698939662914)
XLA Ops:
  2.0 1.7 %fold.2 = (bf16[2,2,2,256,128]{4,3,2,1,0:T(8,128)(2,1)S(1)}, bf16[2,2,2,256,128]{4,3,2,1,0:T(8,128)(2,1)S(1)}, bf16[2,2,2,256,128]{4,3,2,1,0:T(8,128)(2,1)S(1)}, bf16[2,2,2,256,128]{4,3,2,1,0:T(8,128)(2,1)S(1)}) custom-call(s32[16]{0:T(128)S(1)} %copy-done.4, f32[128]{0:T(128)S(1)} %copy-done.9, s32[128]{0:T(128)S(1)} %copy-done.6, ...), custom_call_target="tpu_custom_call" | custom-call | tf_op jit(solution)/shard_map/fold/pallas_call | solution.py:223
  3.7 3.0 %collective-permute-start.3 = (bf16[2,2,2,256,128]{4,3,2,1,0:T(8,128)(2,1)S(1)}, bf16[2,2,2,256,128]{4,3,2,1,0:T(8,128)(2,1)S(1)}, u32[]{:S(2)}, u32[]{:S(2)}) collective-permute-start(bf16[2,2,2,256,128]{4,3,2,1,0:T(8,128)(2,1)S(1)} %get-tuple-element.64), channel_id=1, source_target_pairs={{0,8},{4,12},{8,0},{12,4},{16,24},{20,28},{24,16},{28,20},{1,9},{5... | collective-permute-start | bytes 1572872 | tf_op jit(solution)/shard_map/ppermute | solution.py:242
  8.2 1.7 %fold.3 = (bf16[2,2,2,256,128]{4,3,2,1,0:T(8,128)(2,1)S(1)}, bf16[2,2,2,256,128]{4,3,2,1,0:T(8,128)(2,1)S(1)}, bf16[2,2,2,256,128]{4,3,2,1,0:T(8,128)(2,1)S(1)}, bf16[2,2,2,256,128]{4,3,2,1,0:T(8,128)(2,1)S(1)}) custom-call(s32[16]{0:T(128)S(1)} %copy-done.4, f32[128]{0:T(128)S(1)} %copy-done.9, s32[128]{0:T(128)S(1)} %copy-done.6, ...), custom_call_target="tpu_custom_call" | custom-call | tf_op jit(solution)/shard_map/fold/pallas_call | solution.py:223
  9.9 4.1 %tables.1 = (bf16[2048,640]{1,0:T(8,128)(2,1)S(1)}, bf16[2048,512]{1,0:T(8,128)(2,1)S(1)}) custom-call(s32[16]{0:T(128)S(1)} %copy-done.4, bf16[2,2,1024,512]{3,2,1,0:T(8,128)(2,1)} %leg.1, bf16[2,2,2,256,128]{4,3,2,1,0:T(8,128)(2,1)S(1)} %get-tuple-element.58.refs_0_), custom_call_target="tpu_custom_call" | custom-call | tf_op jit(solution)/shard_map/tables/pallas_call | solution.py:223
  15.4 4.0 %collective-permute-done.3.refs_1_ = bf16[2,2,2,256,128]{4,3,2,1,0:T(8,128)(2,1)S(1)} collective-permute-done((bf16[2,2,2,256,128]{4,3,2,1,0:T(8,128)(2,1)S(1)}, bf16[2,2,2,256,128]{4,3,2,1,0:T(8,128)(2,1)S(1)}, u32[]{:S(2)}, u32[]{:S(2)}) %collective-permute-start.3) | collective-permute-done | bytes 524320 | tf_op jit(solution)/shard_map/ppermute | solution.py:242
  19.4 11.9 %collective-permute-done.4.refs_2_ = bf16[2,2,2,256,128]{4,3,2,1,0:T(8,128)(2,1)S(1)} collective-permute-done((bf16[2,2,2,256,128]{4,3,2,1,0:T(8,128)(2,1)S(1)}, bf16[2,2,2,256,128]{4,3,2,1,0:T(8,128)(2,1)S(1)}, u32[]{:S(2)}, u32[]{:S(2)}) %collective-permute-start.4) | collective-permute-done | bytes 524320 | tf_op jit(solution)/shard_map/ppermute | solution.py:242
  35.0 3.3 %forward.2 = (bf16[64,1152]{1,0:T(8,128)(2,1)S(1)}, bf16[64,1152]{1,0:T(8,128)(2,1)S(1)}, bf16[64,1152]{1,0:T(8,128)(2,1)S(1)}, bf16[64,1152]{1,0:T(8,128)(2,1)S(1)}) custom-call(bf16[2048,640]{1,0:T(8,128)(2,1)} %copy-done.1, bf16[2048,512]{1,0:T(8,128)(2,1)S(1)} %get-tuple-element.60.refs_4_.table1, ...), custom_call_target="tpu_custom_call" | custom-call | tf_op jit(solution)/shard_map/forward/pallas_call | solution.py:223
  38.3 1.6 %collective-permute-start.7 = (bf16[64,1152]{1,0:T(8,128)(2,1)S(1)}, bf16[64,1152]{1,0:T(8,128)(2,1)S(1)}, u32[]{:S(2)}, u32[]{:S(2)}) collective-permute-start(bf16[64,1152]{1,0:T(8,128)(2,1)S(1)} %get-tuple-element.69), channel_id=1, source_target_pairs={{0,1},{1,0},{2,3},{3,2},{4,5},{5,4},{6,7},{7,6},{8,9},{9,8},{10,11... | collective-permute-start | bytes 442376 | tf_op jit(solution)/shard_map/ppermute | solution.py:254
  40.0 2.6 %collective-permute-start.8 = (bf16[64,1152]{1,0:T(8,128)(2,1)S(1)}, bf16[64,1152]{1,0:T(8,128)(2,1)S(1)}, u32[]{:S(2)}, u32[]{:S(2)}) collective-permute-start(bf16[64,1152]{1,0:T(8,128)(2,1)S(1)} %get-tuple-element.71), channel_id=1, source_target_pairs={{0,2},{1,3},{2,0},{3,1},{4,6},{5,7},{6,4},{7,5},{8,10},{9,11},{10,... | collective-permute-start | bytes 442376 | tf_op jit(solution)/shard_map/ppermute | solution.py:254
  42.5 3.6 %collective-permute-done.7.refs_1_ = bf16[64,1152]{1,0:T(8,128)(2,1)S(1)} collective-permute-done((bf16[64,1152]{1,0:T(8,128)(2,1)S(1)}, bf16[64,1152]{1,0:T(8,128)(2,1)S(1)}, u32[]{:S(2)}, u32[]{:S(2)}) %collective-permute-start.7) | collective-permute-done | bytes 147488 | tf_op jit(solution)/shard_map/ppermute | solution.py:254
  46.2 3.0 %collective-permute-start.9 = (bf16[64,1152]{1,0:T(8,128)(2,1)S(1)}, bf16[64,1152]{1,0:T(8,128)(2,1)S(1)}, u32[]{:S(2)}, u32[]{:S(2)}) collective-permute-start(bf16[64,1152]{1,0:T(8,128)(2,1)S(1)} %get-tuple-element.72), channel_id=1, source_target_pairs={{0,3},{1,2},{2,1},{3,0},{4,7},{5,6},{6,5},{7,4},{8,11},{9,10},{10,... | collective-permute-start | bytes 442376 | tf_op jit(solution)/shard_map/ppermute | solution.py:254
  49.2 2.1 %collective-permute-done.8.refs_2_ = bf16[64,1152]{1,0:T(8,128)(2,1)S(1)} collective-permute-done((bf16[64,1152]{1,0:T(8,128)(2,1)S(1)}, bf16[64,1152]{1,0:T(8,128)(2,1)S(1)}, u32[]{:S(2)}, u32[]{:S(2)}) %collective-permute-start.8) | collective-permute-done | bytes 147488 | tf_op jit(solution)/shard_map/ppermute | solution.py:254
  51.2 2.0 %collective-permute-done.9.refs_3_ = bf16[64,1152]{1,0:T(8,128)(2,1)S(1)} collective-permute-done((bf16[64,1152]{1,0:T(8,128)(2,1)S(1)}, bf16[64,1152]{1,0:T(8,128)(2,1)S(1)}, u32[]{:S(2)}, u32[]{:S(2)}) %collective-permute-start.9) | collective-permute-done | bytes 147488 | tf_op jit(solution)/shard_map/ppermute | solution.py:254
  54.5 1.9 %collective-permute-done.1.refs_2_ = bf16[2,2,2,256,128]{4,3,2,1,0:T(8,128)(2,1)S(1)} collective-permute-done((bf16[2,2,2,256,128]{4,3,2,1,0:T(8,128)(2,1)S(1)}, bf16[2,2,2,256,128]{4,3,2,1,0:T(8,128)(2,1)S(1)}, u32[]{:S(2)}, u32[]{:S(2)}) %collective-permute-start.1) | collective-permute-done | bytes 524320 | tf_op jit(solution)/shard_map/ppermute | solution.py:242
  59.8 2.6 %collective-permute-start.15 = (bf16[64,1152]{1,0:T(8,128)(2,1)S(1)}, bf16[64,1152]{1,0:T(8,128)(2,1)S(1)}, u32[]{:S(2)}, u32[]{:S(2)}) collective-permute-start(bf16[64,1152]{1,0:T(8,128)(2,1)S(1)} %get-tuple-element.83), channel_id=1, source_target_pairs={{0,2},{1,3},{2,0},{3,1},{4,6},{5,7},{6,4},{7,5},{8,10},{9,11},{10,... | collective-permute-start | bytes 442376 | tf_op jit(solution)/shard_map/ppermute | solution.py:254
  62.4 5.1 %collective-permute-done.14.refs_1_ = bf16[64,1152]{1,0:T(8,128)(2,1)S(1)} collective-permute-done((bf16[64,1152]{1,0:T(8,128)(2,1)S(1)}, bf16[64,1152]{1,0:T(8,128)(2,1)S(1)}, u32[]{:S(2)}, u32[]{:S(2)}) %collective-permute-start.14) | collective-permute-done | bytes 147488 | tf_op jit(solution)/shard_map/ppermute | solution.py:254
  67.5 2.5 %collective-permute-start.16 = (bf16[64,1152]{1,0:T(8,128)(2,1)S(1)}, bf16[64,1152]{1,0:T(8,128)(2,1)S(1)}, u32[]{:S(2)}, u32[]{:S(2)}) collective-permute-start(bf16[64,1152]{1,0:T(8,128)(2,1)S(1)} %get-tuple-element.84), channel_id=1, source_target_pairs={{0,3},{1,2},{2,1},{3,0},{4,7},{5,6},{6,5},{7,4},{8,11},{9,10},{10,... | collective-permute-start | bytes 442376 | tf_op jit(solution)/shard_map/ppermute | solution.py:254
  70.0 3.3 %forward.3 = (bf16[64,1152]{1,0:T(8,128)(2,1)S(1)}, bf16[64,1152]{1,0:T(8,128)(2,1)S(1)}, bf16[64,1152]{1,0:T(8,128)(2,1)S(1)}, bf16[64,1152]{1,0:T(8,128)(2,1)S(1)}) custom-call(bf16[2048,640]{1,0:T(8,128)(2,1)} %copy-done.1, bf16[2048,512]{1,0:T(8,128)(2,1)S(1)} %get-tuple-element.60.refs_4_.table1, ...), custom_call_target="tpu_custom_call" | custom-call | tf_op jit(solution)/shard_map/forward/pallas_call | solution.py:223
  74.7 3.3 %inverse.2 = (bf16[2,2,2,256,128]{4,3,2,1,0:T(8,128)(2,1)S(1)}, bf16[2,2,2,256,128]{4,3,2,1,0:T(8,128)(2,1)S(1)}, bf16[2,2,2,256,128]{4,3,2,1,0:T(8,128)(2,1)S(1...) custom-call(bf16[2048,640]{1,0:T(8,128)(2,1)} %copy-done.1, ...), custom_call_target="tpu_custom_call" | custom-call | tf_op jit(solution)/shard_map/inverse/pallas_call | solution.py:223
  78.1 2.1 %collective-permute-start.11 = (bf16[64,1152]{1,0:T(8,128)(2,1)S(1)}, bf16[64,1152]{1,0:T(8,128)(2,1)S(1)}, u32[]{:S(2)}, u32[]{:S(2)}) collective-permute-start(bf16[64,1152]{1,0:T(8,128)(2,1)S(1)} %get-tuple-element.76), channel_id=1, source_target_pairs={{0,1},{1,0},{2,3},{3,2},{4,5},{5,4},{6,7},{7,6},{8,9},{9,8},{10,11... | collective-permute-start | bytes 442376 | tf_op jit(solution)/shard_map/ppermute | solution.py:254
  84.4 3.0 %collective-permute-start.12 = (bf16[64,1152]{1,0:T(8,128)(2,1)S(1)}, bf16[64,1152]{1,0:T(8,128)(2,1)S(1)}, u32[]{:S(2)}, u32[]{:S(2)}) collective-permute-start(bf16[64,1152]{1,0:T(8,128)(2,1)S(1)} %get-tuple-element.78), channel_id=1, source_target_pairs={{0,2},{1,3},{2,0},{3,1},{4,6},{5,7},{6,4},{7,5},{8,10},{9,11},{10,... | collective-permute-start | bytes 442376 | tf_op jit(solution)/shard_map/ppermute | solution.py:254
  88.7 9.5 %collective-permute-done.12.refs_2_ = bf16[64,1152]{1,0:T(8,128)(2,1)S(1)} collective-permute-done((bf16[64,1152]{1,0:T(8,128)(2,1)S(1)}, bf16[64,1152]{1,0:T(8,128)(2,1)S(1)}, u32[]{:S(2)}, u32[]{:S(2)}) %collective-permute-start.12) | collective-permute-done | bytes 147488 | tf_op jit(solution)/shard_map/ppermute | solution.py:254
  99.5 2.6 %collective-permute-start.18 = (bf16[64,1152]{1,0:T(8,128)(2,1)S(1)}, bf16[64,1152]{1,0:T(8,128)(2,1)S(1)}, u32[]{:S(2)}, u32[]{:S(2)}) collective-permute-start(bf16[64,1152]{1,0:T(8,128)(2,1)S(1)} %get-tuple-element.93), channel_id=1, source_target_pairs={{0,1},{1,0},{2,3},{3,2},{4,5},{5,4},{6,7},{7,6},{8,9},{9,8},{10,11... | collective-permute-start | bytes 442376 | tf_op jit(solution)/shard_map/ppermute | solution.py:254
  102.9 3.3 %collective-permute-done.18.refs_1_ = bf16[64,1152]{1,0:T(8,128)(2,1)S(1)} collective-permute-done((bf16[64,1152]{1,0:T(8,128)(2,1)S(1)}, bf16[64,1152]{1,0:T(8,128)(2,1)S(1)}, u32[]{:S(2)}, u32[]{:S(2)}) %collective-permute-start.18) | collective-permute-done | bytes 147488 | tf_op jit(solution)/shard_map/ppermute | solution.py:254
  106.2 2.8 %collective-permute-start.20 = (bf16[64,1152]{1,0:T(8,128)(2,1)S(1)}, bf16[64,1152]{1,0:T(8,128)(2,1)S(1)}, u32[]{:S(2)}, u32[]{:S(2)}) collective-permute-start(bf16[64,1152]{1,0:T(8,128)(2,1)S(1)} %get-tuple-element.96), channel_id=1, source_target_pairs={{0,3},{1,2},{2,1},{3,0},{4,7},{5,6},{6,5},{7,4},{8,11},{9,10},{10,... | collective-permute-start | bytes 442376 | tf_op jit(solution)/shard_map/ppermute | solution.py:254
  109.0 5.9 %collective-permute-done.19.refs_2_ = bf16[64,1152]{1,0:T(8,128)(2,1)S(1)} collective-permute-done((bf16[64,1152]{1,0:T(8,128)(2,1)S(1)}, bf16[64,1152]{1,0:T(8,128)(2,1)S(1)}, u32[]{:S(2)}, u32[]{:S(2)}) %collective-permute-start.19) | collective-permute-done | bytes 147488 | tf_op jit(solution)/shard_map/ppermute | solution.py:254
  114.9 3.9 %inverse.3 = (bf16[2,2,2,256,128]{4,3,2,1,0:T(8,128)(2,1)S(1)}, bf16[2,2,2,256,128]{4,3,2,1,0:T(8,128)(2,1)S(1)}, bf16[2,2,2,256,128]{4,3,2,1,0:T(8,128)(2,1)S(1...) custom-call(bf16[2048,640]{1,0:T(8,128)(2,1)} %copy-done.1, bf16[2048,512]{1,0:T(8,128)(2,1)} %copy-done, ...), custom_call_target="tpu_custom_call" | custom-call | tf_op jit(solution)/shard_map/inverse/pallas_call | solution.py:223
  118.9 2.6 %collective-permute-done.24.swapped = bf16[4,2,2,256,128]{4,3,2,1,0:T(8,128)(2,1)S(1)} collective-permute-done((bf16[4,2,2,256,128]{4,3,2,1,0:T(8,128)(2,1)S(1)}, bf16[4,2,2,256,128]{4,3,2,1,0:T(8,128)(2,1)S(1)}, u32[]{:S(2)}, u32[]{:S(2)}) %collective-permute-start.24) | collective-permute-done | bytes 1048608 | tf_op jit(solution)/shard_map/ppermute | solution.py:259
  125.2 2.0 %unfold.2.refs_4_ = bf16[16,2,512,128]{3,2,1,0:T(8,128)(2,1)} custom-call(s32[16]{0:T(128)S(1)} %copy-done.5, s32[1,128]{1,0:T(1,128)S(1)} %bitcast.7, bf16[2,2,2,256,128]{4,3,2,1,0:T(8,128)(2,1)S(1)} %get-tuple-element.90.refs_4_.refs_0_, bf16[2,2,2,256,128]{4,3,2,1,0:T(8,128)(2,1)S(1)} %collective-permute-done.21.refs_5_.refs_1_, ...), custom_call_target="tpu_custom_call" | custom-call | tf_op jit(solution)/shard_map/unfold/pallas_call | solution.py:223
  127.2 9.3 %collective-permute-done.25.refs_1_ = bf16[2,2,2,256,128]{4,3,2,1,0:T(8,128)(2,1)S(1)} collective-permute-done((bf16[2,2,2,256,128]{4,3,2,1,0:T(8,128)(2,1)S(1)}, bf16[2,2,2,256,128]{4,3,2,1,0:T(8,128)(2,1)S(1)}, u32[]{:S(2)}, u32[]{:S(2)}) %collective-permute-start.25) | collective-permute-done | bytes 524320 | tf_op jit(solution)/shard_map/ppermute | solution.py:242
  136.5 11.0 %collective-permute-done.26.refs_2_ = bf16[2,2,2,256,128]{4,3,2,1,0:T(8,128)(2,1)S(1)} collective-permute-done((bf16[2,2,2,256,128]{4,3,2,1,0:T(8,128)(2,1)S(1)}, bf16[2,2,2,256,128]{4,3,2,1,0:T(8,128)(2,1)S(1)}, u32[]{:S(2)}, u32[]{:S(2)}) %collective-permute-start.26) | collective-permute-done | bytes 524320 | tf_op jit(solution)/shard_map/ppermute | solution.py:242
  147.4 2.0 %unfold.3 = bf16[16,2,512,128]{3,2,1,0:T(8,128)(2,1)} custom-call(s32[16]{0:T(128)S(1)} %copy-done.5, s32[1,128]{1,0:T(1,128)S(1)} %bitcast.8, bf16[2,2,2,256,128]{4,3,2,1,0:T(8,128)(2,1)S(1)} %get-tuple-element.105.refs_0_, bf16[2,2,2,256,128]{4,3,2,1,0:T(8,128)(2,1)S(1)} %collective-permute-done.25.refs_1_, ...), custom_call_target="tpu_custom_call", output_to_operand_aliasing={{}: (6, {})} | custom-call | tf_op jit(solution)/shard_map/unfold/pallas_call | solution.py:223
  (59 shorter events, 26.2 us)
Async XLA Ops:
  3.7 15.8 %collective-permute-start.3 = (bf16[2,2,2,256,128]{4,3,2,1,0:T(8,128)(2,1)S(1)}, bf16[2,2,2,256,128]{4,3,2,1,0:T(8,128)(2,1)S(1)}, u32[]{:S(2)}, u32[]{:S(2)}) collective-permute-start(bf16[2,2,2,256,128]{4,3,2,1,0:T(8,128)(2,1)S(1)} %get-tuple-element.64), channel_id=1, source_target_pairs={{0,8},{4,12},{8,0},{12,4},{16,24},{20,28},{24,16},{28,20},{1,9},{5... | collective-permute-start | bytes 1572872 | tf_op jit(solution)/shard_map/ppermute | solution.py:242
  6.7 24.6 %collective-permute-start.4 = (bf16[2,2,2,256,128]{4,3,2,1,0:T(8,128)(2,1)S(1)}, bf16[2,2,2,256,128]{4,3,2,1,0:T(8,128)(2,1)S(1)}, u32[]{:S(2)}, u32[]{:S(2)}) collective-permute-start(bf16[2,2,2,256,128]{4,3,2,1,0:T(8,128)(2,1)S(1)} %get-tuple-element.65), channel_id=1, source_target_pairs={{0,16},{4,20},{8,24},{12,28},{16,0},{20,4},{24,8},{28,12},{1,17},{... | collective-permute-start | bytes 1572872 | tf_op jit(solution)/shard_map/ppermute | solution.py:242
  8.2 23.1 %collective-permute-start.5 = (bf16[2,2,2,256,128]{4,3,2,1,0:T(8,128)(2,1)S(1)}, bf16[2,2,2,256,128]{4,3,2,1,0:T(8,128)(2,1)S(1)}, u32[]{:S(2)}, u32[]{:S(2)}) collective-permute-start(bf16[2,2,2,256,128]{4,3,2,1,0:T(8,128)(2,1)S(1)} %get-tuple-element.66), channel_id=1, source_target_pairs={{0,24},{4,28},{8,16},{12,20},{16,8},{20,12},{24,0},{28,4},{1,25},{... | collective-permute-start | bytes 1572872 | tf_op jit(solution)/shard_map/ppermute | solution.py:242
  15.4 59.3 %copy-start = (bf16[2048,512]{1,0:T(8,128)(2,1)}, bf16[2048,512]{1,0:T(8,128)(2,1)S(1)}, u32[]{:S(2)}) copy-start(bf16[2048,512]{1,0:T(8,128)(2,1)S(1)} %get-tuple-element.60.refs_4_.table1) | copy-start | bytes 6291460
  31.4 21.9 %copy-start.2 = (bf16[128,128]{1,0:T(8,128)(2,1)S(1)}, bf16[128,128]{1,0:T(8,128)(2,1)}, u32[]{:S(2)}) copy-start(bf16[128,128]{1,0:T(8,128)(2,1)} %project.3) | copy-start | bytes 98308
  31.4 21.9 %copy-start.3 = (bf16[128,128]{1,0:T(8,128)(2,1)S(1)}, bf16[128,128]{1,0:T(8,128)(2,1)}, u32[]{:S(2)}) copy-start(bf16[128,128]{1,0:T(8,128)(2,1)} %vertical.3) | copy-start | bytes 98308
  31.4 21.9 %copy-start.5 = (s32[16]{0:T(128)S(1)}, s32[16]{0:T(128)}, u32[]{:S(2)}) copy-start(s32[16]{0:T(128)} %wave.9) | copy-start | bytes 196
  31.4 3.6 %collective-permute-start.6 = (bf16[4,2,2,256,128]{4,3,2,1,0:T(8,128)(2,1)S(1)}, bf16[4,2,2,256,128]{4,3,2,1,0:T(8,128)(2,1)S(1)}, u32[]{:S(2)}, u32[]{:S(2)}) collective-permute-start(bf16[4,2,2,256,128]{4,3,2,1,0:T(8,128)(2,1)S(1)} %gather.2), channel_id=1, source_target_pairs={{0,4},{4,0},{8,12},{12,8},{16,20},{20,16},{24,28},{28,24},{1,5},{5... | collective-permute-start | bytes 3145736 | tf_op jit(solution)/shard_map/ppermute | solution.py:259
  31.5 23.0 %collective-permute-start = (bf16[2,2,2,256,128]{4,3,2,1,0:T(8,128)(2,1)S(1)}, bf16[2,2,2,256,128]{4,3,2,1,0:T(8,128)(2,1)S(1)}, u32[]{:S(2)}, u32[]{:S(2)}) collective-permute-start(bf16[2,2,2,256,128]{4,3,2,1,0:T(8,128)(2,1)S(1)} %get-tuple-element.61), channel_id=1, source_target_pairs={{0,8},{4,12},{8,0},{12,4},{16,24},{20,28},{24,16},{28,20},{1,9},{5... | collective-permute-start | bytes 1572872 | tf_op jit(solution)/shard_map/ppermute | solution.py:242
  32.8 23.6 %collective-permute-start.1 = (bf16[2,2,2,256,128]{4,3,2,1,0:T(8,128)(2,1)S(1)}, bf16[2,2,2,256,128]{4,3,2,1,0:T(8,128)(2,1)S(1)}, u32[]{:S(2)}, u32[]{:S(2)}) collective-permute-start(bf16[2,2,2,256,128]{4,3,2,1,0:T(8,128)(2,1)S(1)} %get-tuple-element.62), channel_id=1, source_target_pairs={{0,16},{4,20},{8,24},{12,28},{16,0},{20,4},{24,8},{28,12},{1,17},{... | collective-permute-start | bytes 1572872 | tf_op jit(solution)/shard_map/ppermute | solution.py:242
  33.6 24.4 %collective-permute-start.2 = (bf16[2,2,2,256,128]{4,3,2,1,0:T(8,128)(2,1)S(1)}, bf16[2,2,2,256,128]{4,3,2,1,0:T(8,128)(2,1)S(1)}, u32[]{:S(2)}, u32[]{:S(2)}) collective-permute-start(bf16[2,2,2,256,128]{4,3,2,1,0:T(8,128)(2,1)S(1)} %get-tuple-element.63), channel_id=1, source_target_pairs={{0,24},{4,28},{8,16},{12,20},{16,8},{20,12},{24,0},{28,4},{1,25},{... | collective-permute-start | bytes 1572872 | tf_op jit(solution)/shard_map/ppermute | solution.py:242
  38.3 7.9 %collective-permute-start.7 = (bf16[64,1152]{1,0:T(8,128)(2,1)S(1)}, bf16[64,1152]{1,0:T(8,128)(2,1)S(1)}, u32[]{:S(2)}, u32[]{:S(2)}) collective-permute-start(bf16[64,1152]{1,0:T(8,128)(2,1)S(1)} %get-tuple-element.69), channel_id=1, source_target_pairs={{0,1},{1,0},{2,3},{3,2},{4,5},{5,4},{6,7},{7,6},{8,9},{9,8},{10,11... | collective-permute-start | bytes 442376 | tf_op jit(solution)/shard_map/ppermute | solution.py:254
  40.0 11.3 %collective-permute-start.8 = (bf16[64,1152]{1,0:T(8,128)(2,1)S(1)}, bf16[64,1152]{1,0:T(8,128)(2,1)S(1)}, u32[]{:S(2)}, u32[]{:S(2)}) collective-permute-start(bf16[64,1152]{1,0:T(8,128)(2,1)S(1)} %get-tuple-element.71), channel_id=1, source_target_pairs={{0,2},{1,3},{2,0},{3,1},{4,6},{5,7},{6,4},{7,5},{8,10},{9,11},{10,... | collective-permute-start | bytes 442376 | tf_op jit(solution)/shard_map/ppermute | solution.py:254
  46.2 7.0 %collective-permute-start.9 = (bf16[64,1152]{1,0:T(8,128)(2,1)S(1)}, bf16[64,1152]{1,0:T(8,128)(2,1)S(1)}, u32[]{:S(2)}, u32[]{:S(2)}) collective-permute-start(bf16[64,1152]{1,0:T(8,128)(2,1)S(1)} %get-tuple-element.72), channel_id=1, source_target_pairs={{0,3},{1,2},{2,1},{3,0},{4,7},{5,6},{6,5},{7,4},{8,11},{9,10},{10,... | collective-permute-start | bytes 442376 | tf_op jit(solution)/shard_map/ppermute | solution.py:254
  58.1 11.9 %collective-permute-start.10 = (bf16[4,2,2,256,128]{4,3,2,1,0:T(8,128)(2,1)S(1)}, bf16[4,2,2,256,128]{4,3,2,1,0:T(8,128)(2,1)S(1)}, u32[]{:S(2)}, u32[]{:S(2)}) collective-permute-start(bf16[4,2,2,256,128]{4,3,2,1,0:T(8,128)(2,1)S(1)} %gather.3), channel_id=1, source_target_pairs={{0,4},{4,0},{8,12},{12,8},{16,20},{20,16},{24,28},{28,24},{1,5},{5... | collective-permute-start | bytes 3145736 | tf_op jit(solution)/shard_map/ppermute | solution.py:259
  58.2 9.3 %collective-permute-start.14 = (bf16[64,1152]{1,0:T(8,128)(2,1)S(1)}, bf16[64,1152]{1,0:T(8,128)(2,1)S(1)}, u32[]{:S(2)}, u32[]{:S(2)}) collective-permute-start(bf16[64,1152]{1,0:T(8,128)(2,1)S(1)} %get-tuple-element.81), channel_id=1, source_target_pairs={{0,1},{1,0},{2,3},{3,2},{4,5},{5,4},{6,7},{7,6},{8,9},{9,8},{10,11... | collective-permute-start | bytes 442376 | tf_op jit(solution)/shard_map/ppermute | solution.py:254
  59.8 13.4 %collective-permute-start.15 = (bf16[64,1152]{1,0:T(8,128)(2,1)S(1)}, bf16[64,1152]{1,0:T(8,128)(2,1)S(1)}, u32[]{:S(2)}, u32[]{:S(2)}) collective-permute-start(bf16[64,1152]{1,0:T(8,128)(2,1)S(1)} %get-tuple-element.83), channel_id=1, source_target_pairs={{0,2},{1,3},{2,0},{3,1},{4,6},{5,7},{6,4},{7,5},{8,10},{9,11},{10,... | collective-permute-start | bytes 442376 | tf_op jit(solution)/shard_map/ppermute | solution.py:254
  67.5 7.2 %collective-permute-start.16 = (bf16[64,1152]{1,0:T(8,128)(2,1)S(1)}, bf16[64,1152]{1,0:T(8,128)(2,1)S(1)}, u32[]{:S(2)}, u32[]{:S(2)}) collective-permute-start(bf16[64,1152]{1,0:T(8,128)(2,1)S(1)} %get-tuple-element.84), channel_id=1, source_target_pairs={{0,3},{1,2},{2,1},{3,0},{4,7},{5,6},{6,5},{7,4},{8,11},{9,10},{10,... | collective-permute-start | bytes 442376 | tf_op jit(solution)/shard_map/ppermute | solution.py:254
  78.0 2.7 %collective-permute-start.17 = (bf16[4,2,2,256,128]{4,3,2,1,0:T(8,128)(2,1)S(1)}, bf16[4,2,2,256,128]{4,3,2,1,0:T(8,128)(2,1)S(1)}, u32[]{:S(2)}, u32[]{:S(2)}) collective-permute-start(bf16[4,2,2,256,128]{4,3,2,1,0:T(8,128)(2,1)S(1)} %get-tuple-element.85), channel_id=1, source_target_pairs={{0,4},{4,0},{8,12},{12,8},{16,20},{20,16},{24,28},{28,24},{1,5},{5... | collective-permute-start | bytes 3145736 | tf_op jit(solution)/shard_map/ppermute | solution.py:259
  78.1 9.3 %collective-permute-start.11 = (bf16[64,1152]{1,0:T(8,128)(2,1)S(1)}, bf16[64,1152]{1,0:T(8,128)(2,1)S(1)}, u32[]{:S(2)}, u32[]{:S(2)}) collective-permute-start(bf16[64,1152]{1,0:T(8,128)(2,1)S(1)} %get-tuple-element.76), channel_id=1, source_target_pairs={{0,1},{1,0},{2,3},{3,2},{4,5},{5,4},{6,7},{7,6},{8,9},{9,8},{10,11... | collective-permute-start | bytes 442376 | tf_op jit(solution)/shard_map/ppermute | solution.py:254
  80.8 34.1 %collective-permute-start.21 = (bf16[2,2,2,256,128]{4,3,2,1,0:T(8,128)(2,1)S(1)}, bf16[2,2,2,256,128]{4,3,2,1,0:T(8,128)(2,1)S(1)}, u32[]{:S(2)}, u32[]{:S(2)}) collective-permute-start(bf16[2,2,2,256,128]{4,3,2,1,0:T(8,128)(2,1)S(1)} %get-tuple-element.97), channel_id=1, source_target_pairs={{0,8},{4,12},{8,0},{12,4},{16,24},{20,28},{24,16},{28,20},{1,9},{5... | collective-permute-start | bytes 1572872 | tf_op jit(solution)/shard_map/ppermute | solution.py:242
  81.7 33.2 %collective-permute-start.22 = (bf16[2,2,2,256,128]{4,3,2,1,0:T(8,128)(2,1)S(1)}, bf16[2,2,2,256,128]{4,3,2,1,0:T(8,128)(2,1)S(1)}, u32[]{:S(2)}, u32[]{:S(2)}) collective-permute-start(bf16[2,2,2,256,128]{4,3,2,1,0:T(8,128)(2,1)S(1)} %get-tuple-element.98), channel_id=1, source_target_pairs={{0,16},{4,20},{8,24},{12,28},{16,0},{20,4},{24,8},{28,12},{1,17},{... | collective-permute-start | bytes 1572872 | tf_op jit(solution)/shard_map/ppermute | solution.py:242
  83.2 31.7 %collective-permute-start.23 = (bf16[2,2,2,256,128]{4,3,2,1,0:T(8,128)(2,1)S(1)}, bf16[2,2,2,256,128]{4,3,2,1,0:T(8,128)(2,1)S(1)}, u32[]{:S(2)}, u32[]{:S(2)}) collective-permute-start(bf16[2,2,2,256,128]{4,3,2,1,0:T(8,128)(2,1)S(1)} %get-tuple-element.99), channel_id=1, source_target_pairs={{0,24},{4,28},{8,16},{12,20},{16,8},{20,12},{24,0},{28,4},{1,25},{... | collective-permute-start | bytes 1572872 | tf_op jit(solution)/shard_map/ppermute | solution.py:242
  84.4 13.9 %collective-permute-start.12 = (bf16[64,1152]{1,0:T(8,128)(2,1)S(1)}, bf16[64,1152]{1,0:T(8,128)(2,1)S(1)}, u32[]{:S(2)}, u32[]{:S(2)}) collective-permute-start(bf16[64,1152]{1,0:T(8,128)(2,1)S(1)} %get-tuple-element.78), channel_id=1, source_target_pairs={{0,2},{1,3},{2,0},{3,1},{4,6},{5,7},{6,4},{7,5},{8,10},{9,11},{10,... | collective-permute-start | bytes 442376 | tf_op jit(solution)/shard_map/ppermute | solution.py:254
  87.4 10.8 %collective-permute-start.13 = (bf16[64,1152]{1,0:T(8,128)(2,1)S(1)}, bf16[64,1152]{1,0:T(8,128)(2,1)S(1)}, u32[]{:S(2)}, u32[]{:S(2)}) collective-permute-start(bf16[64,1152]{1,0:T(8,128)(2,1)S(1)} %get-tuple-element.79), channel_id=1, source_target_pairs={{0,3},{1,2},{2,1},{3,0},{4,7},{5,6},{6,5},{7,4},{8,11},{9,10},{10,... | collective-permute-start | bytes 442376 | tf_op jit(solution)/shard_map/ppermute | solution.py:254
  99.5 6.7 %collective-permute-start.18 = (bf16[64,1152]{1,0:T(8,128)(2,1)S(1)}, bf16[64,1152]{1,0:T(8,128)(2,1)S(1)}, u32[]{:S(2)}, u32[]{:S(2)}) collective-permute-start(bf16[64,1152]{1,0:T(8,128)(2,1)S(1)} %get-tuple-element.93), channel_id=1, source_target_pairs={{0,1},{1,0},{2,3},{3,2},{4,5},{5,4},{6,7},{7,6},{8,9},{9,8},{10,11... | collective-permute-start | bytes 442376 | tf_op jit(solution)/shard_map/ppermute | solution.py:254
  102.1 12.8 %collective-permute-start.19 = (bf16[64,1152]{1,0:T(8,128)(2,1)S(1)}, bf16[64,1152]{1,0:T(8,128)(2,1)S(1)}, u32[]{:S(2)}, u32[]{:S(2)}) collective-permute-start(bf16[64,1152]{1,0:T(8,128)(2,1)S(1)} %get-tuple-element.95), channel_id=1, source_target_pairs={{0,2},{1,3},{2,0},{3,1},{4,6},{5,7},{6,4},{7,5},{8,10},{9,11},{10,... | collective-permute-start | bytes 442376 | tf_op jit(solution)/shard_map/ppermute | solution.py:254
  106.2 8.7 %collective-permute-start.20 = (bf16[64,1152]{1,0:T(8,128)(2,1)S(1)}, bf16[64,1152]{1,0:T(8,128)(2,1)S(1)}, u32[]{:S(2)}, u32[]{:S(2)}) collective-permute-start(bf16[64,1152]{1,0:T(8,128)(2,1)S(1)} %get-tuple-element.96), channel_id=1, source_target_pairs={{0,3},{1,2},{2,1},{3,0},{4,7},{5,6},{6,5},{7,4},{8,11},{9,10},{10,... | collective-permute-start | bytes 442376 | tf_op jit(solution)/shard_map/ppermute | solution.py:254
  118.8 2.7 %collective-permute-start.24 = (bf16[4,2,2,256,128]{4,3,2,1,0:T(8,128)(2,1)S(1)}, bf16[4,2,2,256,128]{4,3,2,1,0:T(8,128)(2,1)S(1)}, u32[]{:S(2)}, u32[]{:S(2)}) collective-permute-start(bf16[4,2,2,256,128]{4,3,2,1,0:T(8,128)(2,1)S(1)} %get-tuple-element.100), channel_id=1, source_target_pairs={{0,4},{4,0},{8,12},{12,8},{16,20},{20,16},{24,28},{28,24},{1,5},{5... | collective-permute-start | bytes 3145736 | tf_op jit(solution)/shard_map/ppermute | solution.py:259
  121.6 14.8 %collective-permute-start.25 = (bf16[2,2,2,256,128]{4,3,2,1,0:T(8,128)(2,1)S(1)}, bf16[2,2,2,256,128]{4,3,2,1,0:T(8,128)(2,1)S(1)}, u32[]{:S(2)}, u32[]{:S(2)}) collective-permute-start(bf16[2,2,2,256,128]{4,3,2,1,0:T(8,128)(2,1)S(1)} %get-tuple-element.106), channel_id=1, source_target_pairs={{0,8},{4,12},{8,0},{12,4},{16,24},{20,28},{24,16},{28,20},{1,9},{5... | collective-permute-start | bytes 1572872 | tf_op jit(solution)/shard_map/ppermute | solution.py:242
  122.5 24.9 %collective-permute-start.26 = (bf16[2,2,2,256,128]{4,3,2,1,0:T(8,128)(2,1)S(1)}, bf16[2,2,2,256,128]{4,3,2,1,0:T(8,128)(2,1)S(1)}, u32[]{:S(2)}, u32[]{:S(2)}) collective-permute-start(bf16[2,2,2,256,128]{4,3,2,1,0:T(8,128)(2,1)S(1)} %get-tuple-element.107), channel_id=1, source_target_pairs={{0,16},{4,20},{8,24},{12,28},{16,0},{20,4},{24,8},{28,12},{1,17},{... | collective-permute-start | bytes 1572872 | tf_op jit(solution)/shard_map/ppermute | solution.py:242
  124.0 23.4 %collective-permute-start.27 = (bf16[2,2,2,256,128]{4,3,2,1,0:T(8,128)(2,1)S(1)}, bf16[2,2,2,256,128]{4,3,2,1,0:T(8,128)(2,1)S(1)}, u32[]{:S(2)}, u32[]{:S(2)}) collective-permute-start(bf16[2,2,2,256,128]{4,3,2,1,0:T(8,128)(2,1)S(1)} %get-tuple-element.108), channel_id=1, source_target_pairs={{0,24},{4,28},{8,16},{12,20},{16,8},{20,12},{24,0},{28,4},{1,25},{... | collective-permute-start | bytes 1572872 | tf_op jit(solution)/shard_map/ppermute | solution.py:242
  (6 other events, 35.6 us)

commit v3 on v2

--- a/solution.py
+++ b/solution.py
@@ -8,8 +8,8 @@
 from jax.sharding import PartitionSpec as P
 
 coupling = 2.0
+CFG = {'zc': (2, 2, 2, 2), 'g1': 0, 'i0': 0, 's1': 0, 'i1': 1, 'late': (1, 0), 'vm': 24, 'fvm': 48, 'u': 0}
 LANES = 128
-VMEM_BYTES = 48 * 1024 * 1024
 
 
 def packed_counts(wave_a, wave_b, parity, modes):
@@ -47,9 +47,11 @@
         ).astype(jnp.bfloat16)
 
 
-def fold_kernel(cut, row0, wave_in, quad_in, cycles_in, grid, *refs):
+def fold_kernel(cut, row0, late, wave_in, quad_in, cycles_in, grid, *refs):
     lat_n = cut["lat"]
     outs = refs[-6 - lat_n // 2 : -6]
+    if not late:
+        outs, others = refs[-7 - lat_n // 2 : -7], refs[-7]
     held, wave, quad, cycles, sems, small = refs[-6:]
     rows = held.shape[3]
     me = lax.axis_index("lat")
@@ -78,8 +80,11 @@
             weight = jnp.where(2 * wave[2 * owner + slot] < cycles[...], quad[...], 0.0)[None]
             north = held[step, slot, 0].astype(jnp.float32)
             south = held[step, slot, 1].astype(jnp.float32)
-            outs[step // 2][step % 2, slot, 0] = (weight * (north + south)).astype(jnp.bfloat16)
-            outs[step // 2][step % 2, slot, 1] = (weight * (north - south)).astype(jnp.bfloat16)
+            out = outs[step // 2].at[step % 2]
+            if step % 2 and not late:
+                out = others.at[step // 2]
+            out[slot, 0] = (weight * (north + south)).astype(jnp.bfloat16)
+            out[slot, 1] = (weight * (north - south)).astype(jnp.bfloat16)
 
 
 def in_order(values):
@@ -91,26 +96,27 @@
     return values
 
 
+def arrivals(refs, lat_n, late):
+    if late:
+        return [refs[lat_n // 2].at[r // 2] if r % 2 else refs[r // 2].at[0] for r in range(lat_n)]
+    return [refs[r // 2].at[r % 2] for r in range(lat_n)]
+
+
 def gather_kernel(cut, *refs):
     parts, out = refs[: cut["lat"] // 2], refs[-1]
     for step, part in enumerate(parts):
         out[step] = part[1]
 
 
-def forward_kernel(cut, table0, table1, *refs):
+def forward_kernel(cut, late, table0, table1, *refs):
     lat_n, lev_n = cut["lat"], cut["lev"]
-    near, swapped, outs = refs[: lat_n // 2], refs[lat_n // 2], refs[-lev_n:]
+    parts, outs = arrivals(refs, lat_n, late), refs[-lev_n:]
     share = outs[0].shape[0]
     at = 0
     for parity, table in enumerate((table0, table1)):
         kk = table.shape[1]
         values = jnp.concatenate(
-            [
-                swapped[step // 2, slot, parity] if step % 2 else near[step // 2][0, slot, parity]
-                for slot in range(2)
-                for step in range(lat_n)
-            ],
-            axis=1,
+            [parts[step][slot, parity] for slot in range(2) for step in range(lat_n)], axis=1
         )
         packed = jnp.dot(values, table[...], preferred_element_type=jnp.float32)
         packed = packed.astype(jnp.bfloat16)
@@ -159,9 +165,11 @@
             outs[step][at, :] = values[step]
 
 
-def inverse_kernel(cut, table0, table1, *refs):
+def inverse_kernel(cut, late, table0, table1, *refs):
     lat_n, lev_n, width = cut["lat"], cut["lev"], cut["cycles"]
     parts, near, swapped = refs[:lev_n], refs[-1 - lat_n // 2 : -1], refs[-1]
+    if late:
+        near = refs[-(lat_n // 2) :]
     at = 0
     for parity, table in enumerate((table0, table1)):
         kk = table.shape[1]
@@ -176,10 +184,10 @@
             for step in range(lat_n):
                 start = (slot * lat_n + step) * width
                 part = returned[:, start : start + width]
-                if step % 2:
+                if step % 2 and not late:
                     swapped[step // 2, slot, parity] = part
                 else:
-                    near[step // 2][0, slot, parity] = part
+                    near[step // 2][step % 2, slot, parity] = part
         at += kk
 
 
@@ -189,10 +197,9 @@
         out[1] = swapped[step]
 
 
-def unfold_kernel(cut, row0, wave, cycles, *refs):
+def unfold_kernel(cut, row0, late, wave, cycles, *refs):
     lat_n = cut["lat"]
-    parts = refs[: lat_n // 2]
-    out, held, sems = refs[-3:]
+    parts, (out, held, sems) = arrivals(refs, lat_n, late), refs[-3:]
     rows = held.shape[3]
     me = lax.axis_index("lat")
     copies = []
@@ -200,8 +207,8 @@
         owner = jnp.bitwise_xor(me, step)
         for slot in range(2):
             seen = 2 * wave[2 * owner + slot] < cycles[...]
-            even = parts[step // 2][step % 2, slot, 0].astype(jnp.float32)
-            odd = parts[step // 2][step % 2, slot, 1].astype(jnp.float32)
+            even = parts[step][slot, 0].astype(jnp.float32)
+            odd = parts[step][slot, 1].astype(jnp.float32)
             held[step, slot, 0] = jnp.where(seen, even + odd, 0.0).astype(jnp.bfloat16)
             held[step, slot, 1] = jnp.where(seen, even - odd, 0.0).astype(jnp.bfloat16)
         copy = pltpu.make_async_copy(
@@ -219,7 +226,7 @@
 in_hbm = pl.BlockSpec(memory_space=pltpu.HBM)
 
 
-def call(body, name, ins, in_specs, outs, out_specs, scratch, aliases=None, after=()):
+def call(body, name, ins, in_specs, outs, out_specs, scratch, aliases=None, after=(), vm=None):
     return pl.pallas_call(
         body,
         name=name,
@@ -229,7 +236,7 @@
         scratch_shapes=list(scratch),
         input_output_aliases=aliases or {},
         cost_estimate=pl.CostEstimate(flops=0, bytes_accessed=0, transcendentals=0),
-        compiler_params=pltpu.CompilerParams(vmem_limit_bytes=VMEM_BYTES),
+        compiler_params=pltpu.CompilerParams(vmem_limit_bytes=(vm or CFG["vm"]) * 2**20),
     )(*ins, *after)
 
 
@@ -245,13 +252,15 @@
     ]
 
 
-def between_levels(parts, count):
-    out = [parts[0]]
-    for r in range(1, count):
+def between_levels(parts, count, mode):
+    out = [parts[0]] + [None] * (count - 1)
+    waits = {0: {}, 1: {3: 1}, 2: {1: 3}, 3: {1: 2}, 4: {3: 2}, 5: {2: 1}}[mode]
+    order = sorted(range(1, count), key=lambda r: (r in waits, r))
+    for r in order:
         part = parts[r]
-        if r > 2:
-            part, out[r - 2] = lax.optimization_barrier((part, out[r - 2]))
-        out.append(lax.ppermute(part, "lev", [(i, i ^ r) for i in range(count)]))
+        if r in waits:
+            part, out[waits[r]] = lax.optimization_barrier((part, out[waits[r]]))
+        out[r] = lax.ppermute(part, "lev", [(i, i ^ r) for i in range(count)])
     return out
 
 
@@ -288,17 +297,48 @@
 
     blocks = blocks_of(cols, lev_n)
     near_n = lat_n // 2
+    lates = [bool(CFG["late"][block]) for block in range(len(blocks))]
     last = ()
     arrived = []
-    for first, count in blocks:
+
+    def swap(near, others):
+        return call(
+            functools.partial(merge_kernel, cut),
+            "merge",
+            (swap_cores(others, lat_n), *near),
+            [vmem] * (1 + near_n),
+            [struct(*part.shape) for part in near],
+            [vmem] * near_n,
+            [],
+            aliases={1 + r: r for r in range(near_n)},
+        )
+
+    def gather(near, last):
+        (others,) = call(
+            functools.partial(gather_kernel, cut),
+            "gather",
+            near,
+            [vmem] * near_n,
+            [struct(near_n, *near[0].shape[1:])],
+            [vmem],
+            [],
+            after=last,
+        )
+        return [*near, swap_cores(others, lat_n)]
+
+    def outgoing(rows, late):
+        shapes = [struct(2, 2, 2, rows, width)] * near_n
+        return shapes if late else shapes + [struct(near_n, 2, 2, rows, width)]
+
+    for (first, count), late in zip(blocks, lates):
         rows = count * levels
         folded = call(
-            functools.partial(fold_kernel, cut, first * levels),
+            functools.partial(fold_kernel, cut, first * levels, late),
             "fold",
             (wave_ids, quad, cycle_points, lines),
             [in_hbm] * 4,
-            [struct(2, 2, 2, rows, width)] * near_n,
-            [vmem] * near_n,
+            outgoing(rows, late),
+            [vmem] * len(outgoing(rows, late)),
             [
                 pltpu.VMEM((lat_n, 2, 2, rows, width), jnp.bfloat16),
                 pltpu.SMEM((slots,), jnp.int32),
@@ -308,8 +348,11 @@
                 pltpu.SemaphoreType.DMA((3,)),
             ],
             after=last,
+            vm=CFG["fvm"],
         )
         last = (folded[0],)
+        if not late:
+            folded = swap(folded[:near_n], folded[near_n])
         arrived.append(exchange(folded, "lat", lat_n, 2))
 
     table0, table1 = call(
@@ -327,30 +370,22 @@
     def forward(block, last):
         rows = blocks[block][1] * levels
         share = rows // lev_n
-        near = arrived[block]
-        (swapped,) = call(
-            functools.partial(gather_kernel, cut),
-            "gather",
-            near,
-            [vmem] * near_n,
-            [struct(near_n, 2, 2, rows, width)],
-            [vmem],
-            [],
-            after=last,
-        )
-        swapped = swap_cores(swapped, lat_n)
+        parts, late = arrived[block], lates[block]
+        if late:
+            parts, last = gather(parts, last), ()
         packed = call(
-            functools.partial(forward_kernel, cut),
+            functools.partial(forward_kernel, cut, late),
             "forward",
-            (table0, table1, *near, swapped),
-            [vmem] * (3 + near_n),
+            (table0, table1, *parts),
+            [vmem] * (2 + len(parts)),
             [struct(share, kk_all)] * lev_n,
             [vmem] * lev_n,
             [],
-        )
-        return between_levels(packed, lev_n), (packed[0],)
-
-    def solve(packed, last):
+            after=last,
+        )
+        return between_levels(packed, lev_n, CFG["zc"][2 * block]), (packed[0],)
+
+    def solve(block, packed, last):
         share = packed[0].shape[0]
         solved = call(
             functools.partial(solve_kernel, cut),
@@ -362,59 +397,67 @@
             [],
             after=last,
         )
-        return between_levels(solved, lev_n), (solved[0],)
-
-    def inverse(solved, last):
+        return between_levels(solved, lev_n, CFG["zc"][2 * block + 1]), (solved[0],)
+
+    def inverse(block, solved, last, hold=()):
         rows = solved[0].shape[0] * lev_n
-        *near, swapped = call(
-            functools.partial(inverse_kernel, cut),
+        late = lates[block]
+        returned = call(
+            functools.partial(inverse_kernel, cut, late),
             "inverse",
             (table0, table1, *solved),
             [vmem] * (2 + lev_n),
-            [struct(2, 2, 2, rows, width)] * near_n + [struct(near_n, 2, 2, rows, width)],
-            [vmem] * (near_n + 1),
+            outgoing(rows, late),
+            [vmem] * len(outgoing(rows, late)),
             [],
             after=last,
         )
-        swapped = swap_cores(swapped, lat_n)
-        merged = call(
-            functools.partial(merge_kernel, cut),
-            "merge",
-            (swapped, *near),
-            [vmem] * (1 + near_n),
-            [struct(2, 2, 2, rows, width)] * near_n,
-            [vmem] * near_n,
-            [],
-            aliases={1 + r: r for r in range(near_n)},
-        )
-        return exchange(merged, "lat", lat_n, 2), (merged[0],)
+        last = (returned[0],)
+        if not late:
+            returned = swap(returned[:near_n], returned[near_n])
+        if hold:
+            returned = lax.optimization_barrier((*returned, *hold))[: len(returned)]
+        return exchange(returned, "lat", lat_n, 2), last
 
     def unfold(block, returned, out):
+        if lates[block]:
+            returned = gather(returned, ())
         rows = blocks[block][1] * levels
         return call(
-            functools.partial(unfold_kernel, cut, blocks[block][0] * levels),
+            functools.partial(unfold_kernel, cut, blocks[block][0] * levels, lates[block]),
             "unfold",
             (wave_ids, cycle_row, *returned) + out,
-            [smem] + [vmem] * (1 + near_n) + [anywhere] * len(out),
+            [smem] + [vmem] * (1 + len(returned)) + [anywhere] * len(out),
             [struct(slots, halves, cols * levels, width)],
             [anywhere],
             [
                 pltpu.VMEM((lat_n, 2, 2, rows, width), jnp.bfloat16),
                 pltpu.SemaphoreType.DMA((lat_n,)),
             ],
-            aliases={2 + near_n: 0} if out else None,
+            aliases={2 + len(returned): 0} if out else None,
         )
 
     count = len(blocks)
     packed, solved, returned = [None] * count, [None] * count, [None] * count
     for turn in range(count + 2):
         if 0 <= turn - 2:
-            before = returned[turn - 3][1:] if turn - 3 >= 0 else []
-            returned[turn - 2], last = inverse(solved[turn - 2], (*last, *before))
+            extra = []
+            if turn == 2 and count > 1:
+                extra = [packed[1][r] for r in {0: [], 1: [1], 2: [2], 3: [1, 2, 3], 4: [3], 5: [1, 2]}[CFG["i0"]]]
+            if turn == 3:
+                extra = returned[0][1:] if CFG["i1"] == 1 else []
+            hold = returned[0][1:] if turn == 3 and CFG["i1"] == 2 else []
+            returned[turn - 2], last = inverse(turn - 2, solved[turn - 2], (*last, *extra), hold)
         if 0 <= turn - 1 < count:
-            solved[turn - 1], last = solve(packed[turn - 1], last)
+            extra = []
+            if turn == 2:
+                extra = {0: [], 1: returned[0][1:2], 2: returned[0][2:3], 3: returned[0][1:4]}[CFG["s1"]]
+            solved[turn - 1], last = solve(turn - 1, packed[turn - 1], (*last, *extra))
         if turn < count:
-            packed[turn], last = forward(turn, last)
+            extra = []
+            if turn == 1:
+                extra = [solved[0][r] for r in {0: [], 1: [1], 2: [2], 3: [1, 2], 4: [3]}[CFG["g1"]]]
+            packed[turn], last = forward(turn, (*last, *extra))
     out = ()
     for block in range(count):
         out = tuple(unfold(block, returned[block], out))

time: 150 us -> 135 us (0.900)
  Pallas kernels: 27.9 us -> 18.9 us
  waiting for transfers between devices: 75.7 us -> 70.8 us
  local copies, waits for them, and re-layouts: 3.49 us -> 1.99 us
    pallas_call x15, Pallas kernels: 27.9 us -> 18.9 us  [call(): pl.pallas_call(body, name=name, out_shape=list(outs), in_specs=list(in_sp...]
    ppermute x12, waiting for transfers between devices: 32.9 us -> 28 us  [between_levels(): out[r] = lax.ppermute(part, 'lev', [(i, i ^ r) for i in range(count)])]
    unnamed x20 -> x14, local copies, waits for them, and re-layouts: 3.49 us -> 1.99 us
  transfers between devices with their start and end apart: 28 -> 28, of which waited for: 16 -> 18; matrix products, arithmetic and copies ran while one was open for 0% -> 0% of each run, Pallas kernels for 11% -> 10%
where the time goes in v3:
time: 135 us
  waiting for transfers between devices  70.8 us (52%)
  starting transfers between devices  43.2 us (32%)
  Pallas kernels  18.9 us (14%)
  local copies, waits for them, and re-layouts  1.99 us (1%)
    ppermute x12, waiting for transfers between devices, exchange(): lax.ppermute(part, axis, [(i, i ^ r * stride) for i in range(count)])  39.6 us
    ppermute x12, waiting for transfers between devices, between_levels(): out[r] = lax.ppermute(part, 'lev', [(i, i ^ r) for i in range(count)])  28 us
    ppermute x12, starting transfers between devices, between_levels(): out[r] = lax.ppermute(part, 'lev', [(i, i ^ r) for i in range(count)])  26.8 us
    pallas_call x15, Pallas kernels, call(): pl.pallas_call(body, name=name, out_shape=list(outs), in_specs=list(in_sp...  18.9 us
    ppermute x12, starting transfers between devices, exchange(): lax.ppermute(part, axis, [(i, i ^ r * stride) for i in range(count)])  15.6 us
    ppermute x4, waiting for transfers between devices, swap_cores(): return lax.ppermute(array, 'lat', [(i, i ^ 1) for i in range(count)])  3.24 us
  transfers between devices with their start and end apart: 28, of which 18 were waited for; matrix products, arithmetic and copies ran while one was open for 0% of the time, Pallas kernels for 10%

profile of v3, /device:TPU:0, one launch (start us, length us, event | category | flops | bytes accessed | tf_op | source)
XLA Modules:
  0.0 135.0 jit_solution(4783512862108873958)
XLA Ops:
  2.0 1.8 %fold.2 = (bf16[2,2,2,256,128]{4,3,2,1,0:T(8,128)(2,1)S(1)}, bf16[2,2,2,256,128]{4,3,2,1,0:T(8,128)(2,1)S(1)}, bf16[2,2,2,256,128]{4,3,2,1,0:T(8,128)(2,1)S(1)}, bf16[2,2,2,256,128]{4,3,2,1,0:T(8,128)(2,1)S(1)}) custom-call(s32[16]{0:T(128)S(1)} %copy-done.3, f32[128]{0:T(128)S(1)} %copy-done.6, s32[128]{0:T(128)S(1)} %copy-done.4, ...), custom_call_target="tpu_custom_call" | custom-call | tf_op jit(solution)/shard_map/fold/pallas_call | solution.py:230
  3.8 3.0 %collective-permute-start.4 = (bf16[2,2,2,256,128]{4,3,2,1,0:T(8,128)(2,1)S(1)}, bf16[2,2,2,256,128]{4,3,2,1,0:T(8,128)(2,1)S(1)}, u32[]{:S(2)}, u32[]{:S(2)}) collective-permute-start(bf16[2,2,2,256,128]{4,3,2,1,0:T(8,128)(2,1)S(1)} %get-tuple-element.69), channel_id=1, source_target_pairs={{0,8},{4,12},{8,0},{12,4},{16,24},{20,28},{24,16},{28,20},{1,9},{5... | collective-permute-start | bytes 1572872 | tf_op jit(solution)/shard_map/ppermute | solution.py:249
  6.8 1.5 %collective-permute-start.5 = (bf16[2,2,2,256,128]{4,3,2,1,0:T(8,128)(2,1)S(1)}, bf16[2,2,2,256,128]{4,3,2,1,0:T(8,128)(2,1)S(1)}, u32[]{:S(2)}, u32[]{:S(2)}) collective-permute-start(bf16[2,2,2,256,128]{4,3,2,1,0:T(8,128)(2,1)S(1)} %get-tuple-element.70), channel_id=1, source_target_pairs={{0,16},{4,20},{8,24},{12,28},{16,0},{20,4},{24,8},{28,12},{1,17},{... | collective-permute-start | bytes 1572872 | tf_op jit(solution)/shard_map/ppermute | solution.py:249
  8.3 1.7 %fold.3 = (bf16[2,2,2,256,128]{4,3,2,1,0:T(8,128)(2,1)S(1)}, bf16[2,2,2,256,128]{4,3,2,1,0:T(8,128)(2,1)S(1)}, bf16[2,2,2,256,128]{4,3,2,1,0:T(8,128)(2,1)S(1)},...) custom-call(s32[16]{0:T(128)S(1)} %copy-done.3, f32[128]{0:T(128)S(1)} %copy-done.6, ...), custom_call_target="tpu_custom_call" | custom-call | tf_op jit(solution)/shard_map/fold/pallas_call | solution.py:230
  10.1 2.4 %tables.1 = (bf16[2048,640]{1,0:T(8,128)(2,1)S(1)}, bf16[2048,512]{1,0:T(8,128)(2,1)S(1)}) custom-call(s32[16]{0:T(128)S(1)} %copy-done.3, bf16[2,2,1024,512]{3,2,1,0:T(8,128)(2,1)S(1)} %copy-done, bf16[2,2,2,256,128]{4,3,2,1,0:T(8,128)(2,1)S(1)} %get-tuple-element.58.refs_0_), custom_call_target="tpu_custom_call" | custom-call | tf_op jit(solution)/shard_map/tables/pallas_call | solution.py:230
  12.5 7.0 %collective-permute-done.4.refs_1_ = bf16[2,2,2,256,128]{4,3,2,1,0:T(8,128)(2,1)S(1)} collective-permute-done((bf16[2,2,2,256,128]{4,3,2,1,0:T(8,128)(2,1)S(1)}, bf16[2,2,2,256,128]{4,3,2,1,0:T(8,128)(2,1)S(1)}, u32[]{:S(2)}, u32[]{:S(2)}) %collective-permute-start.4) | collective-permute-done | bytes 524320 | tf_op jit(solution)/shard_map/ppermute | solution.py:249
  19.6 11.9 %collective-permute-done.5.refs_2_ = bf16[2,2,2,256,128]{4,3,2,1,0:T(8,128)(2,1)S(1)} collective-permute-done((bf16[2,2,2,256,128]{4,3,2,1,0:T(8,128)(2,1)S(1)}, bf16[2,2,2,256,128]{4,3,2,1,0:T(8,128)(2,1)S(1)}, u32[]{:S(2)}, u32[]{:S(2)}) %collective-permute-start.5) | collective-permute-done | bytes 524320 | tf_op jit(solution)/shard_map/ppermute | solution.py:249
  34.2 1.6 %forward.2 = (bf16[64,1152]{1,0:T(8,128)(2,1)S(1)}, bf16[64,1152]{1,0:T(8,128)(2,1)S(1)}, bf16[64,1152]{1,0:T(8,128)(2,1)S(1)}, bf16[64,1152]{1,0:T(8,128)(2,1)S(1)}) custom-call(bf16[2048,640]{1,0:T(8,128)(2,1)S(1)} %get-tuple-element.59.table0, bf16[2048,512]{1,0:T(8,128)(2,1)S(1)} %get-tuple-element.60.refs_4_.table1, ...), custom_call_target="tpu_custom_call" | custom-call | tf_op jit(solution)/shard_map/forward/pallas_call | solution.py:230
  35.8 3.7 %collective-permute-start.8 = (bf16[64,1152]{1,0:T(8,128)(2,1)S(1)}, bf16[64,1152]{1,0:T(8,128)(2,1)S(1)}, u32[]{:S(2)}, u32[]{:S(2)}) collective-permute-start(bf16[64,1152]{1,0:T(8,128)(2,1)S(1)} %get-tuple-element.74), channel_id=1, source_target_pairs={{0,3},{1,2},{2,1},{3,0},{4,7},{5,6},{6,5},{7,4},{8,11},{9,10},{10,... | collective-permute-start | bytes 442376 | tf_op jit(solution)/shard_map/ppermute | solution.py:263
  42.2 1.6 %collective-permute-done.8.refs_3_ = bf16[64,1152]{1,0:T(8,128)(2,1)S(1)} collective-permute-done((bf16[64,1152]{1,0:T(8,128)(2,1)S(1)}, bf16[64,1152]{1,0:T(8,128)(2,1)S(1)}, u32[]{:S(2)}, u32[]{:S(2)}) %collective-permute-start.8) | collective-permute-done | bytes 147488 | tf_op jit(solution)/shard_map/ppermute | solution.py:263
  43.7 6.7 %collective-permute-start.9 = (bf16[64,1152]{1,0:T(8,128)(2,1)S(1)}, bf16[64,1152]{1,0:T(8,128)(2,1)S(1)}, u32[]{:S(2)}, u32[]{:S(2)}) collective-permute-start(bf16[64,1152]{1,0:T(8,128)(2,1)S(1)} %get-tuple-element.75), channel_id=1, source_target_pairs={{0,1},{1,0},{2,3},{3,2},{4,5},{5,4},{6,7},{7,6},{8,9},{9,8},{10,11... | collective-permute-start | bytes 442376 | tf_op jit(solution)/shard_map/ppermute | solution.py:263
  50.4 1.9 %collective-permute-done.10.refs_2_ = bf16[64,1152]{1,0:T(8,128)(2,1)S(1)} collective-permute-done((bf16[64,1152]{1,0:T(8,128)(2,1)S(1)}, bf16[64,1152]{1,0:T(8,128)(2,1)S(1)}, u32[]{:S(2)}, u32[]{:S(2)}) %collective-permute-start.10) | collective-permute-done | bytes 147488 | tf_op jit(solution)/shard_map/ppermute | solution.py:263
  52.3 3.0 %collective-permute-done.9.refs_1_ = bf16[64,1152]{1,0:T(8,128)(2,1)S(1)} collective-permute-done((bf16[64,1152]{1,0:T(8,128)(2,1)S(1)}, bf16[64,1152]{1,0:T(8,128)(2,1)S(1)}, u32[]{:S(2)}, u32[]{:S(2)}) %collective-permute-start.9) | collective-permute-done | bytes 147488 | tf_op jit(solution)/shard_map/ppermute | solution.py:263
  56.6 2.5 %collective-permute-start.14 = (bf16[64,1152]{1,0:T(8,128)(2,1)S(1)}, bf16[64,1152]{1,0:T(8,128)(2,1)S(1)}, u32[]{:S(2)}, u32[]{:S(2)}) collective-permute-start(bf16[64,1152]{1,0:T(8,128)(2,1)S(1)} %get-tuple-element.86), channel_id=1, source_target_pairs={{0,3},{1,2},{2,1},{3,0},{4,7},{5,6},{6,5},{7,4},{8,11},{9,10},{10,... | collective-permute-start | bytes 442376 | tf_op jit(solution)/shard_map/ppermute | solution.py:263
  59.2 6.1 %collective-permute-done.14.refs_3_ = bf16[64,1152]{1,0:T(8,128)(2,1)S(1)} collective-permute-done((bf16[64,1152]{1,0:T(8,128)(2,1)S(1)}, bf16[64,1152]{1,0:T(8,128)(2,1)S(1)}, u32[]{:S(2)}, u32[]{:S(2)}) %collective-permute-start.14) | collective-permute-done | bytes 147488 | tf_op jit(solution)/shard_map/ppermute | solution.py:263
  65.3 3.4 %collective-permute-start.15 = (bf16[64,1152]{1,0:T(8,128)(2,1)S(1)}, bf16[64,1152]{1,0:T(8,128)(2,1)S(1)}, u32[]{:S(2)}, u32[]{:S(2)}) collective-permute-start(bf16[64,1152]{1,0:T(8,128)(2,1)S(1)} %get-tuple-element.87), channel_id=1, source_target_pairs={{0,1},{1,0},{2,3},{3,2},{4,5},{5,4},{6,7},{7,6},{8,9},{9,8},{10,11... | collective-permute-start | bytes 442376 | tf_op jit(solution)/shard_map/ppermute | solution.py:263
  68.7 1.6 %forward.3 = (bf16[64,1152]{1,0:T(8,128)(2,1)S(1)}, bf16[64,1152]{1,0:T(8,128)(2,1)S(1)}, bf16[64,1152]{1,0:T(8,128)(2,1)S(1)}, bf16[64,1152]{1,0:T(8,128)(2,1)S(1)}) custom-call(bf16[2048,640]{1,0:T(8,128)(2,1)S(1)} %get-tuple-element.59.table0, bf16[2048,512]{1,0:T(8,128)(2,1)S(1)} %get-tuple-element.60.refs_4_.table1, ...), custom_call_target="tpu_custom_call" | custom-call | tf_op jit(solution)/shard_map/forward/pallas_call | solution.py:230
  70.3 2.3 %collective-permute-start.11 = (bf16[64,1152]{1,0:T(8,128)(2,1)S(1)}, bf16[64,1152]{1,0:T(8,128)(2,1)S(1)}, u32[]{:S(2)}, u32[]{:S(2)}) collective-permute-start(bf16[64,1152]{1,0:T(8,128)(2,1)S(1)} %get-tuple-element.81), channel_id=1, source_target_pairs={{0,3},{1,2},{2,1},{3,0},{4,7},{5,6},{6,5},{7,4},{8,11},{9,10},{10,... | collective-permute-start | bytes 442376 | tf_op jit(solution)/shard_map/ppermute | solution.py:263
  74.1 1.6 %inverse.2 = (bf16[2,2,2,256,128]{4,3,2,1,0:T(8,128)(2,1)S(1)}, bf16[2,2,2,256,128]{4,3,2,1,0:T(8,128)(2,1)S(1)}, bf16[2,2,2,256,128]{4,3,2,1,0:T(8,128)(2,1)S(1)}, bf16[2,2,2,256,128]{4,3,2,1,0:T(8,128)(2,1)S(1)}) custom-call(bf16[2048,640]{1,0:T(8,128)(2,1)S(1)} %get-tuple-element.59.table0, bf16[2048,512]{1,0:T(8,128)(2,1)S(1)} %get-tuple-element.60.refs_4_.table1, ...), custom_call_target="tpu_custom_call" | custom-call | tf_op jit(solution)/shard_map/inverse/pallas_call | solution.py:230
  79.8 2.5 %collective-permute-start.12 = (bf16[64,1152]{1,0:T(8,128)(2,1)S(1)}, bf16[64,1152]{1,0:T(8,128)(2,1)S(1)}, u32[]{:S(2)}, u32[]{:S(2)}) collective-permute-start(bf16[64,1152]{1,0:T(8,128)(2,1)S(1)} %get-tuple-element.82), channel_id=1, source_target_pairs={{0,1},{1,0},{2,3},{3,2},{4,5},{5,4},{6,7},{7,6},{8,9},{9,8},{10,11... | collective-permute-start | bytes 442376 | tf_op jit(solution)/shard_map/ppermute | solution.py:263
  82.3 4.2 %collective-permute-done.13.refs_2_ = bf16[64,1152]{1,0:T(8,128)(2,1)S(1)} collective-permute-done((bf16[64,1152]{1,0:T(8,128)(2,1)S(1)}, bf16[64,1152]{1,0:T(8,128)(2,1)S(1)}, u32[]{:S(2)}, u32[]{:S(2)}) %collective-permute-start.13) | collective-permute-done | bytes 147488 | tf_op jit(solution)/shard_map/ppermute | solution.py:263
  88.2 1.7 %collective-permute-start.17 = (bf16[64,1152]{1,0:T(8,128)(2,1)S(1)}, bf16[64,1152]{1,0:T(8,128)(2,1)S(1)}, u32[]{:S(2)}, u32[]{:S(2)}) collective-permute-start(bf16[64,1152]{1,0:T(8,128)(2,1)S(1)} %get-tuple-element.93), channel_id=1, source_target_pairs={{0,3},{1,2},{2,1},{3,0},{4,7},{5,6},{6,5},{7,4},{8,11},{9,10},{10,... | collective-permute-start | bytes 442376 | tf_op jit(solution)/shard_map/ppermute | solution.py:263
  90.2 6.0 %collective-permute-done.17.refs_3_ = bf16[64,1152]{1,0:T(8,128)(2,1)S(1)} collective-permute-done((bf16[64,1152]{1,0:T(8,128)(2,1)S(1)}, bf16[64,1152]{1,0:T(8,128)(2,1)S(1)}, u32[]{:S(2)}, u32[]{:S(2)}) %collective-permute-start.17) | collective-permute-done | bytes 147488 | tf_op jit(solution)/shard_map/ppermute | solution.py:263
  96.3 3.1 %collective-permute-start.18 = (bf16[64,1152]{1,0:T(8,128)(2,1)S(1)}, bf16[64,1152]{1,0:T(8,128)(2,1)S(1)}, u32[]{:S(2)}, u32[]{:S(2)}) collective-permute-start(bf16[64,1152]{1,0:T(8,128)(2,1)S(1)} %get-tuple-element.94), channel_id=1, source_target_pairs={{0,1},{1,0},{2,3},{3,2},{4,5},{5,4},{6,7},{7,6},{8,9},{9,8},{10,11... | collective-permute-start | bytes 442376 | tf_op jit(solution)/shard_map/ppermute | solution.py:263
  100.3 2.1 %collective-permute-done.18.refs_1_ = bf16[64,1152]{1,0:T(8,128)(2,1)S(1)} collective-permute-done((bf16[64,1152]{1,0:T(8,128)(2,1)S(1)}, bf16[64,1152]{1,0:T(8,128)(2,1)S(1)}, u32[]{:S(2)}, u32[]{:S(2)}) %collective-permute-start.18) | collective-permute-done | bytes 147488 | tf_op jit(solution)/shard_map/ppermute | solution.py:263
  102.5 1.6 %inverse.3 = (bf16[2,2,2,256,128]{4,3,2,1,0:T(8,128)(2,1)S(1)}, bf16[2,2,2,256,128]{4,3,2,1,0:T(8,128)(2,1)S(1)}, bf16[2,2,2,256,128]{4,3,2,1,0:T(8,128)(2,1)S(1...) custom-call(bf16[2048,640]{1,0:T(8,128)(2,1)S(1)} %get-tuple-element.59.table0, ...), custom_call_target="tpu_custom_call" | custom-call | tf_op jit(solution)/shard_map/inverse/pallas_call | solution.py:230
  104.7 2.0 %collective-permute-done.23.swapped = bf16[4,2,2,256,128]{4,3,2,1,0:T(8,128)(2,1)S(1)} collective-permute-done((bf16[4,2,2,256,128]{4,3,2,1,0:T(8,128)(2,1)S(1)}, bf16[4,2,2,256,128]{4,3,2,1,0:T(8,128)(2,1)S(1)}, u32[]{:S(2)}, u32[]{:S(2)}) %collective-permute-start.23) | collective-permute-done | bytes 1048608 | tf_op jit(solution)/shard_map/ppermute | solution.py:268
  110.4 2.0 %unfold.2.refs_4_ = bf16[16,2,512,128]{3,2,1,0:T(8,128)(2,1)} custom-call(s32[16]{0:T(128)S(1)} %copy-done.3, s32[1,128]{1,0:T(1,128)S(1)} %bitcast.7, bf16[2,2,2,256,128]{4,3,2,1,0:T(8,128)(2,1)S(1)} %get-tuple-element.90.refs_4_.refs_0_, bf16[2,2,2,256,128]{4,3,2,1,0:T(8,128)(2,1)S(1)} %collective-permute-done.20.refs_5_.refs_1_, ...), custom_call_target="tpu_custom_call" | custom-call | tf_op jit(solution)/shard_map/unfold/pallas_call | solution.py:230
  112.4 9.3 %collective-permute-done.24.refs_1_ = bf16[2,2,2,256,128]{4,3,2,1,0:T(8,128)(2,1)S(1)} collective-permute-done((bf16[2,2,2,256,128]{4,3,2,1,0:T(8,128)(2,1)S(1)}, bf16[2,2,2,256,128]{4,3,2,1,0:T(8,128)(2,1)S(1)}, u32[]{:S(2)}, u32[]{:S(2)}) %collective-permute-start.24) | collective-permute-done | bytes 524320 | tf_op jit(solution)/shard_map/ppermute | solution.py:249
  121.7 9.8 %collective-permute-done.25.refs_2_ = bf16[2,2,2,256,128]{4,3,2,1,0:T(8,128)(2,1)S(1)} collective-permute-done((bf16[2,2,2,256,128]{4,3,2,1,0:T(8,128)(2,1)S(1)}, bf16[2,2,2,256,128]{4,3,2,1,0:T(8,128)(2,1)S(1)}, u32[]{:S(2)}, u32[]{:S(2)}) %collective-permute-start.25) | collective-permute-done | bytes 524320 | tf_op jit(solution)/shard_map/ppermute | solution.py:249
  131.4 1.6 %collective-permute-done.26.refs_3_ = bf16[2,2,2,256,128]{4,3,2,1,0:T(8,128)(2,1)S(1)} collective-permute-done((bf16[2,2,2,256,128]{4,3,2,1,0:T(8,128)(2,1)S(1)}, bf16[2,2,2,256,128]{4,3,2,1,0:T(8,128)(2,1)S(1)}, u32[]{:S(2)}, u32[]{:S(2)}) %collective-permute-start.26) | collective-permute-done | bytes 524320 | tf_op jit(solution)/shard_map/ppermute | solution.py:249
  133.0 2.0 %unfold.3 = bf16[16,2,512,128]{3,2,1,0:T(8,128)(2,1)} custom-call(s32[16]{0:T(128)S(1)} %copy-done.3, s32[1,128]{1,0:T(1,128)S(1)} %bitcast.8, bf16[2,2,2,256,128]{4,3,2,1,0:T(8,128)(2,1)S(1)} %get-tuple-element.105.refs_0_, bf16[2,2,2,256,128]{4,3,2,1,0:T(8,128)(2,1)S(1)} %collective-permute-done.24.refs_1_, ...), custom_call_target="tpu_custom_call", output_to_operand_aliasing={{}: (6, {})} | custom-call | tf_op jit(solution)/shard_map/unfold/pallas_call | solution.py:230
  (53 shorter events, 21.8 us)
Async XLA Ops:
  2.0 8.1 %copy-start = (bf16[2,2,1024,512]{3,2,1,0:T(8,128)(2,1)S(1)}, bf16[2,2,1024,512]{3,2,1,0:T(8,128)(2,1)}, u32[]{:S(2)}) copy-start(bf16[2,2,1024,512]{3,2,1,0:T(8,128)(2,1)} %leg.1) | copy-start | bytes 12582916
  3.8 15.8 %collective-permute-start.4 = (bf16[2,2,2,256,128]{4,3,2,1,0:T(8,128)(2,1)S(1)}, bf16[2,2,2,256,128]{4,3,2,1,0:T(8,128)(2,1)S(1)}, u32[]{:S(2)}, u32[]{:S(2)}) collective-permute-start(bf16[2,2,2,256,128]{4,3,2,1,0:T(8,128)(2,1)S(1)} %get-tuple-element.69), channel_id=1, source_target_pairs={{0,8},{4,12},{8,0},{12,4},{16,24},{20,28},{24,16},{28,20},{1,9},{5... | collective-permute-start | bytes 1572872 | tf_op jit(solution)/shard_map/ppermute | solution.py:249
  6.8 24.6 %collective-permute-start.5 = (bf16[2,2,2,256,128]{4,3,2,1,0:T(8,128)(2,1)S(1)}, bf16[2,2,2,256,128]{4,3,2,1,0:T(8,128)(2,1)S(1)}, u32[]{:S(2)}, u32[]{:S(2)}) collective-permute-start(bf16[2,2,2,256,128]{4,3,2,1,0:T(8,128)(2,1)S(1)} %get-tuple-element.70), channel_id=1, source_target_pairs={{0,16},{4,20},{8,24},{12,28},{16,0},{20,4},{24,8},{28,12},{1,17},{... | collective-permute-start | bytes 1572872 | tf_op jit(solution)/shard_map/ppermute | solution.py:249
  8.3 23.1 %collective-permute-start.6 = (bf16[2,2,2,256,128]{4,3,2,1,0:T(8,128)(2,1)S(1)}, bf16[2,2,2,256,128]{4,3,2,1,0:T(8,128)(2,1)S(1)}, u32[]{:S(2)}, u32[]{:S(2)}) collective-permute-start(bf16[2,2,2,256,128]{4,3,2,1,0:T(8,128)(2,1)S(1)} %get-tuple-element.71), channel_id=1, source_target_pairs={{0,24},{4,28},{8,16},{12,20},{16,8},{20,12},{24,0},{28,4},{1,25},{... | collective-permute-start | bytes 1572872 | tf_op jit(solution)/shard_map/ppermute | solution.py:249
  10.0 21.6 %collective-permute-start = (bf16[4,2,2,256,128]{4,3,2,1,0:T(8,128)(2,1)S(1)}, bf16[4,2,2,256,128]{4,3,2,1,0:T(8,128)(2,1)S(1)}, u32[]{:S(2)}, u32[]{:S(2)}) collective-permute-start(bf16[4,2,2,256,128]{4,3,2,1,0:T(8,128)(2,1)S(1)} %get-tuple-element.61), channel_id=1, source_target_pairs={{0,4},{4,0},{8,12},{12,8},{16,20},{20,16},{24,28},{28,24},{1,5},{5... | collective-permute-start | bytes 3145736 | tf_op jit(solution)/shard_map/ppermute | solution.py:268
  31.5 2.7 %collective-permute-start.7 = (bf16[4,2,2,256,128]{4,3,2,1,0:T(8,128)(2,1)S(1)}, bf16[4,2,2,256,128]{4,3,2,1,0:T(8,128)(2,1)S(1)}, u32[]{:S(2)}, u32[]{:S(2)}) collective-permute-start(bf16[4,2,2,256,128]{4,3,2,1,0:T(8,128)(2,1)S(1)} %gather.2), channel_id=1, source_target_pairs={{0,4},{4,0},{8,12},{12,8},{16,20},{20,16},{24,28},{28,24},{1,5},{5... | collective-permute-start | bytes 3145736 | tf_op jit(solution)/shard_map/ppermute | solution.py:268
  31.7 23.7 %copy-start.1 = (bf16[128,128]{1,0:T(8,128)(2,1)S(1)}, bf16[128,128]{1,0:T(8,128)(2,1)}, u32[]{:S(2)}) copy-start(bf16[128,128]{1,0:T(8,128)(2,1)} %project.3) | copy-start | bytes 98308
  31.7 23.7 %copy-start.2 = (bf16[128,128]{1,0:T(8,128)(2,1)S(1)}, bf16[128,128]{1,0:T(8,128)(2,1)}, u32[]{:S(2)}) copy-start(bf16[128,128]{1,0:T(8,128)(2,1)} %vertical.3) | copy-start | bytes 98308
  31.7 23.7 %copy-start.5 = (f32[128]{0:T(128)S(1)}, f32[128]{0:T(128)}, u32[]{:S(2)}) copy-start(f32[128]{0:T(128)} %rates.3) | copy-start | bytes 1540
  31.7 37.0 %collective-permute-start.1 = (bf16[2,2,2,256,128]{4,3,2,1,0:T(8,128)(2,1)S(1)}, bf16[2,2,2,256,128]{4,3,2,1,0:T(8,128)(2,1)S(1)}, u32[]{:S(2)}, u32[]{:S(2)}) collective-permute-start(bf16[2,2,2,256,128]{4,3,2,1,0:T(8,128)(2,1)S(1)} %get-tuple-element.66), channel_id=1, source_target_pairs={{0,8},{4,12},{8,0},{12,4},{16,24},{20,28},{24,16},{28,20},{1,9},{5... | collective-permute-start | bytes 1572872 | tf_op jit(solution)/shard_map/ppermute | solution.py:249
  35.8 7.9 %collective-permute-start.8 = (bf16[64,1152]{1,0:T(8,128)(2,1)S(1)}, bf16[64,1152]{1,0:T(8,128)(2,1)S(1)}, u32[]{:S(2)}, u32[]{:S(2)}) collective-permute-start(bf16[64,1152]{1,0:T(8,128)(2,1)S(1)} %get-tuple-element.74), channel_id=1, source_target_pairs={{0,3},{1,2},{2,1},{3,0},{4,7},{5,6},{6,5},{7,4},{8,11},{9,10},{10,... | collective-permute-start | bytes 442376 | tf_op jit(solution)/shard_map/ppermute | solution.py:263
  39.5 29.2 %collective-permute-start.2 = (bf16[2,2,2,256,128]{4,3,2,1,0:T(8,128)(2,1)S(1)}, bf16[2,2,2,256,128]{4,3,2,1,0:T(8,128)(2,1)S(1)}, u32[]{:S(2)}, u32[]{:S(2)}) collective-permute-start(bf16[2,2,2,256,128]{4,3,2,1,0:T(8,128)(2,1)S(1)} %get-tuple-element.67), channel_id=1, source_target_pairs={{0,16},{4,20},{8,24},{12,28},{16,0},{20,4},{24,8},{28,12},{1,17},{... | collective-permute-start | bytes 1572872 | tf_op jit(solution)/shard_map/ppermute | solution.py:249
  41.0 27.7 %collective-permute-start.3 = (bf16[2,2,2,256,128]{4,3,2,1,0:T(8,128)(2,1)S(1)}, bf16[2,2,2,256,128]{4,3,2,1,0:T(8,128)(2,1)S(1)}, u32[]{:S(2)}, u32[]{:S(2)}) collective-permute-start(bf16[2,2,2,256,128]{4,3,2,1,0:T(8,128)(2,1)S(1)} %get-tuple-element.68), channel_id=1, source_target_pairs={{0,24},{4,28},{8,16},{12,20},{16,8},{20,12},{24,0},{28,4},{1,25},{... | collective-permute-start | bytes 1572872 | tf_op jit(solution)/shard_map/ppermute | solution.py:249
  42.1 10.2 %collective-permute-start.10 = (bf16[64,1152]{1,0:T(8,128)(2,1)S(1)}, bf16[64,1152]{1,0:T(8,128)(2,1)S(1)}, u32[]{:S(2)}, u32[]{:S(2)}) collective-permute-start(bf16[64,1152]{1,0:T(8,128)(2,1)S(1)} %get-tuple-element.76), channel_id=1, source_target_pairs={{0,2},{1,3},{2,0},{3,1},{4,6},{5,7},{6,4},{7,5},{8,10},{9,11},{10,... | collective-permute-start | bytes 442376 | tf_op jit(solution)/shard_map/ppermute | solution.py:263
  43.7 11.6 %collective-permute-start.9 = (bf16[64,1152]{1,0:T(8,128)(2,1)S(1)}, bf16[64,1152]{1,0:T(8,128)(2,1)S(1)}, u32[]{:S(2)}, u32[]{:S(2)}) collective-permute-start(bf16[64,1152]{1,0:T(8,128)(2,1)S(1)} %get-tuple-element.75), channel_id=1, source_target_pairs={{0,1},{1,0},{2,3},{3,2},{4,5},{5,4},{6,7},{7,6},{8,9},{9,8},{10,11... | collective-permute-start | bytes 442376 | tf_op jit(solution)/shard_map/ppermute | solution.py:263
  56.6 8.6 %collective-permute-start.14 = (bf16[64,1152]{1,0:T(8,128)(2,1)S(1)}, bf16[64,1152]{1,0:T(8,128)(2,1)S(1)}, u32[]{:S(2)}, u32[]{:S(2)}) collective-permute-start(bf16[64,1152]{1,0:T(8,128)(2,1)S(1)} %get-tuple-element.86), channel_id=1, source_target_pairs={{0,3},{1,2},{2,1},{3,0},{4,7},{5,6},{6,5},{7,4},{8,11},{9,10},{10,... | collective-permute-start | bytes 442376 | tf_op jit(solution)/shard_map/ppermute | solution.py:263
  59.2 13.7 %collective-permute-start.16 = (bf16[64,1152]{1,0:T(8,128)(2,1)S(1)}, bf16[64,1152]{1,0:T(8,128)(2,1)S(1)}, u32[]{:S(2)}, u32[]{:S(2)}) collective-permute-start(bf16[64,1152]{1,0:T(8,128)(2,1)S(1)} %get-tuple-element.88), channel_id=1, source_target_pairs={{0,2},{1,3},{2,0},{3,1},{4,6},{5,7},{6,4},{7,5},{8,10},{9,11},{10,... | collective-permute-start | bytes 442376 | tf_op jit(solution)/shard_map/ppermute | solution.py:263
  65.3 8.9 %collective-permute-start.15 = (bf16[64,1152]{1,0:T(8,128)(2,1)S(1)}, bf16[64,1152]{1,0:T(8,128)(2,1)S(1)}, u32[]{:S(2)}, u32[]{:S(2)}) collective-permute-start(bf16[64,1152]{1,0:T(8,128)(2,1)S(1)} %get-tuple-element.87), channel_id=1, source_target_pairs={{0,1},{1,0},{2,3},{3,2},{4,5},{5,4},{6,7},{7,6},{8,9},{9,8},{10,11... | collective-permute-start | bytes 442376 | tf_op jit(solution)/shard_map/ppermute | solution.py:263
  70.3 9.6 %collective-permute-start.11 = (bf16[64,1152]{1,0:T(8,128)(2,1)S(1)}, bf16[64,1152]{1,0:T(8,128)(2,1)S(1)}, u32[]{:S(2)}, u32[]{:S(2)}) collective-permute-start(bf16[64,1152]{1,0:T(8,128)(2,1)S(1)} %get-tuple-element.81), channel_id=1, source_target_pairs={{0,3},{1,2},{2,1},{3,0},{4,7},{5,6},{6,5},{7,4},{8,11},{9,10},{10,... | collective-permute-start | bytes 442376 | tf_op jit(solution)/shard_map/ppermute | solution.py:263
  75.7 26.7 %collective-permute-start.20 = (bf16[2,2,2,256,128]{4,3,2,1,0:T(8,128)(2,1)S(1)}, bf16[2,2,2,256,128]{4,3,2,1,0:T(8,128)(2,1)S(1)}, u32[]{:S(2)}, u32[]{:S(2)}) collective-permute-start(bf16[2,2,2,256,128]{4,3,2,1,0:T(8,128)(2,1)S(1)} %get-tuple-element.97), channel_id=1, source_target_pairs={{0,8},{4,12},{8,0},{12,4},{16,24},{20,28},{24,16},{28,20},{1,9},{5... | collective-permute-start | bytes 1572872 | tf_op jit(solution)/shard_map/ppermute | solution.py:249
  77.0 25.5 %collective-permute-start.21 = (bf16[2,2,2,256,128]{4,3,2,1,0:T(8,128)(2,1)S(1)}, bf16[2,2,2,256,128]{4,3,2,1,0:T(8,128)(2,1)S(1)}, u32[]{:S(2)}, u32[]{:S(2)}) collective-permute-start(bf16[2,2,2,256,128]{4,3,2,1,0:T(8,128)(2,1)S(1)} %get-tuple-element.98), channel_id=1, source_target_pairs={{0,16},{4,20},{8,24},{12,28},{16,0},{20,4},{24,8},{28,12},{1,17},{... | collective-permute-start | bytes 1572872 | tf_op jit(solution)/shard_map/ppermute | solution.py:249
  77.8 24.6 %collective-permute-start.22 = (bf16[2,2,2,256,128]{4,3,2,1,0:T(8,128)(2,1)S(1)}, bf16[2,2,2,256,128]{4,3,2,1,0:T(8,128)(2,1)S(1)}, u32[]{:S(2)}, u32[]{:S(2)}) collective-permute-start(bf16[2,2,2,256,128]{4,3,2,1,0:T(8,128)(2,1)S(1)} %get-tuple-element.99), channel_id=1, source_target_pairs={{0,24},{4,28},{8,16},{12,20},{16,8},{20,12},{24,0},{28,4},{1,25},{... | collective-permute-start | bytes 1572872 | tf_op jit(solution)/shard_map/ppermute | solution.py:249
  79.3 7.3 %collective-permute-start.13 = (bf16[64,1152]{1,0:T(8,128)(2,1)S(1)}, bf16[64,1152]{1,0:T(8,128)(2,1)S(1)}, u32[]{:S(2)}, u32[]{:S(2)}) collective-permute-start(bf16[64,1152]{1,0:T(8,128)(2,1)S(1)} %get-tuple-element.83), channel_id=1, source_target_pairs={{0,2},{1,3},{2,0},{3,1},{4,6},{5,7},{6,4},{7,5},{8,10},{9,11},{10,... | collective-permute-start | bytes 442376 | tf_op jit(solution)/shard_map/ppermute | solution.py:263
  79.8 7.2 %collective-permute-start.12 = (bf16[64,1152]{1,0:T(8,128)(2,1)S(1)}, bf16[64,1152]{1,0:T(8,128)(2,1)S(1)}, u32[]{:S(2)}, u32[]{:S(2)}) collective-permute-start(bf16[64,1152]{1,0:T(8,128)(2,1)S(1)} %get-tuple-element.82), channel_id=1, source_target_pairs={{0,1},{1,0},{2,3},{3,2},{4,5},{5,4},{6,7},{7,6},{8,9},{9,8},{10,11... | collective-permute-start | bytes 442376 | tf_op jit(solution)/shard_map/ppermute | solution.py:263
  88.2 8.0 %collective-permute-start.17 = (bf16[64,1152]{1,0:T(8,128)(2,1)S(1)}, bf16[64,1152]{1,0:T(8,128)(2,1)S(1)}, u32[]{:S(2)}, u32[]{:S(2)}) collective-permute-start(bf16[64,1152]{1,0:T(8,128)(2,1)S(1)} %get-tuple-element.93), channel_id=1, source_target_pairs={{0,3},{1,2},{2,1},{3,0},{4,7},{5,6},{6,5},{7,4},{8,11},{9,10},{10,... | collective-permute-start | bytes 442376 | tf_op jit(solution)/shard_map/ppermute | solution.py:263
  89.9 10.4 %collective-permute-start.19 = (bf16[64,1152]{1,0:T(8,128)(2,1)S(1)}, bf16[64,1152]{1,0:T(8,128)(2,1)S(1)}, u32[]{:S(2)}, u32[]{:S(2)}) collective-permute-start(bf16[64,1152]{1,0:T(8,128)(2,1)S(1)} %get-tuple-element.95), channel_id=1, source_target_pairs={{0,2},{1,3},{2,0},{3,1},{4,6},{5,7},{6,4},{7,5},{8,10},{9,11},{10,... | collective-permute-start | bytes 442376 | tf_op jit(solution)/shard_map/ppermute | solution.py:263
  96.3 6.2 %collective-permute-start.18 = (bf16[64,1152]{1,0:T(8,128)(2,1)S(1)}, bf16[64,1152]{1,0:T(8,128)(2,1)S(1)}, u32[]{:S(2)}, u32[]{:S(2)}) collective-permute-start(bf16[64,1152]{1,0:T(8,128)(2,1)S(1)} %get-tuple-element.94), channel_id=1, source_target_pairs={{0,1},{1,0},{2,3},{3,2},{4,5},{5,4},{6,7},{7,6},{8,9},{9,8},{10,11... | collective-permute-start | bytes 442376 | tf_op jit(solution)/shard_map/ppermute | solution.py:263
  104.0 2.7 %collective-permute-start.23 = (bf16[4,2,2,256,128]{4,3,2,1,0:T(8,128)(2,1)S(1)}, bf16[4,2,2,256,128]{4,3,2,1,0:T(8,128)(2,1)S(1)}, u32[]{:S(2)}, u32[]{:S(2)}) collective-permute-start(bf16[4,2,2,256,128]{4,3,2,1,0:T(8,128)(2,1)S(1)} %get-tuple-element.100), channel_id=1, source_target_pairs={{0,4},{4,0},{8,12},{12,8},{16,20},{20,16},{24,28},{28,24},{1,5},{5... | collective-permute-start | bytes 3145736 | tf_op jit(solution)/shard_map/ppermute | solution.py:268
  104.2 6.2 %collective-permute-start.27 = (bf16[4,2,2,256,128]{4,3,2,1,0:T(8,128)(2,1)S(1)}, bf16[4,2,2,256,128]{4,3,2,1,0:T(8,128)(2,1)S(1)}, u32[]{:S(2)}, u32[]{:S(2)}) collective-permute-start(bf16[4,2,2,256,128]{4,3,2,1,0:T(8,128)(2,1)S(1)} %gather.3), channel_id=1, source_target_pairs={{0,4},{4,0},{8,12},{12,8},{16,20},{20,16},{24,28},{28,24},{1,5},{5... | collective-permute-start | bytes 3145736 | tf_op jit(solution)/shard_map/ppermute | solution.py:268
  106.8 14.8 %collective-permute-start.24 = (bf16[2,2,2,256,128]{4,3,2,1,0:T(8,128)(2,1)S(1)}, bf16[2,2,2,256,128]{4,3,2,1,0:T(8,128)(2,1)S(1)}, u32[]{:S(2)}, u32[]{:S(2)}) collective-permute-start(bf16[2,2,2,256,128]{4,3,2,1,0:T(8,128)(2,1)S(1)} %get-tuple-element.106), channel_id=1, source_target_pairs={{0,8},{4,12},{8,0},{12,4},{16,24},{20,28},{24,16},{28,20},{1,9},{5... | collective-permute-start | bytes 1572872 | tf_op jit(solution)/shard_map/ppermute | solution.py:249
  108.1 23.3 %collective-permute-start.25 = (bf16[2,2,2,256,128]{4,3,2,1,0:T(8,128)(2,1)S(1)}, bf16[2,2,2,256,128]{4,3,2,1,0:T(8,128)(2,1)S(1)}, u32[]{:S(2)}, u32[]{:S(2)}) collective-permute-start(bf16[2,2,2,256,128]{4,3,2,1,0:T(8,128)(2,1)S(1)} %get-tuple-element.107), channel_id=1, source_target_pairs={{0,16},{4,20},{8,24},{12,28},{16,0},{20,4},{24,8},{28,12},{1,17},{... | collective-permute-start | bytes 1572872 | tf_op jit(solution)/shard_map/ppermute | solution.py:249
  108.9 24.1 %collective-permute-start.26 = (bf16[2,2,2,256,128]{4,3,2,1,0:T(8,128)(2,1)S(1)}, bf16[2,2,2,256,128]{4,3,2,1,0:T(8,128)(2,1)S(1)}, u32[]{:S(2)}, u32[]{:S(2)}) collective-permute-start(bf16[2,2,2,256,128]{4,3,2,1,0:T(8,128)(2,1)S(1)} %get-tuple-element.108), channel_id=1, source_target_pairs={{0,24},{4,28},{8,16},{12,20},{16,8},{20,12},{24,0},{28,4},{1,25},{... | collective-permute-start | bytes 1572872 | tf_op jit(solution)/shard_map/ppermute | solution.py:249
  (3 other events, 2.0 us)

commit v4 on v3

--- a/solution.py
+++ b/solution.py
@@ -8,7 +8,8 @@
 from jax.sharding import PartitionSpec as P
 
 coupling = 2.0
-CFG = {'zc': (2, 2, 2, 2), 'g1': 0, 'i0': 0, 's1': 0, 'i1': 1, 'late': (1, 0), 'vm': 24, 'fvm': 48, 'u': 0}
+VMEM_MIB = 24
+FOLD_VMEM_MIB = 48
 LANES = 128
 
 
@@ -47,19 +48,15 @@
         ).astype(jnp.bfloat16)
 
 
-def fold_kernel(cut, row0, late, wave_in, quad_in, cycles_in, grid, *refs):
+def fold_kernel(cut, row0, late, weights, grid, *refs):
     lat_n = cut["lat"]
-    outs = refs[-6 - lat_n // 2 : -6]
+    outs = refs[-2 - lat_n // 2 : -2]
     if not late:
-        outs, others = refs[-7 - lat_n // 2 : -7], refs[-7]
-    held, wave, quad, cycles, sems, small = refs[-6:]
+        outs, others = refs[-3 - lat_n // 2 : -3], refs[-3]
+    held, sems = refs[-2:]
     rows = held.shape[3]
     me = lax.axis_index("lat")
-    copies = [
-        pltpu.make_async_copy(wave_in, wave, small.at[0]),
-        pltpu.make_async_copy(quad_in, quad, small.at[1]),
-        pltpu.make_async_copy(cycles_in, cycles, small.at[2]),
-    ]
+    copies = []
     for step in range(lat_n):
         owner = jnp.bitwise_xor(me, step)
         copies.append(
@@ -71,13 +68,11 @@
         )
     for copy in copies:
         copy.start()
-    for copy in copies[:3]:
-        copy.wait()
     for step in range(lat_n):
         owner = jnp.bitwise_xor(me, step)
-        copies[3 + step].wait()
+        copies[step].wait()
         for slot in range(2):
-            weight = jnp.where(2 * wave[2 * owner + slot] < cycles[...], quad[...], 0.0)[None]
+            weight = weights[pl.ds(2 * owner + slot, 1), :]
             north = held[step, slot, 0].astype(jnp.float32)
             south = held[step, slot, 1].astype(jnp.float32)
             out = outs[step // 2].at[step % 2]
@@ -191,24 +186,29 @@
         at += kk
 
 
+def part_kernel(cut, swapped, *outs):
+    for step, out in enumerate(outs):
+        out[0] = swapped[step]
+
+
 def merge_kernel(cut, swapped, *refs):
     outs = refs[-(cut["lat"] // 2) :]
     for step, out in enumerate(outs):
         out[1] = swapped[step]
 
 
-def unfold_kernel(cut, row0, late, wave, cycles, *refs):
-    lat_n = cut["lat"]
-    parts, (out, held, sems) = arrivals(refs, lat_n, late), refs[-3:]
+def unfold_kernel(row0, places, wave, cycles, *refs):
+    out, held, sems = refs[-3:]
     rows = held.shape[3]
     me = lax.axis_index("lat")
     copies = []
-    for step in range(lat_n):
-        owner = jnp.bitwise_xor(me, step)
+    for step, (r, ref, at) in enumerate(places):
+        part = refs[ref].at[at]
+        owner = jnp.bitwise_xor(me, r)
         for slot in range(2):
             seen = 2 * wave[2 * owner + slot] < cycles[...]
-            even = parts[step][slot, 0].astype(jnp.float32)
-            odd = parts[step][slot, 1].astype(jnp.float32)
+            even = part[slot, 0].astype(jnp.float32)
+            odd = part[slot, 1].astype(jnp.float32)
             held[step, slot, 0] = jnp.where(seen, even + odd, 0.0).astype(jnp.bfloat16)
             held[step, slot, 1] = jnp.where(seen, even - odd, 0.0).astype(jnp.bfloat16)
         copy = pltpu.make_async_copy(
@@ -236,7 +236,7 @@
         scratch_shapes=list(scratch),
         input_output_aliases=aliases or {},
         cost_estimate=pl.CostEstimate(flops=0, bytes_accessed=0, transcendentals=0),
-        compiler_params=pltpu.CompilerParams(vmem_limit_bytes=(vm or CFG["vm"]) * 2**20),
+        compiler_params=pltpu.CompilerParams(vmem_limit_bytes=(vm or VMEM_MIB) * 2**20),
     )(*ins, *after)
 
 
@@ -252,14 +252,12 @@
     ]
 
 
-def between_levels(parts, count, mode):
+def between_levels(parts, count, chained):
     out = [parts[0]] + [None] * (count - 1)
-    waits = {0: {}, 1: {3: 1}, 2: {1: 3}, 3: {1: 2}, 4: {3: 2}, 5: {2: 1}}[mode]
-    order = sorted(range(1, count), key=lambda r: (r in waits, r))
-    for r in order:
+    for r in list(range(2, count)) + [1]:
         part = parts[r]
-        if r in waits:
-            part, out[waits[r]] = lax.optimization_barrier((part, out[waits[r]]))
+        if r == 1 and chained and count > 2:
+            part, out[count - 1] = lax.optimization_barrier((part, out[count - 1]))
         out[r] = lax.ppermute(part, "lev", [(i, i ^ r) for i in range(count)])
     return out
 
@@ -269,9 +267,7 @@
 
 
 def blocks_of(cols, lev_n):
-    pieces = 2
-    while pieces > 1 and cols % (pieces * lev_n):
-        pieces //= 2
+    pieces = 1 if cols % (2 * lev_n) else 2
     return [(p * cols // pieces, cols // pieces) for p in range(pieces)]
 
 
@@ -293,11 +289,13 @@
         "kk": kk,
     }
     lines = jnp.transpose(grid, (0, 2, 3, 4, 5, 1)).reshape(slots, halves, cols * levels, width)
+    present = wave_ids[:, None] < cycle_points[None, :] - wave_ids[:, None]
+    weights = jnp.where(present, quad[None, :], 0.0)
     cycle_row = cycle_points.reshape(1, width)
 
     blocks = blocks_of(cols, lev_n)
     near_n = lat_n // 2
-    lates = [bool(CFG["late"][block]) for block in range(len(blocks))]
+    lates = [block == 0 for block in range(len(blocks))]
     last = ()
     arrived = []
 
@@ -326,8 +324,8 @@
         )
         return [*near, swap_cores(others, lat_n)]
 
-    def outgoing(rows, late):
-        shapes = [struct(2, 2, 2, rows, width)] * near_n
+    def outgoing(rows, late, split=False):
+        shapes = [struct(1 if split else 2, 2, 2, rows, width)] * near_n
         return shapes if late else shapes + [struct(near_n, 2, 2, rows, width)]
 
     for (first, count), late in zip(blocks, lates):
@@ -335,20 +333,16 @@
         folded = call(
             functools.partial(fold_kernel, cut, first * levels, late),
             "fold",
-            (wave_ids, quad, cycle_points, lines),
-            [in_hbm] * 4,
+            (weights, lines),
+            [vmem, in_hbm],
             outgoing(rows, late),
             [vmem] * len(outgoing(rows, late)),
             [
                 pltpu.VMEM((lat_n, 2, 2, rows, width), jnp.bfloat16),
-                pltpu.SMEM((slots,), jnp.int32),
-                pltpu.VMEM((width,), jnp.float32),
-                pltpu.VMEM((width,), jnp.int32),
                 pltpu.SemaphoreType.DMA((lat_n,)),
-                pltpu.SemaphoreType.DMA((3,)),
             ],
             after=last,
-            vm=CFG["fvm"],
+            vm=FOLD_VMEM_MIB,
         )
         last = (folded[0],)
         if not late:
@@ -383,7 +377,7 @@
             [],
             after=last,
         )
-        return between_levels(packed, lev_n, CFG["zc"][2 * block]), (packed[0],)
+        return between_levels(packed, lev_n, True), (packed[0],)
 
     def solve(block, packed, last):
         share = packed[0].shape[0]
@@ -397,9 +391,9 @@
             [],
             after=last,
         )
-        return between_levels(solved, lev_n, CFG["zc"][2 * block + 1]), (solved[0],)
-
-    def inverse(block, solved, last, hold=()):
+        return between_levels(solved, lev_n, block == 0), (solved[0],)
+
+    def inverse(block, solved, last):
         rows = solved[0].shape[0] * lev_n
         late = lates[block]
         returned = call(
@@ -407,58 +401,67 @@
             "inverse",
             (table0, table1, *solved),
             [vmem] * (2 + lev_n),
-            outgoing(rows, late),
+            outgoing(rows, late, not late),
             [vmem] * len(outgoing(rows, late)),
             [],
             after=last,
         )
         last = (returned[0],)
-        if not late:
-            returned = swap(returned[:near_n], returned[near_n])
-        if hold:
-            returned = lax.optimization_barrier((*returned, *hold))[: len(returned)]
-        return exchange(returned, "lat", lat_n, 2), last
+        mine = exchange(returned[:near_n], "lat", lat_n, 2)
+        if late:
+            return mine, last
+        others = call(
+            functools.partial(part_kernel, cut),
+            "part",
+            (swap_cores(returned[near_n], lat_n),),
+            [vmem],
+            [struct(1, 2, 2, rows, width)] * near_n,
+            [vmem] * near_n,
+            [],
+        )
+        others = exchange(others, "lat", lat_n, 2)
+        return [part for pair in zip(mine, others) for part in pair], last
 
     def unfold(block, returned, out):
+        early = lat_n
         if lates[block]:
             returned = gather(returned, ())
+            places = [(r, near_n, r // 2) if r % 2 else (r, r // 2, 0) for r in range(lat_n)]
+        else:
+            places = [(r, r, 0) for r in range(lat_n)]
+            early = 3 * lat_n // 4
         rows = blocks[block][1] * levels
-        return call(
-            functools.partial(unfold_kernel, cut, blocks[block][0] * levels, lates[block]),
-            "unfold",
-            (wave_ids, cycle_row, *returned) + out,
-            [smem] + [vmem] * (1 + len(returned)) + [anywhere] * len(out),
-            [struct(slots, halves, cols * levels, width)],
-            [anywhere],
-            [
-                pltpu.VMEM((lat_n, 2, 2, rows, width), jnp.bfloat16),
-                pltpu.SemaphoreType.DMA((lat_n,)),
-            ],
-            aliases={2 + len(returned): 0} if out else None,
-        )
+        for part in (places[:early], places[early:]):
+            if not part:
+                continue
+            used = sorted({ref for _, ref, _ in part})
+            part = [(r, used.index(ref), at) for r, ref, at in part]
+            out = call(
+                functools.partial(unfold_kernel, blocks[block][0] * levels, part),
+                "unfold",
+                (wave_ids, cycle_row, *[returned[ref] for ref in used], *out),
+                [smem] + [vmem] * (1 + len(used)) + [anywhere] * len(out),
+                [struct(slots, halves, cols * levels, width)],
+                [anywhere],
+                [
+                    pltpu.VMEM((len(part), 2, 2, rows, width), jnp.bfloat16),
+                    pltpu.SemaphoreType.DMA((len(part),)),
+                ],
+                aliases={2 + len(used): 0} if out else None,
+            )
+        return out
 
     count = len(blocks)
+    out = ()
     packed, solved, returned = [None] * count, [None] * count, [None] * count
     for turn in range(count + 2):
         if 0 <= turn - 2:
-            extra = []
-            if turn == 2 and count > 1:
-                extra = [packed[1][r] for r in {0: [], 1: [1], 2: [2], 3: [1, 2, 3], 4: [3], 5: [1, 2]}[CFG["i0"]]]
-            if turn == 3:
-                extra = returned[0][1:] if CFG["i1"] == 1 else []
-            hold = returned[0][1:] if turn == 3 and CFG["i1"] == 2 else []
-            returned[turn - 2], last = inverse(turn - 2, solved[turn - 2], (*last, *extra), hold)
+            sent = returned[turn - 3][1:] if turn >= 3 else ()
+            returned[turn - 2], last = inverse(turn - 2, solved[turn - 2], (*last, *sent))
         if 0 <= turn - 1 < count:
-            extra = []
-            if turn == 2:
-                extra = {0: [], 1: returned[0][1:2], 2: returned[0][2:3], 3: returned[0][1:4]}[CFG["s1"]]
-            solved[turn - 1], last = solve(turn - 1, packed[turn - 1], (*last, *extra))
+            solved[turn - 1], last = solve(turn - 1, packed[turn - 1], last)
         if turn < count:
-            extra = []
-            if turn == 1:
-                extra = [solved[0][r] for r in {0: [], 1: [1], 2: [2], 3: [1, 2], 4: [3]}[CFG["g1"]]]
-            packed[turn], last = forward(turn, (*last, *extra))
-    out = ()
+            packed[turn], last = forward(turn, last)
     for block in range(count):
         out = tuple(unfold(block, returned[block], out))
     (out,) = out

time: 135 us -> 130 us (0.963)
  waiting for transfers between devices: 70.8 us -> 62.8 us
  starting transfers between devices: 43.2 us -> 45.7 us
  local copies, waits for them, and re-layouts: 1.99 us -> 0.02 us
    ppermute x12 -> x15, waiting for transfers between devices: 39.6 us -> 34.3 us  [exchange(): lax.ppermute(part, axis, [(i, i ^ r * stride) for i in range(count)])]
    ppermute x12 -> x15, starting transfers between devices: 15.6 us -> 18.7 us  [exchange(): lax.ppermute(part, axis, [(i, i ^ r * stride) for i in range(count)])]
    unnamed x14 -> x12, local copies, waits for them, and re-layouts: 1.99 us -> 0.02 us
    ppermute x12, waiting for transfers between devices: 28 us -> 26.3 us  [between_levels(): out[r] = lax.ppermute(part, 'lev', [(i, i ^ r) for i in range(count)])]
    pallas_call x15 -> x16, Pallas kernels: 18.9 us -> 20 us  [call(): pl.pallas_call(body, name=name, out_shape=list(outs), in_specs=list(in_sp...]
  transfers between devices with their start and end apart: 28 -> 31, of which waited for: 18 -> 17; matrix products, arithmetic and copies ran while one was open for 0% -> 0% of each run, Pallas kernels for 10% -> 12%
where the time goes in v4:
time: 130 us; the launch traced here: 129 us
  waiting for transfers between devices  62.8 us (48%)
  starting transfers between devices  45.7 us (35%)
  Pallas kernels  20 us (15%)
    ppermute x15, waiting for transfers between devices, exchange(): lax.ppermute(part, axis, [(i, i ^ r * stride) for i in range(count)])  34.3 us
    ppermute x12, waiting for transfers between devices, between_levels(): out[r] = lax.ppermute(part, 'lev', [(i, i ^ r) for i in range(count)])  26.3 us
    ppermute x12, starting transfers between devices, between_levels(): out[r] = lax.ppermute(part, 'lev', [(i, i ^ r) for i in range(count)])  25.8 us
    pallas_call x16, Pallas kernels, call(): pl.pallas_call(body, name=name, out_shape=list(outs), in_specs=list(in_sp...  20 us
    ppermute x15, starting transfers between devices, exchange(): lax.ppermute(part, axis, [(i, i ^ r * stride) for i in range(count)])  18.7 us
  transfers between devices with their start and end apart: 31, of which 17 were waited for; matrix products, arithmetic and copies ran while one was open for 0% of the time, Pallas kernels for 12%

profile of v4, /device:TPU:0, one launch (start us, length us, event | category | flops | bytes accessed | tf_op | source)
XLA Modules:
  0.0 129.5 jit_solution(14793659305405879845)
XLA Ops:
  0.8 1.8 %fold.2 = (bf16[2,2,2,256,128]{4,3,2,1,0:T(8,128)(2,1)S(1)}, bf16[2,2,2,256,128]{4,3,2,1,0:T(8,128)(2,1)S(1)}, bf16[2,2,2,256,128]{4,3,2,1,0:T(8,128)(2,1)S(1)}, bf16[2,2,2,256,128]{4,3,2,1,0:T(8,128)(2,1)S(1)}) custom-call(f32[16,128]{1,0:T(8,128)S(1)} %fusion.weights, bf16[16,2,512,128]{3,2,1,0:T(8,128)(2,1)} %bitcast.10), custom_call_target="tpu_custom_call" | custom-call | tf_op jit(solution)/shard_map/fold/pallas_call | solution.py:230
  2.6 3.0 %collective-permute-start.4 = (bf16[2,2,2,256,128]{4,3,2,1,0:T(8,128)(2,1)S(1)}, bf16[2,2,2,256,128]{4,3,2,1,0:T(8,128)(2,1)S(1)}, u32[]{:S(2)}, u32[]{:S(2)}) collective-permute-start(bf16[2,2,2,256,128]{4,3,2,1,0:T(8,128)(2,1)S(1)} %get-tuple-element.67), channel_id=1, source_target_pairs={{0,8},{4,12},{8,0},{12,4},{16,24},{20,28},{24,16},{28,20},{1,9},{5... | collective-permute-start | bytes 1572872 | tf_op jit(solution)/shard_map/ppermute | solution.py:249
  5.6 1.5 %collective-permute-start.5 = (bf16[2,2,2,256,128]{4,3,2,1,0:T(8,128)(2,1)S(1)}, bf16[2,2,2,256,128]{4,3,2,1,0:T(8,128)(2,1)S(1)}, u32[]{:S(2)}, u32[]{:S(2)}) collective-permute-start(bf16[2,2,2,256,128]{4,3,2,1,0:T(8,128)(2,1)S(1)} %get-tuple-element.68), channel_id=1, source_target_pairs={{0,16},{4,20},{8,24},{12,28},{16,0},{20,4},{24,8},{28,12},{1,17},{... | collective-permute-start | bytes 1572872 | tf_op jit(solution)/shard_map/ppermute | solution.py:249
  7.1 1.6 %fold.3 = (bf16[2,2,2,256,128]{4,3,2,1,0:T(8,128)(2,1)S(1)}, bf16[2,2,2,256,128]{4,3,2,1,0:T(8,128)(2,1)S(1)}, bf16[2,2,2,256,128]{4,3,2,1,0:T(8,128)(2,1)S(1)},...) custom-call(f32[16,128]{1,0:T(8,128)S(1)} %fusion.weights, bf16[16,2,512,128]{3,2,1,0:T(8,128)(2,1)} %bitcast.11, ...), custom_call_target="tpu_custom_call" | custom-call | tf_op jit(solution)/shard_map/fold/pallas_call | solution.py:230
  8.8 2.4 %tables.1 = (bf16[2048,640]{1,0:T(8,128)(2,1)S(1)}, bf16[2048,512]{1,0:T(8,128)(2,1)S(1)}) custom-call(s32[16]{0:T(128)S(1)} %copy-done.3, bf16[2,2,1024,512]{3,2,1,0:T(8,128)(2,1)S(1)} %copy-done, bf16[2,2,2,256,128]{4,3,2,1,0:T(8,128)(2,1)S(1)} %get-tuple-element.56.refs_0_), custom_call_target="tpu_custom_call" | custom-call | tf_op jit(solution)/shard_map/tables/pallas_call | solution.py:230
  11.2 7.1 %collective-permute-done.4.refs_1_ = bf16[2,2,2,256,128]{4,3,2,1,0:T(8,128)(2,1)S(1)} collective-permute-done((bf16[2,2,2,256,128]{4,3,2,1,0:T(8,128)(2,1)S(1)}, bf16[2,2,2,256,128]{4,3,2,1,0:T(8,128)(2,1)S(1)}, u32[]{:S(2)}, u32[]{:S(2)}) %collective-permute-start.4) | collective-permute-done | bytes 524320 | tf_op jit(solution)/shard_map/ppermute | solution.py:249
  18.3 11.9 %collective-permute-done.5.refs_2_ = bf16[2,2,2,256,128]{4,3,2,1,0:T(8,128)(2,1)S(1)} collective-permute-done((bf16[2,2,2,256,128]{4,3,2,1,0:T(8,128)(2,1)S(1)}, bf16[2,2,2,256,128]{4,3,2,1,0:T(8,128)(2,1)S(1)}, u32[]{:S(2)}, u32[]{:S(2)}) %collective-permute-start.5) | collective-permute-done | bytes 524320 | tf_op jit(solution)/shard_map/ppermute | solution.py:249
  30.8 2.1 %collective-permute-done.7.refs_4_ = bf16[4,2,2,256,128]{4,3,2,1,0:T(8,128)(2,1)S(1)} collective-permute-done((bf16[4,2,2,256,128]{4,3,2,1,0:T(8,128)(2,1)S(1)}, bf16[4,2,2,256,128]{4,3,2,1,0:T(8,128)(2,1)S(1)}, u32[]{:S(2)}, u32[]{:S(2)}) %collective-permute-start.7) | collective-permute-done | bytes 1048608 | tf_op jit(solution)/shard_map/ppermute | solution.py:266
  33.0 1.5 %forward.2 = (bf16[64,1152]{1,0:T(8,128)(2,1)S(1)}, bf16[64,1152]{1,0:T(8,128)(2,1)S(1)}, bf16[64,1152]{1,0:T(8,128)(2,1)S(1)}, bf16[64,1152]{1,0:T(8,128)(2,1)S(1)}) custom-call(bf16[2048,640]{1,0:T(8,128)(2,1)S(1)} %get-tuple-element.57.table0, bf16[2048,512]{1,0:T(8,128)(2,1)S(1)} %get-tuple-element.58.refs_4_.table1, ...), custom_call_target="tpu_custom_call" | custom-call | tf_op jit(solution)/shard_map/forward/pallas_call | solution.py:230
  34.5 3.7 %collective-permute-start.8 = (bf16[64,1152]{1,0:T(8,128)(2,1)S(1)}, bf16[64,1152]{1,0:T(8,128)(2,1)S(1)}, u32[]{:S(2)}, u32[]{:S(2)}) collective-permute-start(bf16[64,1152]{1,0:T(8,128)(2,1)S(1)} %get-tuple-element.72), channel_id=1, source_target_pairs={{0,3},{1,2},{2,1},{3,0},{4,7},{5,6},{6,5},{7,4},{8,11},{9,10},{10,... | collective-permute-start | bytes 442376 | tf_op jit(solution)/shard_map/ppermute | solution.py:261
  42.5 6.7 %collective-permute-start.9 = (bf16[64,1152]{1,0:T(8,128)(2,1)S(1)}, bf16[64,1152]{1,0:T(8,128)(2,1)S(1)}, u32[]{:S(2)}, u32[]{:S(2)}) collective-permute-start(bf16[64,1152]{1,0:T(8,128)(2,1)S(1)} %get-tuple-element.73), channel_id=1, source_target_pairs={{0,1},{1,0},{2,3},{3,2},{4,5},{5,4},{6,7},{7,6},{8,9},{9,8},{10,11... | collective-permute-start | bytes 442376 | tf_op jit(solution)/shard_map/ppermute | solution.py:261
  49.2 1.9 %collective-permute-done.10.refs_2_ = bf16[64,1152]{1,0:T(8,128)(2,1)S(1)} collective-permute-done((bf16[64,1152]{1,0:T(8,128)(2,1)S(1)}, bf16[64,1152]{1,0:T(8,128)(2,1)S(1)}, u32[]{:S(2)}, u32[]{:S(2)}) %collective-permute-start.10) | collective-permute-done | bytes 147488 | tf_op jit(solution)/shard_map/ppermute | solution.py:261
  51.1 3.0 %collective-permute-done.9.refs_1_ = bf16[64,1152]{1,0:T(8,128)(2,1)S(1)} collective-permute-done((bf16[64,1152]{1,0:T(8,128)(2,1)S(1)}, bf16[64,1152]{1,0:T(8,128)(2,1)S(1)}, u32[]{:S(2)}, u32[]{:S(2)}) %collective-permute-start.9) | collective-permute-done | bytes 147488 | tf_op jit(solution)/shard_map/ppermute | solution.py:261
  55.4 2.5 %collective-permute-start.14 = (bf16[64,1152]{1,0:T(8,128)(2,1)S(1)}, bf16[64,1152]{1,0:T(8,128)(2,1)S(1)}, u32[]{:S(2)}, u32[]{:S(2)}) collective-permute-start(bf16[64,1152]{1,0:T(8,128)(2,1)S(1)} %get-tuple-element.84), channel_id=1, source_target_pairs={{0,3},{1,2},{2,1},{3,0},{4,7},{5,6},{6,5},{7,4},{8,11},{9,10},{10,... | collective-permute-start | bytes 442376 | tf_op jit(solution)/shard_map/ppermute | solution.py:261
  57.9 6.1 %collective-permute-done.14.refs_3_ = bf16[64,1152]{1,0:T(8,128)(2,1)S(1)} collective-permute-done((bf16[64,1152]{1,0:T(8,128)(2,1)S(1)}, bf16[64,1152]{1,0:T(8,128)(2,1)S(1)}, u32[]{:S(2)}, u32[]{:S(2)}) %collective-permute-start.14) | collective-permute-done | bytes 147488 | tf_op jit(solution)/shard_map/ppermute | solution.py:261
  64.0 3.4 %collective-permute-start.15 = (bf16[64,1152]{1,0:T(8,128)(2,1)S(1)}, bf16[64,1152]{1,0:T(8,128)(2,1)S(1)}, u32[]{:S(2)}, u32[]{:S(2)}) collective-permute-start(bf16[64,1152]{1,0:T(8,128)(2,1)S(1)} %get-tuple-element.85), channel_id=1, source_target_pairs={{0,1},{1,0},{2,3},{3,2},{4,5},{5,4},{6,7},{7,6},{8,9},{9,8},{10,11... | collective-permute-start | bytes 442376 | tf_op jit(solution)/shard_map/ppermute | solution.py:261
  67.4 1.5 %forward.3 = (bf16[64,1152]{1,0:T(8,128)(2,1)S(1)}, bf16[64,1152]{1,0:T(8,128)(2,1)S(1)}, bf16[64,1152]{1,0:T(8,128)(2,1)S(1)}, bf16[64,1152]{1,0:T(8,128)(2,1)S(1)}) custom-call(bf16[2048,640]{1,0:T(8,128)(2,1)S(1)} %get-tuple-element.57.table0, bf16[2048,512]{1,0:T(8,128)(2,1)S(1)} %get-tuple-element.58.refs_4_.table1, ...), custom_call_target="tpu_custom_call" | custom-call | tf_op jit(solution)/shard_map/forward/pallas_call | solution.py:230
  69.0 2.4 %collective-permute-start.11 = (bf16[64,1152]{1,0:T(8,128)(2,1)S(1)}, bf16[64,1152]{1,0:T(8,128)(2,1)S(1)}, u32[]{:S(2)}, u32[]{:S(2)}) collective-permute-start(bf16[64,1152]{1,0:T(8,128)(2,1)S(1)} %get-tuple-element.79), channel_id=1, source_target_pairs={{0,3},{1,2},{2,1},{3,0},{4,7},{5,6},{6,5},{7,4},{8,11},{9,10},{10,... | collective-permute-start | bytes 442376 | tf_op jit(solution)/shard_map/ppermute | solution.py:261
  72.9 1.6 %inverse.2 = (bf16[2,2,2,256,128]{4,3,2,1,0:T(8,128)(2,1)S(1)}, bf16[2,2,2,256,128]{4,3,2,1,0:T(8,128)(2,1)S(1)}, bf16[2,2,2,256,128]{4,3,2,1,0:T(8,128)(2,1)S(1)}, bf16[2,2,2,256,128]{4,3,2,1,0:T(8,128)(2,1)S(1)}) custom-call(bf16[2048,640]{1,0:T(8,128)(2,1)S(1)} %get-tuple-element.57.table0, bf16[2048,512]{1,0:T(8,128)(2,1)S(1)} %get-tuple-element.58.refs_4_.table1, ...), custom_call_target="tpu_custom_call" | custom-call | tf_op jit(solution)/shard_map/inverse/pallas_call | solution.py:230
  78.6 2.5 %collective-permute-start.12 = (bf16[64,1152]{1,0:T(8,128)(2,1)S(1)}, bf16[64,1152]{1,0:T(8,128)(2,1)S(1)}, u32[]{:S(2)}, u32[]{:S(2)}) collective-permute-start(bf16[64,1152]{1,0:T(8,128)(2,1)S(1)} %get-tuple-element.80), channel_id=1, source_target_pairs={{0,1},{1,0},{2,3},{3,2},{4,5},{5,4},{6,7},{7,6},{8,9},{9,8},{10,11... | collective-permute-start | bytes 442376 | tf_op jit(solution)/shard_map/ppermute | solution.py:261
  81.1 4.2 %collective-permute-done.13.refs_2_ = bf16[64,1152]{1,0:T(8,128)(2,1)S(1)} collective-permute-done((bf16[64,1152]{1,0:T(8,128)(2,1)S(1)}, bf16[64,1152]{1,0:T(8,128)(2,1)S(1)}, u32[]{:S(2)}, u32[]{:S(2)}) %collective-permute-start.13) | collective-permute-done | bytes 147488 | tf_op jit(solution)/shard_map/ppermute | solution.py:261
  87.5 1.7 %collective-permute-start.18 = (bf16[64,1152]{1,0:T(8,128)(2,1)S(1)}, bf16[64,1152]{1,0:T(8,128)(2,1)S(1)}, u32[]{:S(2)}, u32[]{:S(2)}) collective-permute-start(bf16[64,1152]{1,0:T(8,128)(2,1)S(1)} %get-tuple-element.91), channel_id=1, source_target_pairs={{0,2},{1,3},{2,0},{3,1},{4,6},{5,7},{6,4},{7,5},{8,10},{9,11},{10,... | collective-permute-start | bytes 442376 | tf_op jit(solution)/shard_map/ppermute | solution.py:261
  89.2 3.2 %collective-permute-done.17.refs_1_ = bf16[64,1152]{1,0:T(8,128)(2,1)S(1)} collective-permute-done((bf16[64,1152]{1,0:T(8,128)(2,1)S(1)}, bf16[64,1152]{1,0:T(8,128)(2,1)S(1)}, u32[]{:S(2)}, u32[]{:S(2)}) %collective-permute-start.17) | collective-permute-done | bytes 147488 | tf_op jit(solution)/shard_map/ppermute | solution.py:261
  92.4 1.8 %collective-permute-start.19 = (bf16[64,1152]{1,0:T(8,128)(2,1)S(1)}, bf16[64,1152]{1,0:T(8,128)(2,1)S(1)}, u32[]{:S(2)}, u32[]{:S(2)}) collective-permute-start(bf16[64,1152]{1,0:T(8,128)(2,1)S(1)} %get-tuple-element.92), channel_id=1, source_target_pairs={{0,3},{1,2},{2,1},{3,0},{4,7},{5,6},{6,5},{7,4},{8,11},{9,10},{10,... | collective-permute-start | bytes 442376 | tf_op jit(solution)/shard_map/ppermute | solution.py:261
  94.3 2.7 %collective-permute-done.18.refs_2_ = bf16[64,1152]{1,0:T(8,128)(2,1)S(1)} collective-permute-done((bf16[64,1152]{1,0:T(8,128)(2,1)S(1)}, bf16[64,1152]{1,0:T(8,128)(2,1)S(1)}, u32[]{:S(2)}, u32[]{:S(2)}) %collective-permute-start.18) | collective-permute-done | bytes 147488 | tf_op jit(solution)/shard_map/ppermute | solution.py:261
  97.0 2.5 %collective-permute-done.19.refs_3_ = bf16[64,1152]{1,0:T(8,128)(2,1)S(1)} collective-permute-done((bf16[64,1152]{1,0:T(8,128)(2,1)S(1)}, bf16[64,1152]{1,0:T(8,128)(2,1)S(1)}, u32[]{:S(2)}, u32[]{:S(2)}) %collective-permute-start.19) | collective-permute-done | bytes 147488 | tf_op jit(solution)/shard_map/ppermute | solution.py:261
  99.5 1.6 %inverse.3 = (bf16[1,2,2,256,128]{4,3,2,1,0:T(8,128)(2,1)S(1)}, bf16[1,2,2,256,128]{4,3,2,1,0:T(8,128)(2,1)S(1)}, bf16[1,2,2,256,128]{4,3,2,1,0:T(8,128)(2,1)S(1...) custom-call(bf16[2048,640]{1,0:T(8,128)(2,1)S(1)} %get-tuple-element.57.table0, ...), custom_call_target="tpu_custom_call" | custom-call | tf_op jit(solution)/shard_map/inverse/pallas_call | solution.py:230
  103.9 1.6 %collective-permute-start.27 = (bf16[1,2,2,256,128]{4,3,2,1,0:T(8,128)(2,1)S(1)}, bf16[1,2,2,256,128]{4,3,2,1,0:T(8,128)(2,1)S(1)}, u32[]{:S(2)}, u32[]{:S(2)}) collective-permute-start(bf16[1,2,2,256,128]{4,3,2,1,0:T(8,128)(2,1)S(1)} %get-tuple-element.102), channel_id=1, source_target_pairs={{0,8},{4,12},{8,0},{12,4},{16,24},{20,28},{24,16},{28,20},{1,9},{5... | collective-permute-start | bytes 786440 | tf_op jit(solution)/shard_map/ppermute | solution.py:249
  106.0 5.0 %collective-permute-done.26.refs_2_ = bf16[1,2,2,256,128]{4,3,2,1,0:T(8,128)(2,1)S(1)} collective-permute-done((bf16[1,2,2,256,128]{4,3,2,1,0:T(8,128)(2,1)S(1)}, bf16[1,2,2,256,128]{4,3,2,1,0:T(8,128)(2,1)S(1)}, u32[]{:S(2)}, u32[]{:S(2)}) %collective-permute-start.26) | collective-permute-done | bytes 262176 | tf_op jit(solution)/shard_map/ppermute | solution.py:249
  113.9 2.0 %unfold.3.refs_6_ = bf16[16,2,512,128]{3,2,1,0:T(8,128)(2,1)} custom-call(s32[16]{0:T(128)S(1)} %copy-done.3, s32[1,128]{1,0:T(1,128)S(1)} %bitcast.7, bf16[2,2,2,256,128]{4,3,2,1,0:T(8,128)(2,1)S(1)} %get-tuple-element.88.refs_4_.refs_0_, bf16[2,2,2,256,128]{4,3,2,1,0:T(8,128)(2,1)S(1)} %collective-permute-done.20.refs_5_.refs_1_, ...), custom_call_target="tpu_custom_call" | custom-call | tf_op jit(solution)/shard_map/unfold/pallas_call | solution.py:230
  116.5 9.7 %collective-permute-done.29.refs_5_ = bf16[1,2,2,256,128]{4,3,2,1,0:T(8,128)(2,1)S(1)} collective-permute-done((bf16[1,2,2,256,128]{4,3,2,1,0:T(8,128)(2,1)S(1)}, bf16[1,2,2,256,128]{4,3,2,1,0:T(8,128)(2,1)S(1)}, u32[]{:S(2)}, u32[]{:S(2)}) %collective-permute-start.29) | collective-permute-done | bytes 262176 | tf_op jit(solution)/shard_map/ppermute | solution.py:249
  126.2 1.8 %unfold.4.refs_2_ = bf16[16,2,512,128]{3,2,1,0:T(8,128)(2,1)} custom-call(s32[16]{0:T(128)S(1)} %copy-done.3, s32[1,128]{1,0:T(1,128)S(1)} %bitcast.8, bf16[1,2,2,256,128]{4,3,2,1,0:T(8,128)(2,1)S(1)} %get-tuple-element.99.refs_0_, bf16[1,2,2,256,128]{4,3,2,1,0:T(8,128)(2,1)S(1)} %get-tuple-element.100.refs_1_, ...), custom_call_target="tpu_custom_call", output_to_operand_aliasing={{}: (8, {})} | custom-call | tf_op jit(solution)/shard_map/unfold/pallas_call | solution.py:230
  (59 shorter events, 23.2 us)
Async XLA Ops:
  2.6 15.8 %collective-permute-start.4 = (bf16[2,2,2,256,128]{4,3,2,1,0:T(8,128)(2,1)S(1)}, bf16[2,2,2,256,128]{4,3,2,1,0:T(8,128)(2,1)S(1)}, u32[]{:S(2)}, u32[]{:S(2)}) collective-permute-start(bf16[2,2,2,256,128]{4,3,2,1,0:T(8,128)(2,1)S(1)} %get-tuple-element.67), channel_id=1, source_target_pairs={{0,8},{4,12},{8,0},{12,4},{16,24},{20,28},{24,16},{28,20},{1,9},{5... | collective-permute-start | bytes 1572872 | tf_op jit(solution)/shard_map/ppermute | solution.py:249
  5.6 24.6 %collective-permute-start.5 = (bf16[2,2,2,256,128]{4,3,2,1,0:T(8,128)(2,1)S(1)}, bf16[2,2,2,256,128]{4,3,2,1,0:T(8,128)(2,1)S(1)}, u32[]{:S(2)}, u32[]{:S(2)}) collective-permute-start(bf16[2,2,2,256,128]{4,3,2,1,0:T(8,128)(2,1)S(1)} %get-tuple-element.68), channel_id=1, source_target_pairs={{0,16},{4,20},{8,24},{12,28},{16,0},{20,4},{24,8},{28,12},{1,17},{... | collective-permute-start | bytes 1572872 | tf_op jit(solution)/shard_map/ppermute | solution.py:249
  7.1 23.1 %collective-permute-start.6 = (bf16[2,2,2,256,128]{4,3,2,1,0:T(8,128)(2,1)S(1)}, bf16[2,2,2,256,128]{4,3,2,1,0:T(8,128)(2,1)S(1)}, u32[]{:S(2)}, u32[]{:S(2)}) collective-permute-start(bf16[2,2,2,256,128]{4,3,2,1,0:T(8,128)(2,1)S(1)} %get-tuple-element.69), channel_id=1, source_target_pairs={{0,24},{4,28},{8,16},{12,20},{16,8},{20,12},{24,0},{28,4},{1,25},{... | collective-permute-start | bytes 1572872 | tf_op jit(solution)/shard_map/ppermute | solution.py:249
  30.3 2.7 %collective-permute-start.7 = (bf16[4,2,2,256,128]{4,3,2,1,0:T(8,128)(2,1)S(1)}, bf16[4,2,2,256,128]{4,3,2,1,0:T(8,128)(2,1)S(1)}, u32[]{:S(2)}, u32[]{:S(2)}) collective-permute-start(bf16[4,2,2,256,128]{4,3,2,1,0:T(8,128)(2,1)S(1)} %gather.2), channel_id=1, source_target_pairs={{0,4},{4,0},{8,12},{12,8},{16,20},{20,16},{24,28},{28,24},{1,5},{5... | collective-permute-start | bytes 3145736 | tf_op jit(solution)/shard_map/ppermute | solution.py:266
  30.4 7.9 %collective-permute-start = (bf16[4,2,2,256,128]{4,3,2,1,0:T(8,128)(2,1)S(1)}, bf16[4,2,2,256,128]{4,3,2,1,0:T(8,128)(2,1)S(1)}, u32[]{:S(2)}, u32[]{:S(2)}) collective-permute-start(bf16[4,2,2,256,128]{4,3,2,1,0:T(8,128)(2,1)S(1)} %get-tuple-element.59), channel_id=1, source_target_pairs={{0,4},{4,0},{8,12},{12,8},{16,20},{20,16},{24,28},{28,24},{1,5},{5... | collective-permute-start | bytes 3145736 | tf_op jit(solution)/shard_map/ppermute | solution.py:266
  33.0 21.1 %copy-start.5 = (f32[128]{0:T(128)S(1)}, f32[128]{0:T(128)}, u32[]{:S(2)}) copy-start(f32[128]{0:T(128)} %rates.3) | copy-start | bytes 1540
  34.5 7.9 %collective-permute-start.8 = (bf16[64,1152]{1,0:T(8,128)(2,1)S(1)}, bf16[64,1152]{1,0:T(8,128)(2,1)S(1)}, u32[]{:S(2)}, u32[]{:S(2)}) collective-permute-start(bf16[64,1152]{1,0:T(8,128)(2,1)S(1)} %get-tuple-element.72), channel_id=1, source_target_pairs={{0,3},{1,2},{2,1},{3,0},{4,7},{5,6},{6,5},{7,4},{8,11},{9,10},{10,... | collective-permute-start | bytes 442376 | tf_op jit(solution)/shard_map/ppermute | solution.py:261
  38.3 29.1 %collective-permute-start.1 = (bf16[2,2,2,256,128]{4,3,2,1,0:T(8,128)(2,1)S(1)}, bf16[2,2,2,256,128]{4,3,2,1,0:T(8,128)(2,1)S(1)}, u32[]{:S(2)}, u32[]{:S(2)}) collective-permute-start(bf16[2,2,2,256,128]{4,3,2,1,0:T(8,128)(2,1)S(1)} %get-tuple-element.64), channel_id=1, source_target_pairs={{0,8},{4,12},{8,0},{12,4},{16,24},{20,28},{24,16},{28,20},{1,9},{5... | collective-permute-start | bytes 1572872 | tf_op jit(solution)/shard_map/ppermute | solution.py:249
  39.6 27.8 %collective-permute-start.2 = (bf16[2,2,2,256,128]{4,3,2,1,0:T(8,128)(2,1)S(1)}, bf16[2,2,2,256,128]{4,3,2,1,0:T(8,128)(2,1)S(1)}, u32[]{:S(2)}, u32[]{:S(2)}) collective-permute-start(bf16[2,2,2,256,128]{4,3,2,1,0:T(8,128)(2,1)S(1)} %get-tuple-element.65), channel_id=1, source_target_pairs={{0,16},{4,20},{8,24},{12,28},{16,0},{20,4},{24,8},{28,12},{1,17},{... | collective-permute-start | bytes 1572872 | tf_op jit(solution)/shard_map/ppermute | solution.py:249
  40.4 27.0 %collective-permute-start.3 = (bf16[2,2,2,256,128]{4,3,2,1,0:T(8,128)(2,1)S(1)}, bf16[2,2,2,256,128]{4,3,2,1,0:T(8,128)(2,1)S(1)}, u32[]{:S(2)}, u32[]{:S(2)}) collective-permute-start(bf16[2,2,2,256,128]{4,3,2,1,0:T(8,128)(2,1)S(1)} %get-tuple-element.66), channel_id=1, source_target_pairs={{0,24},{4,28},{8,16},{12,20},{16,8},{20,12},{24,0},{28,4},{1,25},{... | collective-permute-start | bytes 1572872 | tf_op jit(solution)/shard_map/ppermute | solution.py:249
  41.8 9.3 %collective-permute-start.10 = (bf16[64,1152]{1,0:T(8,128)(2,1)S(1)}, bf16[64,1152]{1,0:T(8,128)(2,1)S(1)}, u32[]{:S(2)}, u32[]{:S(2)}) collective-permute-start(bf16[64,1152]{1,0:T(8,128)(2,1)S(1)} %get-tuple-element.74), channel_id=1, source_target_pairs={{0,2},{1,3},{2,0},{3,1},{4,6},{5,7},{6,4},{7,5},{8,10},{9,11},{10,... | collective-permute-start | bytes 442376 | tf_op jit(solution)/shard_map/ppermute | solution.py:261
  42.5 11.6 %collective-permute-start.9 = (bf16[64,1152]{1,0:T(8,128)(2,1)S(1)}, bf16[64,1152]{1,0:T(8,128)(2,1)S(1)}, u32[]{:S(2)}, u32[]{:S(2)}) collective-permute-start(bf16[64,1152]{1,0:T(8,128)(2,1)S(1)} %get-tuple-element.73), channel_id=1, source_target_pairs={{0,1},{1,0},{2,3},{3,2},{4,5},{5,4},{6,7},{7,6},{8,9},{9,8},{10,11... | collective-permute-start | bytes 442376 | tf_op jit(solution)/shard_map/ppermute | solution.py:261
  55.4 8.7 %collective-permute-start.14 = (bf16[64,1152]{1,0:T(8,128)(2,1)S(1)}, bf16[64,1152]{1,0:T(8,128)(2,1)S(1)}, u32[]{:S(2)}, u32[]{:S(2)}) collective-permute-start(bf16[64,1152]{1,0:T(8,128)(2,1)S(1)} %get-tuple-element.84), channel_id=1, source_target_pairs={{0,3},{1,2},{2,1},{3,0},{4,7},{5,6},{6,5},{7,4},{8,11},{9,10},{10,... | collective-permute-start | bytes 442376 | tf_op jit(solution)/shard_map/ppermute | solution.py:261
  57.9 13.7 %collective-permute-start.16 = (bf16[64,1152]{1,0:T(8,128)(2,1)S(1)}, bf16[64,1152]{1,0:T(8,128)(2,1)S(1)}, u32[]{:S(2)}, u32[]{:S(2)}) collective-permute-start(bf16[64,1152]{1,0:T(8,128)(2,1)S(1)} %get-tuple-element.86), channel_id=1, source_target_pairs={{0,2},{1,3},{2,0},{3,1},{4,6},{5,7},{6,4},{7,5},{8,10},{9,11},{10,... | collective-permute-start | bytes 442376 | tf_op jit(solution)/shard_map/ppermute | solution.py:261
  64.0 8.9 %collective-permute-start.15 = (bf16[64,1152]{1,0:T(8,128)(2,1)S(1)}, bf16[64,1152]{1,0:T(8,128)(2,1)S(1)}, u32[]{:S(2)}, u32[]{:S(2)}) collective-permute-start(bf16[64,1152]{1,0:T(8,128)(2,1)S(1)} %get-tuple-element.85), channel_id=1, source_target_pairs={{0,1},{1,0},{2,3},{3,2},{4,5},{5,4},{6,7},{7,6},{8,9},{9,8},{10,11... | collective-permute-start | bytes 442376 | tf_op jit(solution)/shard_map/ppermute | solution.py:261
  69.0 9.6 %collective-permute-start.11 = (bf16[64,1152]{1,0:T(8,128)(2,1)S(1)}, bf16[64,1152]{1,0:T(8,128)(2,1)S(1)}, u32[]{:S(2)}, u32[]{:S(2)}) collective-permute-start(bf16[64,1152]{1,0:T(8,128)(2,1)S(1)} %get-tuple-element.79), channel_id=1, source_target_pairs={{0,3},{1,2},{2,1},{3,0},{4,7},{5,6},{6,5},{7,4},{8,11},{9,10},{10,... | collective-permute-start | bytes 442376 | tf_op jit(solution)/shard_map/ppermute | solution.py:261
  74.5 25.0 %collective-permute-start.20 = (bf16[2,2,2,256,128]{4,3,2,1,0:T(8,128)(2,1)S(1)}, bf16[2,2,2,256,128]{4,3,2,1,0:T(8,128)(2,1)S(1)}, u32[]{:S(2)}, u32[]{:S(2)}) collective-permute-start(bf16[2,2,2,256,128]{4,3,2,1,0:T(8,128)(2,1)S(1)} %get-tuple-element.93), channel_id=1, source_target_pairs={{0,8},{4,12},{8,0},{12,4},{16,24},{20,28},{24,16},{28,20},{1,9},{5... | collective-permute-start | bytes 1572872 | tf_op jit(solution)/shard_map/ppermute | solution.py:249
  75.8 23.7 %collective-permute-start.21 = (bf16[2,2,2,256,128]{4,3,2,1,0:T(8,128)(2,1)S(1)}, bf16[2,2,2,256,128]{4,3,2,1,0:T(8,128)(2,1)S(1)}, u32[]{:S(2)}, u32[]{:S(2)}) collective-permute-start(bf16[2,2,2,256,128]{4,3,2,1,0:T(8,128)(2,1)S(1)} %get-tuple-element.94), channel_id=1, source_target_pairs={{0,16},{4,20},{8,24},{12,28},{16,0},{20,4},{24,8},{28,12},{1,17},{... | collective-permute-start | bytes 1572872 | tf_op jit(solution)/shard_map/ppermute | solution.py:249
  76.6 22.9 %collective-permute-start.22 = (bf16[2,2,2,256,128]{4,3,2,1,0:T(8,128)(2,1)S(1)}, bf16[2,2,2,256,128]{4,3,2,1,0:T(8,128)(2,1)S(1)}, u32[]{:S(2)}, u32[]{:S(2)}) collective-permute-start(bf16[2,2,2,256,128]{4,3,2,1,0:T(8,128)(2,1)S(1)} %get-tuple-element.95), channel_id=1, source_target_pairs={{0,24},{4,28},{8,16},{12,20},{16,8},{20,12},{24,0},{28,4},{1,25},{... | collective-permute-start | bytes 1572872 | tf_op jit(solution)/shard_map/ppermute | solution.py:249
  78.0 7.3 %collective-permute-start.13 = (bf16[64,1152]{1,0:T(8,128)(2,1)S(1)}, bf16[64,1152]{1,0:T(8,128)(2,1)S(1)}, u32[]{:S(2)}, u32[]{:S(2)}) collective-permute-start(bf16[64,1152]{1,0:T(8,128)(2,1)S(1)} %get-tuple-element.81), channel_id=1, source_target_pairs={{0,2},{1,3},{2,0},{3,1},{4,6},{5,7},{6,4},{7,5},{8,10},{9,11},{10,... | collective-permute-start | bytes 442376 | tf_op jit(solution)/shard_map/ppermute | solution.py:261
  78.6 7.2 %collective-permute-start.12 = (bf16[64,1152]{1,0:T(8,128)(2,1)S(1)}, bf16[64,1152]{1,0:T(8,128)(2,1)S(1)}, u32[]{:S(2)}, u32[]{:S(2)}) collective-permute-start(bf16[64,1152]{1,0:T(8,128)(2,1)S(1)} %get-tuple-element.80), channel_id=1, source_target_pairs={{0,1},{1,0},{2,3},{3,2},{4,5},{5,4},{6,7},{7,6},{8,9},{9,8},{10,11... | collective-permute-start | bytes 442376 | tf_op jit(solution)/shard_map/ppermute | solution.py:261
  87.0 5.4 %collective-permute-start.17 = (bf16[64,1152]{1,0:T(8,128)(2,1)S(1)}, bf16[64,1152]{1,0:T(8,128)(2,1)S(1)}, u32[]{:S(2)}, u32[]{:S(2)}) collective-permute-start(bf16[64,1152]{1,0:T(8,128)(2,1)S(1)} %get-tuple-element.90), channel_id=1, source_target_pairs={{0,1},{1,0},{2,3},{3,2},{4,5},{5,4},{6,7},{7,6},{8,9},{9,8},{10,11... | collective-permute-start | bytes 442376 | tf_op jit(solution)/shard_map/ppermute | solution.py:261
  87.5 9.5 %collective-permute-start.18 = (bf16[64,1152]{1,0:T(8,128)(2,1)S(1)}, bf16[64,1152]{1,0:T(8,128)(2,1)S(1)}, u32[]{:S(2)}, u32[]{:S(2)}) collective-permute-start(bf16[64,1152]{1,0:T(8,128)(2,1)S(1)} %get-tuple-element.91), channel_id=1, source_target_pairs={{0,2},{1,3},{2,0},{3,1},{4,6},{5,7},{6,4},{7,5},{8,10},{9,11},{10,... | collective-permute-start | bytes 442376 | tf_op jit(solution)/shard_map/ppermute | solution.py:261
  92.4 7.0 %collective-permute-start.19 = (bf16[64,1152]{1,0:T(8,128)(2,1)S(1)}, bf16[64,1152]{1,0:T(8,128)(2,1)S(1)}, u32[]{:S(2)}, u32[]{:S(2)}) collective-permute-start(bf16[64,1152]{1,0:T(8,128)(2,1)S(1)} %get-tuple-element.92), channel_id=1, source_target_pairs={{0,3},{1,2},{2,1},{3,0},{4,7},{5,6},{6,5},{7,4},{8,11},{9,10},{10,... | collective-permute-start | bytes 442376 | tf_op jit(solution)/shard_map/ppermute | solution.py:261
  101.1 2.8 %collective-permute-start.24 = (bf16[4,2,2,256,128]{4,3,2,1,0:T(8,128)(2,1)S(1)}, bf16[4,2,2,256,128]{4,3,2,1,0:T(8,128)(2,1)S(1)}, u32[]{:S(2)}, u32[]{:S(2)}) collective-permute-start(bf16[4,2,2,256,128]{4,3,2,1,0:T(8,128)(2,1)S(1)} %get-tuple-element.97), channel_id=1, source_target_pairs={{0,4},{4,0},{8,12},{12,8},{16,20},{20,16},{24,28},{28,24},{1,5},{5... | collective-permute-start | bytes 3145736 | tf_op jit(solution)/shard_map/ppermute | solution.py:266
  101.2 11.2 %collective-permute-start.30 = (bf16[4,2,2,256,128]{4,3,2,1,0:T(8,128)(2,1)S(1)}, bf16[4,2,2,256,128]{4,3,2,1,0:T(8,128)(2,1)S(1)}, u32[]{:S(2)}, u32[]{:S(2)}) collective-permute-start(bf16[4,2,2,256,128]{4,3,2,1,0:T(8,128)(2,1)S(1)} %gather.3), channel_id=1, source_target_pairs={{0,4},{4,0},{8,12},{12,8},{16,20},{20,16},{24,28},{28,24},{1,5},{5... | collective-permute-start | bytes 3145736 | tf_op jit(solution)/shard_map/ppermute | solution.py:266
  101.8 9.2 %collective-permute-start.26 = (bf16[1,2,2,256,128]{4,3,2,1,0:T(8,128)(2,1)S(1)}, bf16[1,2,2,256,128]{4,3,2,1,0:T(8,128)(2,1)S(1)}, u32[]{:S(2)}, u32[]{:S(2)}) collective-permute-start(bf16[1,2,2,256,128]{4,3,2,1,0:T(8,128)(2,1)S(1)} %get-tuple-element.101), channel_id=1, source_target_pairs={{0,8},{4,12},{8,0},{12,4},{16,24},{20,28},{24,16},{28,20},{1,9},{5... | collective-permute-start | bytes 786440 | tf_op jit(solution)/shard_map/ppermute | solution.py:249
  103.0 12.9 %collective-permute-start.28 = (bf16[1,2,2,256,128]{4,3,2,1,0:T(8,128)(2,1)S(1)}, bf16[1,2,2,256,128]{4,3,2,1,0:T(8,128)(2,1)S(1)}, u32[]{:S(2)}, u32[]{:S(2)}) collective-permute-start(bf16[1,2,2,256,128]{4,3,2,1,0:T(8,128)(2,1)S(1)} %get-tuple-element.103), channel_id=1, source_target_pairs={{0,16},{4,20},{8,24},{12,28},{16,0},{20,4},{24,8},{28,12},{1,17},{... | collective-permute-start | bytes 786440 | tf_op jit(solution)/shard_map/ppermute | solution.py:249
  103.9 12.7 %collective-permute-start.27 = (bf16[1,2,2,256,128]{4,3,2,1,0:T(8,128)(2,1)S(1)}, bf16[1,2,2,256,128]{4,3,2,1,0:T(8,128)(2,1)S(1)}, u32[]{:S(2)}, u32[]{:S(2)}) collective-permute-start(bf16[1,2,2,256,128]{4,3,2,1,0:T(8,128)(2,1)S(1)} %get-tuple-element.102), channel_id=1, source_target_pairs={{0,8},{4,12},{8,0},{12,4},{16,24},{20,28},{24,16},{28,20},{1,9},{5... | collective-permute-start | bytes 786440 | tf_op jit(solution)/shard_map/ppermute | solution.py:249
  105.4 20.8 %collective-permute-start.29 = (bf16[1,2,2,256,128]{4,3,2,1,0:T(8,128)(2,1)S(1)}, bf16[1,2,2,256,128]{4,3,2,1,0:T(8,128)(2,1)S(1)}, u32[]{:S(2)}, u32[]{:S(2)}) collective-permute-start(bf16[1,2,2,256,128]{4,3,2,1,0:T(8,128)(2,1)S(1)} %get-tuple-element.104), channel_id=1, source_target_pairs={{0,16},{4,20},{8,24},{12,28},{16,0},{20,4},{24,8},{28,12},{1,17},{... | collective-permute-start | bytes 786440 | tf_op jit(solution)/shard_map/ppermute | solution.py:249
  110.9 17.1 %collective-permute-start.23 = (bf16[1,2,2,256,128]{4,3,2,1,0:T(8,128)(2,1)S(1)}, bf16[1,2,2,256,128]{4,3,2,1,0:T(8,128)(2,1)S(1)}, u32[]{:S(2)}, u32[]{:S(2)}) collective-permute-start(bf16[1,2,2,256,128]{4,3,2,1,0:T(8,128)(2,1)S(1)} %get-tuple-element.96), channel_id=1, source_target_pairs={{0,24},{4,28},{8,16},{12,20},{16,8},{20,12},{24,0},{28,4},{1,25},{... | collective-permute-start | bytes 786440 | tf_op jit(solution)/shard_map/ppermute | solution.py:249
  112.4 15.6 %collective-permute-start.25 = (bf16[1,2,2,256,128]{4,3,2,1,0:T(8,128)(2,1)S(1)}, bf16[1,2,2,256,128]{4,3,2,1,0:T(8,128)(2,1)S(1)}, u32[]{:S(2)}, u32[]{:S(2)}) collective-permute-start(bf16[1,2,2,256,128]{4,3,2,1,0:T(8,128)(2,1)S(1)} %get-tuple-element.98), channel_id=1, source_target_pairs={{0,24},{4,28},{8,16},{12,20},{16,8},{20,12},{24,0},{28,4},{1,25},{... | collective-permute-start | bytes 786440 | tf_op jit(solution)/shard_map/ppermute | solution.py:249
  (5 other events, 72.7 us)
